TPU v7x, 512 devices: a whole 4x4x16 slice. The times are simulated.
512 devices in a mesh: grp: 16 (over z), blk: 32 (over y, x, core).
Axes of the slice: x: 4, y: 4, z: 16, core: 2. Of those that a mesh axis runs over, the one named last changes fastest.
Arguments:
- right_side: float32 [4, 131072, 128], P(None, ('grp', 'blk')), may hold values from -6 to 6
- inverse_diag: bfloat16 [131072, 256], P(('grp', 'blk'))
- factor_blocks: bfloat16 [512, 24, 256, 256], P(('grp', 'blk')), may hold values from -0.078125 to 0.078125
- sources: int32 [512, 24], P(('grp', 'blk')), may hold values from 0 to 31, as said below
- counts: int32 [512], P(('grp', 'blk')), may hold values from 1 to 24, as said below
- carry_in: float32 [131072, 128], P(('grp', 'blk')), may hold values from -6 to 6
Outputs:
- solved: float32 [4, 131072, 128], P(None, ('grp', 'blk'))
- carry_out: float32 [131072, 128], P(('grp', 'blk'))
Inputs may be any that keep to these rules, and one draw needn't show every extreme that they name: Slots at or beyond counts[d] take no part; some row block uses all 24 slots. `sources`: slot 0 of row block d reads the opposite block of its group, (b + 32 / 2) modulo 32; every other slot reads a block that differs from d's own block index b by at most 3, counted cyclically within the group of 32 blocks.
All inputs are finite; a program needn't handle non-finite values.
Results may differ from a plain program's by a relative error of at most 0.009.
Values may be sent and summed in bfloat16 or wider, within the bound.
No kernel may reach another device: no remote copies, remote signals or barrier semaphores. Data moves between devices by JAX's collectives and lax.ppermute only.
A program may use at most 64 MiB of HBM per device.

v0:
```python
import jax
import jax.numpy as jnp
from jax import lax
from jax.sharding import PartitionSpec as P


def passed_along(value, axis, by):
    count = lax.axis_size(axis)
    pairs = [(i, i + by) for i in range(count) if 0 <= i + by < count]
    return lax.ppermute(value, axis, pairs)


def slot_sum(held_blocks, source_list, upper_slot, gathered):
    block_rows = held_blocks.shape[1]
    column_count = gathered.shape[1]

    def add_slot(k, running):
        matrix = lax.dynamic_index_in_dim(held_blocks, k, 0, keepdims=False)
        block_piece = lax.dynamic_slice_in_dim(gathered, source_list[k] * block_rows, block_rows, 0)
        return running + jnp.dot(matrix, block_piece, preferred_element_type=jnp.float32)

    return lax.fori_loop(
        jnp.int32(0), upper_slot, add_slot, jnp.zeros((block_rows, column_count), jnp.float32)
    )


def shards(right_side, inverse_diag, factor_blocks, sources, counts, carry_in):
    held_blocks = factor_blocks[0]
    source_list = sources[0]
    live_count = counts[0]
    tick_total = right_side.shape[0]
    incoming = carry_in
    partial_value = carry_in
    solved_ticks = []
    for tick_index in range(tick_total):
        residual = (right_side[tick_index] - incoming).astype(jnp.bfloat16)
        solved = jnp.dot(inverse_diag, residual, preferred_element_type=jnp.float32)
        solved_ticks.append(solved)
        outgoing = solved.astype(jnp.bfloat16)
        gathered = lax.all_gather(outgoing, "blk", axis=0, tiled=True)
        partial_value = slot_sum(held_blocks, source_list, live_count, gathered)
        if tick_index + 1 < tick_total:
            incoming = passed_along(partial_value, "grp", 1)
    return (jnp.stack(solved_ticks), partial_value)


def solution(mesh):
    placed = (
        P(None, ("grp", "blk"), None),
        P(("grp", "blk"), None),
        P(("grp", "blk"), None, None, None),
        P(("grp", "blk"), None),
        P(("grp", "blk")),
        P(("grp", "blk"), None),
    )
    return jax.shard_map(
        shards,
        mesh=mesh,
        in_specs=placed,
        out_specs=(P(None, ("grp", "blk"), None), P(("grp", "blk"), None)),
        check_vma=False,
    )
```

profile of v0, /device:TPU:298, one launch (start us, length us, event | category | flops | bytes accessed | tf_op | source)
XLA Modules:
  0.0 609.8 jit_solution(1359510496809689426)
XLA Ops:
  8.1 1.8 bitcast_convert_fusion.3
  9.9 61.4 %all-gather.5.cloned.1.call-done = bf16[8192,128]{0,1:T(8,128)(2,1)} async-done(((bf16[256,128]{0,1:T(8,128)(2,1)}), bf16[8192,128]{0,1:T(8,128)(2,1)}) %all-gather.5.cloned.1.call-update) | async-done | bytes 2097168 | tf_op jit(solution)/shard_map/all_gather | solution.py:40
  71.3 88.8 %while.40 = (s32[]{:T(128)}, f32[256,128]{1,0:T(8,128)S(1)}, s32[]{:T(128)}, bf16[24,256,256]{2,1,0:T(8,128)(2,1)}, s32[24]{0:T(128)}, /*index=5*/bf16[8192,128]...) while((s32[]{:T(128)}, f32[256,128]{1,0:T(8,128)S(1)}, s32[]{:T(128)}, ...), condition=%wide.region_1.2_spmd, body=%wide.region_0.1_spmd.sunk | while | flops 16809992 | bytes 458961 | solution.py:22
  72.0 1.2 dynamic_slice.75
  75.7 1.2 dynamic_slice.75
  86.7 1.2 dynamic_slice.75
  112.4 1.2 dynamic_slice.75
  123.4 1.2 dynamic_slice.75
  138.1 1.2 dynamic_slice.75
  149.1 1.2 dynamic_slice.75
  160.1 1.9 collective-permute-start
  162.1 4.9 collective-permute-done
  167.9 56.1 %all-gather.7.cloned.1.call-done = bf16[8192,128]{0,1:T(8,128)(2,1)} async-done(((bf16[256,128]{0,1:T(8,128)(2,1)}), bf16[8192,128]{0,1:T(8,128)(2,1)}) %all-gather.7.cloned.1.call-update) | async-done | bytes 2097168 | tf_op jit(solution)/shard_map/all_gather | solution.py:40
  224.0 88.8 %while.41 = (s32[]{:T(128)}, f32[256,128]{1,0:T(8,128)S(1)}, s32[]{:T(128)}, bf16[24,256,256]{2,1,0:T(8,128)(2,1)}, s32[24]{0:T(128)}, /*index=5*/bf16[8192,128]...) while((s32[]{:T(128)}, f32[256,128]{1,0:T(8,128)S(1)}, s32[]{:T(128)}, ...), condition=%wide.region_3.4_spmd, body=%wide.region_2.3_spmd.sunk | while | flops 16809992 | bytes 458961 | solution.py:22
  239.4 1.2 dynamic_slice.78
  250.4 1.2 dynamic_slice.78
  265.1 1.2 dynamic_slice.78
  276.1 1.2 dynamic_slice.78
  290.8 1.2 dynamic_slice.78
  301.8 1.2 dynamic_slice.78
  312.8 1.9 collective-permute-start.1
  314.8 4.9 collective-permute-done.1
  320.6 56.1 %all-gather.9.cloned.1.call-done = bf16[8192,128]{0,1:T(8,128)(2,1)} async-done(((bf16[256,128]{0,1:T(8,128)(2,1)}), bf16[8192,128]{0,1:T(8,128)(2,1)}) %all-gather.9.cloned.1.call-update) | async-done | bytes 2097168 | tf_op jit(solution)/shard_map/all_gather | solution.py:40
  376.8 88.8 %while.42 = (s32[]{:T(128)}, f32[256,128]{1,0:T(8,128)S(1)}, s32[]{:T(128)}, bf16[24,256,256]{2,1,0:T(8,128)(2,1)}, s32[24]{0:T(128)}, /*index=5*/bf16[8192,128]...) while((s32[]{:T(128)}, f32[256,128]{1,0:T(8,128)S(1)}, s32[]{:T(128)}, ...), condition=%wide.region_5.6_spmd, body=%wide.region_4.5_spmd.sunk | while | flops 16809992 | bytes 458961 | solution.py:22
  384.8 1.2 dynamic_slice.81
  399.5 1.2 dynamic_slice.81
  410.5 1.2 dynamic_slice.81
  436.2 1.2 dynamic_slice.81
  465.6 1.9 collective-permute-start.2
  467.5 4.9 collective-permute-done.2
  474.4 55.1 %all-gather.11.cloned.1.call-done = bf16[8192,128]{0,1:T(8,128)(2,1)} async-done(((bf16[256,128]{0,1:T(8,128)(2,1)}), bf16[8192,128]{0,1:T(8,128)(2,1)}) %all-gather.11.cloned.1.call-update) | async-done | bytes 2097168 | tf_op jit(solution)/shard_map/all_gather | solution.py:40
  529.5 73.1 %while.43 = (s32[]{:T(128)}, f32[256,128]{1,0:T(8,128)S(1)}, s32[]{:T(128)}, bf16[24,256,256]{2,1,0:T(8,128)(2,1)}, s32[24]{0:T(128)S(1)}, /*index=5*/bf16[8192,...) while((s32[]{:T(128)}, f32[256,128]{1,0:T(8,128)S(1)}, ...), condition=%wide.region_7.8_spmd, body=%wide.region_6.7_spmd.sunk | while | flops 16809992 | bytes 458961 | solution.py:22
  (200 shorter events, 193.3 us)
Async XLA Ops:
  7.2 0.9 copy-start
  7.2 159.8 %copy-start.2 = (f32[4,256,128]{2,1,0:T(8,128)S(1)}, f32[4,256,128]{2,1,0:T(8,128)}, u32[]{:S(2)}) copy-start(f32[4,256,128]{2,1,0:T(8,128)} %param.14) | copy-start | bytes 1572868
  7.2 64.1 %all-gather.5.cloned.1.call-start = ((), (), s32[]{:S(2)}) async-start(), calls=%async_computation | async-start | bytes 2162688 | tf_op jit(solution)/shard_map/all_gather | solution.py:40
  9.9 214.1 %all-gather.7.cloned.1.call-start = ((), (), s32[]{:S(2)}) async-start(), calls=%async_computation.1 | async-start | bytes 2162688 | tf_op jit(solution)/shard_map/all_gather | solution.py:40
  160.1 6.9 %collective-permute-start = (f32[256,128]{1,0:T(8,128)S(1)}, f32[256,128]{1,0:T(8,128)S(1)}, u32[]{:S(2)}, u32[]{:S(2)}) collective-permute-start(f32[256,128]{1,0:T(8,128)S(1)} %get-tuple-element.134), channel_id=1, source_target_pairs={{0,32},{32,64},{64,96},{96,128},{128,160},{160,192},{192,224},{224... | collective-permute-start | bytes 393224 | tf_op jit(solution)/shard_map/ppermute | solution.py:10
  167.9 208.9 %all-gather.9.cloned.1.call-start = ((), (), s32[]{:S(2)}) async-start(), calls=%async_computation.2 | async-start | bytes 2162688 | tf_op jit(solution)/shard_map/all_gather | solution.py:40
  312.8 6.9 %collective-permute-start.1 = (f32[256,128]{1,0:T(8,128)S(1)}, f32[256,128]{1,0:T(8,128)S(1)}, u32[]{:S(2)}, u32[]{:S(2)}) collective-permute-start(f32[256,128]{1,0:T(8,128)S(1)} %get-tuple-element.135), channel_id=1, source_target_pairs={{0,32},{32,64},{64,96},{96,128},{128,160},{160,192},{192,224},{224... | collective-permute-start | bytes 393224 | tf_op jit(solution)/shard_map/ppermute | solution.py:10
  320.6 208.9 %all-gather.11.cloned.1.call-start = ((), (), s32[]{:S(2)}) async-start(), calls=%async_computation.3 | async-start | bytes 2162688 | tf_op jit(solution)/shard_map/all_gather | solution.py:40
  465.6 63.9 %copy-start.3 = (s32[24]{0:T(128)S(1)}, s32[24]{0:T(128)}, u32[]{:S(2)}) copy-start(s32[24]{0:T(128)} %get-tuple-element.531) | copy-start | bytes 292
  465.6 6.9 %collective-permute-start.2 = (f32[256,128]{1,0:T(8,128)S(1)}, f32[256,128]{1,0:T(8,128)S(1)}, u32[]{:S(2)}, u32[]{:S(2)}) collective-permute-start(f32[256,128]{1,0:T(8,128)S(1)} %get-tuple-element.136), channel_id=1, source_target_pairs={{0,32},{32,64},{64,96},{96,128},{128,160},{160,192},{192,224},{224... | collective-permute-start | bytes 393224 | tf_op jit(solution)/shard_map/ppermute | solution.py:10
  602.6 0.7 copy-start.1
Sparse Core Ops, SparseCore 0:
  11.7 59.6 all-gather.4
  168.0 56.0 all-gather.6
  320.7 56.0 all-gather.8
  473.4 56.0 all-gather.10
where the time goes:
time: 614 us; the launch traced here: 610 us
  waiting for transfers between devices  244 us (40%)
  loops' own time  130 us (21%)
  matrix products  110 us (18%)
  local copies, waits for them, and re-layouts  106 us (17%)
  between operations  13.9 us (2%)
    all_gather x4, waiting for transfers between devices, shards(): gathered = lax.all_gather(outgoing, 'blk', axis=0, tiled=True)  229 us
    another operation x4, loops' own time, slot_sum(): lax.fori_loop(jnp.int32(0), upper_slot, add_slot, jnp.zeros((block_rows,...  130 us
    dot_general x96, matrix products, add_slot(): jnp.dot(matrix, block_piece, preferred_element_type=jnp.float32)  106 us
    dynamic_slice x96, local copies, waits for them, and re-layouts, add_slot(): source_list[k] * block_rows  104 us
    ppermute x3, waiting for transfers between devices, passed_along(): return lax.ppermute(value, axis, pairs)  14.8 us
  transfers between devices with their start and end apart: 7, of which 7 were waited for; matrix products, arithmetic and copies ran while one was open for 0% of the time, Pallas kernels for 0%

commit v1 on v0

v1 whole, which is shorter than its diff:
```python
import functools

import jax
import jax.numpy as jnp
from jax import lax
from jax.experimental import pallas as pl
from jax.experimental.pallas import tpu as pltpu
from jax.sharding import PartitionSpec as P

F32 = jnp.float32
BF16 = jnp.bfloat16
VMEM = pl.BlockSpec(memory_space=pltpu.VMEM)
SMEM = pl.BlockSpec(memory_space=pltpu.SMEM)
ANY = pl.BlockSpec(memory_space=pl.ANY)
LIMIT = 20 * 1024 * 1024


def params():
    return pltpu.CompilerParams(vmem_limit_bytes=LIMIT)


def mm(a, b):
    return jnp.dot(a, b, preferred_element_type=F32)


def combine_kernel(place, source_list, count, blocks, inverse, right, kept, handed, landing, sums, arrived):
    block = inverse.shape[0]
    live = count[0]
    own, sign, around = place[0], place[1], place[2]

    def copy_of(k):
        return pltpu.make_async_copy(blocks.at[0, k], landing.at[k], arrived.at[k])

    def begin(k, carry):
        copy_of(k).start()
        return carry

    lax.fori_loop(0, live, begin, 0)
    sums[...] = jnp.zeros_like(sums)
    handed[3 * block : 4 * block, :] = inverse[...]
    for tick in range(1, right.shape[0]):
        value = right[tick]
        high = value.astype(BF16)
        rows = pl.ds((3 + tick) * block, block)
        handed[rows, 0 : value.shape[1]] = high
        handed[rows, value.shape[1] :] = (value - high.astype(F32)).astype(BF16)

    def add(k, carry):
        copy_of(k).wait()
        offset = lax.rem(source_list[0, k] - own + 3 + around, around) - 3
        turned = offset * sign
        slot = jnp.where(k == 0, 4, jnp.where(turned >= 0, 3 - turned, 8 + turned))
        sums[slot] = sums[slot] + landing[k].astype(F32)
        return carry

    lax.fori_loop(0, live, add, 0)
    for i in range(5):
        kept[i] = sums[i].astype(BF16)
    for i in range(3):
        handed[i * block : (i + 1) * block, :] = sums[5 + i].astype(BF16)


def combine(place, sources, counts, factor_blocks, inverse_diag, right_side):
    slots, block = factor_blocks.shape[1], factor_blocks.shape[2]
    ticks = right_side.shape[0]
    return pl.pallas_call(
        combine_kernel,
        out_shape=(
            jax.ShapeDtypeStruct((5, block, block), BF16),
            jax.ShapeDtypeStruct(((3 + ticks) * block, block), BF16),
        ),
        in_specs=[SMEM, SMEM, SMEM, ANY, VMEM, VMEM],
        out_specs=(VMEM, VMEM),
        scratch_shapes=[
            pltpu.VMEM((slots, block, block), BF16),
            pltpu.VMEM((8, block, block), F32),
            pltpu.SemaphoreType.DMA((slots,)),
        ],
        compiler_params=params(),
        cost_estimate=pl.CostEstimate(flops=4_000_000, bytes_accessed=10_000_000, transcendentals=0),
        name="combine",
    )(place, sources, counts, factor_blocks, inverse_diag, right_side)


def first_kernel(right, incoming, inverse, solved, outgoing):
    value = mm(inverse[...], (right[0] - incoming[...]).astype(BF16))
    solved[...] = value
    outgoing[...] = value.astype(BF16)


def first_solve(right_side, carry_in, inverse_diag):
    ticks, block, columns = right_side.shape
    return pl.pallas_call(
        first_kernel,
        grid=(1,),
        out_shape=(
            jax.ShapeDtypeStruct((block, columns), F32),
            jax.ShapeDtypeStruct((block, columns), BF16),
        ),
        in_specs=[
            pl.BlockSpec((1, block, columns), lambda i: (0, 0, 0)),
            pl.BlockSpec((block, columns), lambda i: (0, 0)),
            pl.BlockSpec((block, block), lambda i: (0, 0)),
        ],
        out_specs=(
            pl.BlockSpec((block, columns), lambda i: (0, 0)),
            pl.BlockSpec((block, columns), lambda i: (0, 0)),
        ),
        compiler_params=params(),
        name="first",
    )(right_side, carry_in, inverse_diag)


def pair_kernel(tick, place, both, right, inverse, given, solved, outgoing):
    block, columns = solved.shape
    mine = place[3] * (2 * block)
    theirs = (1 - place[3]) * (2 * block)

    def part(at):
        return both[pl.ds(pl.multiple_of(at, block), block), :].astype(F32)

    incoming = part(mine) + part(theirs + block)
    other = part(mine + block) + part(theirs)
    value = mm(inverse[...], (right[tick] - incoming).astype(BF16))
    solved[...] = value
    outgoing[0:block] = value.astype(BF16)
    rows = pl.ds((3 + tick) * block, block)
    other_right = given[rows, 0:columns].astype(F32) + given[rows, columns:].astype(F32)
    value = mm(given[3 * block : 4 * block, :], (other_right - other).astype(BF16))
    outgoing[block:] = value.astype(BF16)


def pair_solve(tick, place, both, right_side, inverse_diag, given):
    ticks, block, columns = right_side.shape
    return pl.pallas_call(
        functools.partial(pair_kernel, tick),
        out_shape=(
            jax.ShapeDtypeStruct((block, columns), F32),
            jax.ShapeDtypeStruct((2 * block, columns), BF16),
        ),
        in_specs=[SMEM, VMEM, VMEM, VMEM, VMEM],
        out_specs=(VMEM, VMEM),
        compiler_params=params(),
        name="solve",
    )(place, both, right_side, inverse_diag, given)


def partial_kernel(place, kept, given, own, beside, third, opposite, sums, mine_exact):
    block = own.shape[0] // 2
    near = place[4] * (2 * block)

    def part(at):
        return beside[pl.ds(pl.multiple_of(at, block), block), :]

    odd_one, same_one = part(near), part(near + block)
    self_one = own[0:block]
    value = mm(kept[3], self_one)
    value += mm(kept[1], same_one)
    value += mm(kept[2], odd_one)
    value += mm(kept[0], third[...])
    value += mm(kept[4], opposite[...])
    other = mm(given[0:block, :], same_one)
    other += mm(given[block : 2 * block, :], odd_one)
    other += mm(given[2 * block : 3 * block, :], self_one)
    if mine_exact is not None:
        mine_exact[...] = value
        sums[...] = other.astype(BF16)
    else:
        sums[0:block] = value.astype(BF16)
        sums[block:] = other.astype(BF16)


def moving_kernel(place, kept, given, own, beside, third, opposite, sums):
    partial_kernel(place, kept, given, own, beside, third, opposite, sums, None)


def partial_sums(place, kept, given, own, beside, third, opposite, last):
    block, columns = third.shape
    if last:
        kernel = partial_kernel
        shapes = (
            jax.ShapeDtypeStruct((block, columns), BF16),
            jax.ShapeDtypeStruct((block, columns), F32),
        )
        specs = (VMEM, VMEM)
    else:
        kernel = moving_kernel
        shapes = jax.ShapeDtypeStruct((2 * block, columns), BF16)
        specs = VMEM
    return pl.pallas_call(
        kernel,
        out_shape=shapes,
        in_specs=[SMEM, VMEM, VMEM, VMEM, VMEM, VMEM, VMEM],
        out_specs=specs,
        compiler_params=params(),
        name="partial",
    )(place, kept, given, own, beside, third, opposite)


def carry_kernel(place, exact, both, carry):
    block = exact.shape[0]
    theirs = pl.multiple_of((1 - place[3]) * block, block)
    carry[...] = exact[...] + both[pl.ds(theirs, block), :].astype(F32)


def carry_sum(place, exact, both):
    return pl.pallas_call(
        carry_kernel,
        out_shape=jax.ShapeDtypeStruct(exact.shape, F32),
        in_specs=[SMEM, VMEM, VMEM],
        out_specs=VMEM,
        compiler_params=params(),
        name="carry",
    )(place, exact, both)


def shards(right_side, inverse_diag, factor_blocks, sources, counts, carry_in):
    ticks = right_side.shape[0]
    groups, around = lax.axis_size("grp"), lax.axis_size("blk")
    chips = around // 2
    at = lax.axis_index("blk").astype(jnp.int32)
    odd = lax.rem(at, 2)
    place = jnp.stack([at, 2 * odd - 1, jnp.int32(around), odd, odd])

    chip_pairs = [[2 * c, 2 * c + 1] for c in range(chips)]
    next_pairs = [[2 * c + 1, (2 * c + 2) % around] for c in range(chips)]
    third_of = [(2 * c + 1, (2 * c + 4) % around) for c in range(chips)]
    third_of = third_of + [(b, a) for a, b in third_of]
    opposite_of = [(b, (b + around // 2) % around) for b in range(around)]

    def paired(value, pairs):
        return lax.all_gather(value, "blk", axis=0, tiled=True, axis_index_groups=pairs)

    solved_ticks = []
    solved, first = first_solve(right_side, carry_in, inverse_diag)
    solved_ticks.append(solved)
    kept, handed = combine(place, sources, counts, factor_blocks, inverse_diag, right_side)
    given = lax.ppermute(handed, "blk", [(b, b ^ 1) for b in range(around)])
    carry = None
    for tick in range(ticks):
        if tick == 0:
            mine = first
            chip = paired(first, chip_pairs)
            own = jnp.where(odd == 0, chip, jnp.roll(chip, chip.shape[0] // 2, 0))
        else:
            mine = own[0 : own.shape[0] // 2]
        third = lax.ppermute(mine, "blk", third_of)
        opposite = lax.ppermute(mine, "blk", opposite_of)
        beside = paired(own, next_pairs)
        last = tick + 1 == ticks
        sums = partial_sums(place, kept, given, own, beside, third, opposite, last)
        if last:
            carry = carry_sum(place, sums[1], paired(sums[0], chip_pairs))
        else:
            moved = lax.ppermute(sums, "grp", [(g, g + 1) for g in range(groups - 1)])
            both = paired(moved, chip_pairs)
            solved, own = pair_solve(tick + 1, place, both, right_side, inverse_diag, given)
            solved_ticks.append(solved)
    return (jnp.stack(solved_ticks), carry)


def solution(mesh):
    placed = (
        P(None, ("grp", "blk"), None),
        P(("grp", "blk"), None),
        P(("grp", "blk"), None, None, None),
        P(("grp", "blk"), None),
        P(("grp", "blk")),
        P(("grp", "blk"), None),
    )
    return jax.shard_map(
        shards,
        mesh=mesh,
        in_specs=placed,
        out_specs=(P(None, ("grp", "blk"), None), P(("grp", "blk"), None)),
        check_vma=False,
    )
```

time: 614 us -> 117 us (0.19)
  the two profiles are of different devices: /device:TPU:298 before, /device:TPU:129 now
where the time goes in v1:
time: 117 us; the launch traced here: 116 us
  blocking collectives  47.1 us (40%)
  starting transfers between devices  37.3 us (32%)
  Pallas kernels  12.5 us (11%)
  waiting for transfers between devices  12.3 us (11%)
  local copies, waits for them, and re-layouts  4.62 us (4%)
  between operations  1.51 us (1%)
    all_gather x9, blocking collectives, paired(): lax.all_gather(value, 'blk', axis=0, tiled=True, axis_index_groups=pairs)  47.1 us
    ppermute x4, starting transfers between devices, shards(): opposite = lax.ppermute(mine, 'blk', opposite_of)  18.1 us
    ppermute x3, waiting for transfers between devices, shards(): moved = lax.ppermute(sums, 'grp', [(g, g + 1) for g in range(groups - 1)])  12.2 us
    ppermute x4, starting transfers between devices, shards(): third = lax.ppermute(mine, 'blk', third_of)  8.68 us
    ppermute x3, starting transfers between devices, shards(): moved = lax.ppermute(sums, 'grp', [(g, g + 1) for g in range(groups - 1)])  8.5 us
    pallas_call x1, Pallas kernels, combine(): pl.pallas_call(combine_kernel, out_shape=(jax.ShapeDtypeStruct((5, block,...  4.87 us
    unnamed x14, local copies, waits for them, and re-layouts  4.51 us
    pallas_call x4, Pallas kernels, partial_sums(): pl.pallas_call(kernel, out_shape=shapes, in_specs=[SMEM, VMEM, VMEM, VMEM...  3.89 us
  transfers between devices with their start and end apart: 12, of which 3 were waited for; matrix products, arithmetic and copies ran while one was open for 1% of the time, Pallas kernels for 0%

profile of v1, /device:TPU:129, one launch (start us, length us, event | category | flops | bytes accessed | tf_op | source)
XLA Modules:
  0.0 116.2 jit_solution(4194689374336524327)
XLA Ops:
  1.4 1.0 copy-done
  3.3 1.9 %copy-done.4 = bf16[1,24,256,256]{3,2,1,0:T(8,128)(2,1)S(1)} copy-done((bf16[1,24,256,256]{3,2,1,0:T(8,128)(2,1)S(1)}, bf16[1,24,256,256]{3,2,1,0:T(8,128)(2,1)}, u32[]{:S(2)}) %copy-start.4) | copy-done | bytes 3145752
  5.9 4.9 %combine.1 = (bf16[5,256,256]{2,1,0:T(8,128)(2,1)S(1)}, bf16[1792,256]{1,0:T(8,128)(2,1)S(1)}) custom-call(s32[5]{0:T(128)S(1)} %stack.32.place, s32[1,24]{1,0:T(1,128)S(1)} %copy-done.6, s32[1]{0:T(128)S(6)} %copy.8.count, bf16[1,24,256,256]{3,2,1,0:T(8,128)(2,1)S(1)} %copy-done.4, bf16[256,256]{1,0:T(8,128)(2,1)S(1)} %copy-done.2, f32[4,256,128]{2,1,0:T(8,128)S(1)} %copy-done), custom_call_target="tpu_custom_call" | custom-call | flops 4000000 | bytes 10000000 | tf_op jit(solution)/shard_map/combine/pallas_call | solution.py:66
  10.8 2.1 %collective-permute-start = (bf16[1792,256]{1,0:T(8,128)(2,1)S(1)}, bf16[1792,256]{1,0:T(8,128)(2,1)S(1)}, u32[]{:S(2)}, u32[]{:S(2)}) collective-permute-start(bf16[1792,256]{1,0:T(8,128)(2,1)S(1)} %get-tuple-element.16), channel_id=1, source_target_pairs={{0,1},{1,0},{2,3},{3,2},{4,5},{5,4},{6,7},{7,6},{8,9},{9,8},{10,11... | collective-permute-start | bytes 2752520 | tf_op jit(solution)/shard_map/ppermute | solution.py:238
  13.0 2.9 %collective-permute-start.1 = (bf16[256,128]{1,0:T(8,128)(2,1)S(1)}, bf16[256,128]{1,0:T(8,128)(2,1)S(1)}, u32[]{:S(2)}, u32[]{:S(2)}) collective-permute-start(bf16[256,128]{1,0:T(8,128)(2,1)S(1)} %get-tuple-element.17), channel_id=1, source_target_pairs={{1,4},{3,6},{5,8},{7,10},{9,12},{11,14},{13,16},{15,18},{17,20},{1... | collective-permute-start | bytes 196616 | tf_op jit(solution)/shard_map/ppermute | solution.py:247
  15.9 7.1 %collective-permute-start.2 = (bf16[256,128]{1,0:T(8,128)(2,1)S(1)}, bf16[256,128]{1,0:T(8,128)(2,1)S(1)}, u32[]{:S(2)}, u32[]{:S(2)}) collective-permute-start(bf16[256,128]{1,0:T(8,128)(2,1)S(1)} %get-tuple-element.17), channel_id=1, source_target_pairs={{0,16},{1,17},{2,18},{3,19},{4,20},{5,21},{6,22},{7,23},{8,24},{9,... | collective-permute-start | bytes 196616 | tf_op jit(solution)/shard_map/ppermute | solution.py:248
  23.1 1.9 %all_gather.27 = bf16[512,128]{1,0:T(8,128)(2,1)S(1)} all-gather(bf16[256,128]{1,0:T(8,128)(2,1)S(1)} %get-tuple-element.17), channel_id=1, replica_groups={{0,1},{2,3},{4,5},{6,7},{8,9},{10,11},{12,13},{14,15},{16,17},{18,19},{..., dimensions={0}, use_global_device_ids=true | all-gather | bytes 196608 | tf_op jit(solution)/shard_map/all_gather | solution.py:232
  25.0 5.4 %all_gather.28.beside = bf16[1024,128]{1,0:T(8,128)(2,1)S(1)} all-gather(bf16[512,128]{1,0:T(8,128)(2,1)S(1)} %maximum_select_fusion.own), channel_id=1, replica_groups={{1,2},{3,4},{5,6},{7,8},{9,10},{11,12},{13,14},{15,16},{17,18},{19,20},..., dimensions={0}, use_global_device_ids=true | all-gather | bytes 393216 | tf_op jit(solution)/shard_map/all_gather | solution.py:232
  30.4 1.0 partial.4
  31.4 3.8 %collective-permute-start.3 = (bf16[512,128]{1,0:T(8,128)(2,1)S(1)}, bf16[512,128]{1,0:T(8,128)(2,1)S(1)}, u32[]{:S(2)}, u32[]{:S(2)}) collective-permute-start(bf16[512,128]{1,0:T(8,128)(2,1)S(1)} %partial.4), channel_id=1, source_target_pairs={{0,32},{32,64},{64,96},{96,128},{128,160},{160,192},{192,224},{224... | collective-permute-start | bytes 393224 | tf_op jit(solution)/shard_map/ppermute | solution.py:255
  35.2 3.1 %collective-permute-done.3 = bf16[512,128]{1,0:T(8,128)(2,1)S(1)} collective-permute-done((bf16[512,128]{1,0:T(8,128)(2,1)S(1)}, bf16[512,128]{1,0:T(8,128)(2,1)S(1)}, u32[]{:S(2)}, u32[]{:S(2)}) %collective-permute-start.3) | collective-permute-done | bytes 131104 | tf_op jit(solution)/shard_map/ppermute | solution.py:255
  38.3 6.0 %all_gather.29.both = bf16[1024,128]{1,0:T(8,128)(2,1)S(1)} all-gather(bf16[512,128]{1,0:T(8,128)(2,1)S(1)} %collective-permute-done.3), channel_id=1, replica_groups={{0,1},{2,3},{4,5},{6,7},{8,9},{10,11},{12,13},{14,15},{16,17},{18,19},{..., dimensions={0}, use_global_device_ids=true | all-gather | bytes 393216 | tf_op jit(solution)/shard_map/all_gather | solution.py:232
  45.1 1.9 %collective-permute-start.4 = (bf16[256,128]{1,0:T(8,128)(2,1)S(1)}, bf16[256,128]{1,0:T(8,128)(2,1)S(1)}, u32[]{:S(2)}, u32[]{:S(2)}) collective-permute-start(bf16[256,128]{1,0:T(8,128)(2,1)S(1)} %slice.19), channel_id=1, source_target_pairs={{1,4},{3,6},{5,8},{7,10},{9,12},{11,14},{13,16},{15,18},{17,20},{1... | collective-permute-start | bytes 196616 | tf_op jit(solution)/shard_map/ppermute | solution.py:247
  47.0 3.4 %collective-permute-start.5 = (bf16[256,128]{1,0:T(8,128)(2,1)S(1)}, bf16[256,128]{1,0:T(8,128)(2,1)S(1)}, u32[]{:S(2)}, u32[]{:S(2)}) collective-permute-start(bf16[256,128]{1,0:T(8,128)(2,1)S(1)} %slice.19), channel_id=1, source_target_pairs={{0,16},{1,17},{2,18},{3,19},{4,20},{5,21},{6,22},{7,23},{8,24},{9,... | collective-permute-start | bytes 196616 | tf_op jit(solution)/shard_map/ppermute | solution.py:248
  50.4 5.1 %all_gather.30.beside = bf16[1024,128]{1,0:T(8,128)(2,1)S(1)} all-gather(bf16[512,128]{1,0:T(8,128)(2,1)S(1)} %get-tuple-element.19.own), channel_id=1, replica_groups={{1,2},{3,4},{5,6},{7,8},{9,10},{11,12},{13,14},{15,16},{17,18},{19,20},..., dimensions={0}, use_global_device_ids=true | all-gather | bytes 393216 | tf_op jit(solution)/shard_map/all_gather | solution.py:232
  55.5 1.0 partial.5
  56.4 2.8 %collective-permute-start.6 = (bf16[512,128]{1,0:T(8,128)(2,1)S(1)}, bf16[512,128]{1,0:T(8,128)(2,1)S(1)}, u32[]{:S(2)}, u32[]{:S(2)}) collective-permute-start(bf16[512,128]{1,0:T(8,128)(2,1)S(1)} %partial.5), channel_id=1, source_target_pairs={{0,32},{32,64},{64,96},{96,128},{128,160},{160,192},{192,224},{224... | collective-permute-start | bytes 393224 | tf_op jit(solution)/shard_map/ppermute | solution.py:255
  59.2 4.1 %collective-permute-done.6 = bf16[512,128]{1,0:T(8,128)(2,1)S(1)} collective-permute-done((bf16[512,128]{1,0:T(8,128)(2,1)S(1)}, bf16[512,128]{1,0:T(8,128)(2,1)S(1)}, u32[]{:S(2)}, u32[]{:S(2)}) %collective-permute-start.6) | collective-permute-done | bytes 131104 | tf_op jit(solution)/shard_map/ppermute | solution.py:255
  63.4 6.7 %all_gather.31.both = bf16[1024,128]{1,0:T(8,128)(2,1)S(1)} all-gather(bf16[512,128]{1,0:T(8,128)(2,1)S(1)} %collective-permute-done.6), channel_id=1, replica_groups={{0,1},{2,3},{4,5},{6,7},{8,9},{10,11},{12,13},{14,15},{16,17},{18,19},{..., dimensions={0}, use_global_device_ids=true | all-gather | bytes 393216 | tf_op jit(solution)/shard_map/all_gather | solution.py:232
  70.9 1.9 %collective-permute-start.7 = (bf16[256,128]{1,0:T(8,128)(2,1)S(1)}, bf16[256,128]{1,0:T(8,128)(2,1)S(1)}, u32[]{:S(2)}, u32[]{:S(2)}) collective-permute-start(bf16[256,128]{1,0:T(8,128)(2,1)S(1)} %slice.20), channel_id=1, source_target_pairs={{1,4},{3,6},{5,8},{7,10},{9,12},{11,14},{13,16},{15,18},{17,20},{1... | collective-permute-start | bytes 196616 | tf_op jit(solution)/shard_map/ppermute | solution.py:247
  72.8 3.8 %collective-permute-start.8 = (bf16[256,128]{1,0:T(8,128)(2,1)S(1)}, bf16[256,128]{1,0:T(8,128)(2,1)S(1)}, u32[]{:S(2)}, u32[]{:S(2)}) collective-permute-start(bf16[256,128]{1,0:T(8,128)(2,1)S(1)} %slice.20), channel_id=1, source_target_pairs={{0,16},{1,17},{2,18},{3,19},{4,20},{5,21},{6,22},{7,23},{8,24},{9,... | collective-permute-start | bytes 196616 | tf_op jit(solution)/shard_map/ppermute | solution.py:248
  76.7 5.4 %all_gather.32.beside = bf16[1024,128]{1,0:T(8,128)(2,1)S(1)} all-gather(bf16[512,128]{1,0:T(8,128)(2,1)S(1)} %get-tuple-element.21.own), channel_id=1, replica_groups={{1,2},{3,4},{5,6},{7,8},{9,10},{11,12},{13,14},{15,16},{17,18},{19,20},..., dimensions={0}, use_global_device_ids=true | all-gather | bytes 393216 | tf_op jit(solution)/shard_map/all_gather | solution.py:232
  82.1 1.0 partial.6
  83.0 1.9 %collective-permute-start.9 = (bf16[512,128]{1,0:T(8,128)(2,1)S(1)}, bf16[512,128]{1,0:T(8,128)(2,1)S(1)}, u32[]{:S(2)}, u32[]{:S(2)}) collective-permute-start(bf16[512,128]{1,0:T(8,128)(2,1)S(1)} %partial.6), channel_id=1, source_target_pairs={{0,32},{32,64},{64,96},{96,128},{128,160},{160,192},{192,224},{224... | collective-permute-start | bytes 393224 | tf_op jit(solution)/shard_map/ppermute | solution.py:255
  85.0 5.0 %collective-permute-done.9 = bf16[512,128]{1,0:T(8,128)(2,1)S(1)} collective-permute-done((bf16[512,128]{1,0:T(8,128)(2,1)S(1)}, bf16[512,128]{1,0:T(8,128)(2,1)S(1)}, u32[]{:S(2)}, u32[]{:S(2)}) %collective-permute-start.9) | collective-permute-done | bytes 131104 | tf_op jit(solution)/shard_map/ppermute | solution.py:255
  90.0 6.1 %all_gather.33.both = bf16[1024,128]{1,0:T(8,128)(2,1)S(1)} all-gather(bf16[512,128]{1,0:T(8,128)(2,1)S(1)} %collective-permute-done.9), channel_id=1, replica_groups={{0,1},{2,3},{4,5},{6,7},{8,9},{10,11},{12,13},{14,15},{16,17},{18,19},{..., dimensions={0}, use_global_device_ids=true | all-gather | bytes 393216 | tf_op jit(solution)/shard_map/all_gather | solution.py:232
  96.9 1.9 %collective-permute-start.10 = (bf16[256,128]{1,0:T(8,128)(2,1)S(1)}, bf16[256,128]{1,0:T(8,128)(2,1)S(1)}, u32[]{:S(2)}, u32[]{:S(2)}) collective-permute-start(bf16[256,128]{1,0:T(8,128)(2,1)S(1)} %slice.21), channel_id=1, source_target_pairs={{1,4},{3,6},{5,8},{7,10},{9,12},{11,14},{13,16},{15,18},{17,20},{1... | collective-permute-start | bytes 196616 | tf_op jit(solution)/shard_map/ppermute | solution.py:247
  98.8 3.8 %collective-permute-start.11 = (bf16[256,128]{1,0:T(8,128)(2,1)S(1)}, bf16[256,128]{1,0:T(8,128)(2,1)S(1)}, u32[]{:S(2)}, u32[]{:S(2)}) collective-permute-start(bf16[256,128]{1,0:T(8,128)(2,1)S(1)} %slice.21), channel_id=1, source_target_pairs={{0,16},{1,17},{2,18},{3,19},{4,20},{5,21},{6,22},{7,23},{8,24},{9,... | collective-permute-start | bytes 196616 | tf_op jit(solution)/shard_map/ppermute | solution.py:248
  103.4 5.1 %all_gather.34.beside = bf16[1024,128]{1,0:T(8,128)(2,1)S(1)} all-gather(bf16[512,128]{1,0:T(8,128)(2,1)S(1)} %get-tuple-element.23.own), channel_id=1, replica_groups={{1,2},{3,4},{5,6},{7,8},{9,10},{11,12},{13,14},{15,16},{17,18},{19,20},..., dimensions={0}, use_global_device_ids=true | all-gather | bytes 393216 | tf_op jit(solution)/shard_map/all_gather | solution.py:232
  108.5 1.0 partial.7
  109.5 5.5 %all_gather.35.both = bf16[512,128]{1,0:T(8,128)(2,1)S(1)} all-gather(bf16[256,128]{1,0:T(8,128)(2,1)S(1)} %get-tuple-element.25), channel_id=1, replica_groups={{0,1},{2,3},{4,5},{6,7},{8,9},{10,11},{12,13},{14,15},{16,17},{18,19},{..., dimensions={0}, use_global_device_ids=true | all-gather | bytes 196608 | tf_op jit(solution)/shard_map/all_gather | solution.py:232
  115.0 1.2 %carry.1 = f32[256,128]{1,0:T(8,128)} custom-call(s32[5]{0:T(128)S(1)} %stack.32.place, f32[256,128]{1,0:T(8,128)S(1)} %get-tuple-element.24.exact, bf16[512,128]{1,0:T(8,128)(2,1)S(1)} %all_gather.35.both), custom_call_target="tpu_custom_call" | custom-call | tf_op jit(solution)/shard_map/carry/pallas_call | solution.py:207
  (32 shorter events, 5.1 us)
Async XLA Ops:
  1.4 1.0 copy-start
  2.4 0.9 copy-start.2
  3.3 1.9 %copy-start.4 = (bf16[1,24,256,256]{3,2,1,0:T(8,128)(2,1)S(1)}, bf16[1,24,256,256]{3,2,1,0:T(8,128)(2,1)}, u32[]{:S(2)}) copy-start(bf16[1,24,256,256]{3,2,1,0:T(8,128)(2,1)} %blocks.1) | copy-start | bytes 9437188
  5.2 0.7 copy-start.6
  5.9 7.0 %copy-start.5 = (f32[256,128]{1,0:T(8,128)S(1)}, f32[256,128]{1,0:T(8,128)}, u32[]{:S(2)}) copy-start(f32[256,128]{1,0:T(8,128)} %incoming.1) | copy-start | bytes 393220
  10.7 33.5 %copy-start.1 = (f32[4,256,128]{2,1,0:T(8,128)S(1)}, f32[4,256,128]{2,1,0:T(8,128)}, u32[]{:S(2)}) copy-start(f32[4,256,128]{2,1,0:T(8,128)} %right.9) | copy-start | bytes 1572868
  10.8 33.5 %copy-start.3 = (bf16[256,256]{1,0:T(8,128)(2,1)S(1)}, bf16[256,256]{1,0:T(8,128)(2,1)}, u32[]{:S(2)}) copy-start(bf16[256,256]{1,0:T(8,128)(2,1)} %inverse.9) | copy-start | bytes 393220
  10.8 19.6 %collective-permute-start = (bf16[1792,256]{1,0:T(8,128)(2,1)S(1)}, bf16[1792,256]{1,0:T(8,128)(2,1)S(1)}, u32[]{:S(2)}, u32[]{:S(2)}) collective-permute-start(bf16[1792,256]{1,0:T(8,128)(2,1)S(1)} %get-tuple-element.16), channel_id=1, source_target_pairs={{0,1},{1,0},{2,3},{3,2},{4,5},{5,4},{6,7},{7,6},{8,9},{9,8},{10,11... | collective-permute-start | bytes 2752520 | tf_op jit(solution)/shard_map/ppermute | solution.py:238
  13.0 17.4 %collective-permute-start.1 = (bf16[256,128]{1,0:T(8,128)(2,1)S(1)}, bf16[256,128]{1,0:T(8,128)(2,1)S(1)}, u32[]{:S(2)}, u32[]{:S(2)}) collective-permute-start(bf16[256,128]{1,0:T(8,128)(2,1)S(1)} %get-tuple-element.17), channel_id=1, source_target_pairs={{1,4},{3,6},{5,8},{7,10},{9,12},{11,14},{13,16},{15,18},{17,20},{1... | collective-permute-start | bytes 196616 | tf_op jit(solution)/shard_map/ppermute | solution.py:247
  15.9 14.5 %collective-permute-start.2 = (bf16[256,128]{1,0:T(8,128)(2,1)S(1)}, bf16[256,128]{1,0:T(8,128)(2,1)S(1)}, u32[]{:S(2)}, u32[]{:S(2)}) collective-permute-start(bf16[256,128]{1,0:T(8,128)(2,1)S(1)} %get-tuple-element.17), channel_id=1, source_target_pairs={{0,16},{1,17},{2,18},{3,19},{4,20},{5,21},{6,22},{7,23},{8,24},{9,... | collective-permute-start | bytes 196616 | tf_op jit(solution)/shard_map/ppermute | solution.py:248
  31.4 6.9 %collective-permute-start.3 = (bf16[512,128]{1,0:T(8,128)(2,1)S(1)}, bf16[512,128]{1,0:T(8,128)(2,1)S(1)}, u32[]{:S(2)}, u32[]{:S(2)}) collective-permute-start(bf16[512,128]{1,0:T(8,128)(2,1)S(1)} %partial.4), channel_id=1, source_target_pairs={{0,32},{32,64},{64,96},{96,128},{128,160},{160,192},{192,224},{224... | collective-permute-start | bytes 393224 | tf_op jit(solution)/shard_map/ppermute | solution.py:255
  45.1 10.4 %collective-permute-start.4 = (bf16[256,128]{1,0:T(8,128)(2,1)S(1)}, bf16[256,128]{1,0:T(8,128)(2,1)S(1)}, u32[]{:S(2)}, u32[]{:S(2)}) collective-permute-start(bf16[256,128]{1,0:T(8,128)(2,1)S(1)} %slice.19), channel_id=1, source_target_pairs={{1,4},{3,6},{5,8},{7,10},{9,12},{11,14},{13,16},{15,18},{17,20},{1... | collective-permute-start | bytes 196616 | tf_op jit(solution)/shard_map/ppermute | solution.py:247
  47.0 8.5 %collective-permute-start.5 = (bf16[256,128]{1,0:T(8,128)(2,1)S(1)}, bf16[256,128]{1,0:T(8,128)(2,1)S(1)}, u32[]{:S(2)}, u32[]{:S(2)}) collective-permute-start(bf16[256,128]{1,0:T(8,128)(2,1)S(1)} %slice.19), channel_id=1, source_target_pairs={{0,16},{1,17},{2,18},{3,19},{4,20},{5,21},{6,22},{7,23},{8,24},{9,... | collective-permute-start | bytes 196616 | tf_op jit(solution)/shard_map/ppermute | solution.py:248
  56.4 6.9 %collective-permute-start.6 = (bf16[512,128]{1,0:T(8,128)(2,1)S(1)}, bf16[512,128]{1,0:T(8,128)(2,1)S(1)}, u32[]{:S(2)}, u32[]{:S(2)}) collective-permute-start(bf16[512,128]{1,0:T(8,128)(2,1)S(1)} %partial.5), channel_id=1, source_target_pairs={{0,32},{32,64},{64,96},{96,128},{128,160},{160,192},{192,224},{224... | collective-permute-start | bytes 393224 | tf_op jit(solution)/shard_map/ppermute | solution.py:255
  70.9 11.1 %collective-permute-start.7 = (bf16[256,128]{1,0:T(8,128)(2,1)S(1)}, bf16[256,128]{1,0:T(8,128)(2,1)S(1)}, u32[]{:S(2)}, u32[]{:S(2)}) collective-permute-start(bf16[256,128]{1,0:T(8,128)(2,1)S(1)} %slice.20), channel_id=1, source_target_pairs={{1,4},{3,6},{5,8},{7,10},{9,12},{11,14},{13,16},{15,18},{17,20},{1... | collective-permute-start | bytes 196616 | tf_op jit(solution)/shard_map/ppermute | solution.py:247
  72.8 9.2 %collective-permute-start.8 = (bf16[256,128]{1,0:T(8,128)(2,1)S(1)}, bf16[256,128]{1,0:T(8,128)(2,1)S(1)}, u32[]{:S(2)}, u32[]{:S(2)}) collective-permute-start(bf16[256,128]{1,0:T(8,128)(2,1)S(1)} %slice.20), channel_id=1, source_target_pairs={{0,16},{1,17},{2,18},{3,19},{4,20},{5,21},{6,22},{7,23},{8,24},{9,... | collective-permute-start | bytes 196616 | tf_op jit(solution)/shard_map/ppermute | solution.py:248
  83.0 6.9 %collective-permute-start.9 = (bf16[512,128]{1,0:T(8,128)(2,1)S(1)}, bf16[512,128]{1,0:T(8,128)(2,1)S(1)}, u32[]{:S(2)}, u32[]{:S(2)}) collective-permute-start(bf16[512,128]{1,0:T(8,128)(2,1)S(1)} %partial.6), channel_id=1, source_target_pairs={{0,32},{32,64},{64,96},{96,128},{128,160},{160,192},{192,224},{224... | collective-permute-start | bytes 393224 | tf_op jit(solution)/shard_map/ppermute | solution.py:255
  96.9 11.6 %collective-permute-start.10 = (bf16[256,128]{1,0:T(8,128)(2,1)S(1)}, bf16[256,128]{1,0:T(8,128)(2,1)S(1)}, u32[]{:S(2)}, u32[]{:S(2)}) collective-permute-start(bf16[256,128]{1,0:T(8,128)(2,1)S(1)} %slice.21), channel_id=1, source_target_pairs={{1,4},{3,6},{5,8},{7,10},{9,12},{11,14},{13,16},{15,18},{17,20},{1... | collective-permute-start | bytes 196616 | tf_op jit(solution)/shard_map/ppermute | solution.py:247
  98.8 9.7 %collective-permute-start.11 = (bf16[256,128]{1,0:T(8,128)(2,1)S(1)}, bf16[256,128]{1,0:T(8,128)(2,1)S(1)}, u32[]{:S(2)}, u32[]{:S(2)}) collective-permute-start(bf16[256,128]{1,0:T(8,128)(2,1)S(1)} %slice.21), channel_id=1, source_target_pairs={{0,16},{1,17},{2,18},{3,19},{4,20},{5,21},{6,22},{7,23},{8,24},{9,... | collective-permute-start | bytes 196616 | tf_op jit(solution)/shard_map/ppermute | solution.py:248

commit v2 on v1

v2 whole, which is shorter than its diff:
```python
import functools

import jax
import jax.numpy as jnp
from jax import lax
from jax.experimental import pallas as pl
from jax.experimental.pallas import tpu as pltpu
from jax.sharding import PartitionSpec as P

F32 = jnp.float32
BF16 = jnp.bfloat16
VMEM = pl.BlockSpec(memory_space=pltpu.VMEM)
SMEM = pl.BlockSpec(memory_space=pltpu.SMEM)
HBM = pl.BlockSpec(memory_space=pltpu.HBM)
LIMIT = 20 * 1024 * 1024


def params():
    return pltpu.CompilerParams(vmem_limit_bytes=LIMIT)


def mm(a, b):
    return jnp.dot(a, b, preferred_element_type=F32)


def combine_kernel(around, source_list, count, blocks, inverse, right, kept, handed, landing, sums, arrived):
    block = inverse.shape[0]
    live = count[0]
    own = lax.axis_index("blk")
    sign = 2 * lax.rem(own, 2) - 1

    def copy_of(k):
        return pltpu.make_async_copy(blocks.at[0, k], landing.at[k], arrived.at[k])

    def begin(k, carry):
        copy_of(k).start()
        return carry

    lax.fori_loop(0, live, begin, 0)
    sums[...] = jnp.zeros_like(sums)
    handed[3 * block : 4 * block, :] = inverse[...]
    for tick in range(1, right.shape[0]):
        value = right[tick]
        high = value.astype(BF16)
        rows = pl.ds((3 + tick) * block, block)
        handed[rows, 0 : value.shape[1]] = high
        handed[rows, value.shape[1] :] = (value - high.astype(F32)).astype(BF16)

    def add(k, carry):
        copy_of(k).wait()
        offset = lax.rem(source_list[0, k] - own + 3 + around, around) - 3
        turned = offset * sign
        slot = jnp.where(k == 0, 4, jnp.where(turned >= 0, 3 - turned, 8 + turned))
        sums[slot] = sums[slot] + landing[k].astype(F32)
        return carry

    lax.fori_loop(0, live, add, 0)
    for i in range(5):
        kept[i] = sums[i].astype(BF16)
    for i in range(3):
        handed[i * block : (i + 1) * block, :] = sums[5 + i].astype(BF16)


def combine(around, sources, counts, factor_blocks, inverse_diag, right_side):
    slots, block = factor_blocks.shape[1], factor_blocks.shape[2]
    ticks = right_side.shape[0]
    return pl.pallas_call(
        functools.partial(combine_kernel, around),
        out_shape=(
            jax.ShapeDtypeStruct((5, block, block), BF16),
            jax.ShapeDtypeStruct(((3 + ticks) * block, block), BF16),
        ),
        in_specs=[SMEM, SMEM, HBM, VMEM, VMEM],
        out_specs=(VMEM, VMEM),
        scratch_shapes=[
            pltpu.VMEM((slots, block, block), BF16),
            pltpu.VMEM((8, block, block), F32),
            pltpu.SemaphoreType.DMA((slots,)),
        ],
        compiler_params=params(),
        cost_estimate=pl.CostEstimate(flops=4_000_000, bytes_accessed=10_000_000, transcendentals=0),
        name="combine",
    )(sources, counts, factor_blocks, inverse_diag, right_side)


def first_kernel(right, incoming, inverse, solved, outgoing, right_here, incoming_here, inverse_here, arrived):
    copies = (
        pltpu.make_async_copy(right.at[0], right_here, arrived.at[0]),
        pltpu.make_async_copy(incoming, incoming_here, arrived.at[1]),
        pltpu.make_async_copy(inverse, inverse_here, arrived.at[2]),
    )
    for copy in copies:
        copy.start()
    for copy in copies:
        copy.wait()
    value = mm(inverse_here[...], (right_here[...] - incoming_here[...]).astype(BF16))
    solved[...] = value
    outgoing[...] = value.astype(BF16)


def first_solve(right_side, carry_in, inverse_diag):
    ticks, block, columns = right_side.shape
    return pl.pallas_call(
        first_kernel,
        out_shape=(
            jax.ShapeDtypeStruct((block, columns), F32),
            jax.ShapeDtypeStruct((block, columns), BF16),
        ),
        in_specs=[HBM, HBM, HBM],
        out_specs=(VMEM, VMEM),
        scratch_shapes=[
            pltpu.VMEM((block, columns), F32),
            pltpu.VMEM((block, columns), F32),
            pltpu.VMEM((block, block), BF16),
            pltpu.SemaphoreType.DMA((3,)),
        ],
        compiler_params=params(),
        name="first",
    )(right_side, carry_in, inverse_diag)


def pair_kernel(tick, both, right, inverse, given, solved, outgoing):
    block, columns = solved.shape
    odd = lax.rem(lax.axis_index("blk"), 2)
    mine = odd * (2 * block)
    theirs = (1 - odd) * (2 * block)

    def part(at):
        return both[pl.ds(pl.multiple_of(at, block), block), :].astype(F32)

    incoming = part(mine) + part(theirs + block)
    other = part(mine + block) + part(theirs)
    value = mm(inverse[...], (right[tick] - incoming).astype(BF16))
    solved[...] = value
    outgoing[0:block] = value.astype(BF16)
    rows = pl.ds((3 + tick) * block, block)
    other_right = given[rows, 0:columns].astype(F32) + given[rows, columns:].astype(F32)
    value = mm(given[3 * block : 4 * block, :], (other_right - other).astype(BF16))
    outgoing[block:] = value.astype(BF16)


def pair_solve(tick, both, right_side, inverse_diag, given):
    ticks, block, columns = right_side.shape
    return pl.pallas_call(
        functools.partial(pair_kernel, tick),
        out_shape=(
            jax.ShapeDtypeStruct((block, columns), F32),
            jax.ShapeDtypeStruct((2 * block, columns), BF16),
        ),
        in_specs=[VMEM, VMEM, VMEM, VMEM],
        out_specs=(VMEM, VMEM),
        compiler_params=params(),
        name="solve",
    )(both, right_side, inverse_diag, given)


def partial_kernel(tick, last, kept, given, own, beside, third, opposite, solved, *refs):
    sums, outputs, leaving = refs[-3:]
    copy = pltpu.make_async_copy(solved, outputs.at[tick], leaving)
    copy.start()
    block = own.shape[0] // 2
    near = lax.rem(lax.axis_index("blk"), 2) * (2 * block)

    def part(at):
        return beside[pl.ds(pl.multiple_of(at, block), block), :]

    odd_one, same_one = part(near), part(near + block)
    self_one = own[0:block]
    value = mm(kept[3], self_one)
    value += mm(kept[1], same_one)
    value += mm(kept[2], odd_one)
    value += mm(kept[0], third[...])
    value += mm(kept[4], opposite[...])
    other = mm(given[0:block, :], same_one)
    other += mm(given[block : 2 * block, :], odd_one)
    other += mm(given[2 * block : 3 * block, :], self_one)
    if last:
        refs[-4][...] = value
        sums[...] = other.astype(BF16)
    else:
        sums[0:block] = value.astype(BF16)
        sums[block:] = other.astype(BF16)
    copy.wait()


def partial_sums(tick, ticks, kept, given, own, beside, third, opposite, solved, outputs):
    block, columns = third.shape
    last = tick + 1 == ticks
    shapes = [jax.ShapeDtypeStruct((ticks, block, columns), F32)]
    specs = [VMEM, HBM]
    if last:
        shapes = [
            jax.ShapeDtypeStruct((block, columns), F32),
            jax.ShapeDtypeStruct((block, columns), BF16),
        ] + shapes
        specs = [VMEM] + specs
    else:
        shapes = [jax.ShapeDtypeStruct((2 * block, columns), BF16)] + shapes
    operands = [kept, given, own, beside, third, opposite, solved]
    in_specs = [VMEM] * 7
    aliases = {}
    if outputs is not None:
        aliases = {len(operands): len(shapes) - 1}
        operands.append(outputs)
        in_specs.append(HBM)
    return pl.pallas_call(
        functools.partial(partial_kernel, tick, last),
        out_shape=tuple(shapes),
        in_specs=in_specs,
        out_specs=tuple(specs),
        input_output_aliases=aliases,
        scratch_shapes=[pltpu.SemaphoreType.DMA],
        compiler_params=params(),
        name="partial",
    )(*operands)


def carry_kernel(exact, both, carry):
    block = exact.shape[0]
    odd = lax.rem(lax.axis_index("blk"), 2)
    theirs = pl.multiple_of((1 - odd) * block, block)
    carry[...] = exact[...] + both[pl.ds(theirs, block), :].astype(F32)


def carry_sum(exact, both):
    return pl.pallas_call(
        carry_kernel,
        out_shape=jax.ShapeDtypeStruct(exact.shape, F32),
        in_specs=[VMEM, VMEM],
        out_specs=VMEM,
        compiler_params=params(),
        name="carry",
    )(exact, both)


def shards(right_side, inverse_diag, factor_blocks, sources, counts, carry_in):
    ticks, block = right_side.shape[0], right_side.shape[1]
    groups, around = lax.axis_size("grp"), lax.axis_size("blk")
    chips = around // 2
    at = lax.axis_index("blk").astype(jnp.int32)
    odd = lax.rem(at, 2)
    chip_pairs = [[2 * c, 2 * c + 1] for c in range(chips)]
    next_pairs = [[2 * c + 1, (2 * c + 2) % around] for c in range(chips)]
    third_pairs = [[2 * c + 1, (2 * c + 4) % around] for c in range(chips)]
    opposite_pairs = [[b, b + chips] for b in range(chips)]

    def paired(value, pairs):
        return lax.all_gather(value, "blk", axis=0, tiled=True, axis_index_groups=pairs)

    def swapped(value, pairs):
        partner = [(a, b) for a, b in pairs] + [(b, a) for a, b in pairs]
        return lax.ppermute(value, "blk", partner)

    solved, own = first_solve(right_side, carry_in, inverse_diag)
    outputs = kept = given = None
    for tick in range(ticks):
        mine = own[0:block]
        third = swapped(mine, third_pairs)
        opposite = swapped(mine, opposite_pairs)
        if tick == 0:
            chip = paired(own, chip_pairs)
            own = jnp.where(odd == 0, chip, jnp.roll(chip, block, 0))
            near = swapped(own, next_pairs)
            beside = jnp.concatenate([near, near], 0)
            held = (sources, counts, factor_blocks, inverse_diag, right_side)
            held = lax.optimization_barrier((own, *held))[1:]
            kept, handed = combine(around, *held)
            given = swapped(handed, chip_pairs)
        else:
            beside = paired(own, next_pairs)
        *sums, outputs = partial_sums(tick, ticks, kept, given, own, beside, third, opposite, solved, outputs)
        if tick + 1 == ticks:
            carry = carry_sum(sums[0], paired(sums[1], chip_pairs))
        else:
            moved = lax.ppermute(sums[0], "grp", [(g, g + 1) for g in range(groups - 1)])
            both = paired(moved, chip_pairs)
            solved, own = pair_solve(tick + 1, both, right_side, inverse_diag, given)
    return (outputs, carry)


def solution(mesh):
    placed = (
        P(None, ("grp", "blk"), None),
        P(("grp", "blk"), None),
        P(("grp", "blk"), None, None, None),
        P(("grp", "blk"), None),
        P(("grp", "blk")),
        P(("grp", "blk"), None),
    )
    return jax.shard_map(
        shards,
        mesh=mesh,
        in_specs=placed,
        out_specs=(P(None, ("grp", "blk"), None), P(("grp", "blk"), None)),
        check_vma=False,
    )
```

time: 117 us -> 118 us (level)
  the two profiles are of different devices: /device:TPU:129 before, /device:TPU:257 now
where the time goes in v2:
time: 118 us; the launch traced here: 117 us
  blocking collectives  44.9 us (38%)
  starting transfers between devices  39.4 us (33%)
  waiting for transfers between devices  16.5 us (14%)
  local copies, waits for them, and re-layouts  7.36 us (6%)
  Pallas kernels  7.12 us (6%)
  between operations  1.55 us (1%)
    all_gather x8, blocking collectives, paired(): lax.all_gather(value, 'blk', axis=0, tiled=True, axis_index_groups=pairs)  44.9 us
    ppermute x10, starting transfers between devices, swapped(): return lax.ppermute(value, 'blk', partner)  31.9 us
    ppermute x3, waiting for transfers between devices, shards(): lax.ppermute(sums[0], 'grp', [(g, g + 1) for g in range(groups - 1)])  13.3 us
    ppermute x3, starting transfers between devices, shards(): lax.ppermute(sums[0], 'grp', [(g, g + 1) for g in range(groups - 1)])  7.45 us
    unnamed x18, local copies, waits for them, and re-layouts  7.34 us
    pallas_call x4, Pallas kernels, partial_sums(): pl.pallas_call(functools.partial(partial_kernel, tick, last), out_shape=t...  3.3 us
    ppermute x10, waiting for transfers between devices, swapped(): return lax.ppermute(value, 'blk', partner)  3.17 us
  transfers between devices with their start and end apart: 13, of which 5 were waited for; matrix products, arithmetic and copies ran while one was open for 0% of the time, Pallas kernels for 0%

profile of v2, /device:TPU:257, one launch (start us, length us, event | category | flops | bytes accessed | tf_op | source)
XLA Modules:
  0.0 116.8 jit_solution(9327530294867453136)
XLA Ops:
  1.3 1.0 copy-done
  2.3 0.9 copy-done.3
  4.8 2.2 %all_gather.24 = bf16[512,128]{1,0:T(8,128)(2,1)S(1)} all-gather(bf16[256,128]{1,0:T(8,128)(2,1)S(1)} %get-tuple-element.26), channel_id=1, replica_groups={{0,1},{2,3},{4,5},{6,7},{8,9},{10,11},{12,13},{14,15},{16,17},{18,19},{..., dimensions={0}, use_global_device_ids=true | all-gather | bytes 196608 | tf_op jit(solution)/shard_map/all_gather | solution.py:248
  7.1 1.0 copy-done.1
  9.1 1.9 %copy-done.6 = bf16[1,24,256,256]{3,2,1,0:T(8,128)(2,1)S(1)} copy-done((bf16[1,24,256,256]{3,2,1,0:T(8,128)(2,1)S(1)}, bf16[1,24,256,256]{3,2,1,0:T(8,128)(2,1)}, u32[]{:S(2)}) %copy-start.6) | copy-done | bytes 3145752
  11.6 1.7 %combine.1 = (bf16[5,256,256]{2,1,0:T(8,128)(2,1)S(1)}, bf16[1792,256]{1,0:T(8,128)(2,1)S(1)}) custom-call(s32[1,24]{1,0:T(1,128)S(1)} %copy-done.8, s32[1]{0:T(128)S(6)} %copy.14.count, bf16[1,24,256,256]{3,2,1,0:T(8,128)(2,1)S(1)} %copy-done.6, bf16[256,256]{1,0:T(8,128)(2,1)S(1)} %copy-done.4, f32[4,256,128]{2,1,0:T(8,128)S(1)} %copy-done.1), custom_call_target="tpu_custom_call" | custom-call | flops 4000000 | bytes 10000000 | tf_op jit(solution)/shard_map/combine/pallas_call | solution.py:67
  13.3 1.9 %collective-permute-start = (bf16[1792,256]{1,0:T(8,128)(2,1)S(1)}, bf16[1792,256]{1,0:T(8,128)(2,1)S(1)}, u32[]{:S(2)}, u32[]{:S(2)}) collective-permute-start(bf16[1792,256]{1,0:T(8,128)(2,1)S(1)} %get-tuple-element.33), channel_id=1, source_target_pairs={{0,1},{2,3},{4,5},{6,7},{8,9},{10,11},{12,13},{14,15},{16,17},{18,... | collective-permute-start | bytes 2752520 | tf_op jit(solution)/shard_map/ppermute | solution.py:252
  15.2 4.5 %collective-permute-start.1 = (bf16[512,128]{1,0:T(8,128)(2,1)S(1)}, bf16[512,128]{1,0:T(8,128)(2,1)S(1)}, u32[]{:S(2)}, u32[]{:S(2)}) collective-permute-start(bf16[512,128]{1,0:T(8,128)(2,1)S(1)} %maximum_select_fusion.own), channel_id=1, source_target_pairs={{1,2},{3,4},{5,6},{7,8},{9,10},{11,12},{13,14},{15,16},{17,18},{19... | collective-permute-start | bytes 393224 | tf_op jit(solution)/shard_map/ppermute | solution.py:252
  19.8 5.1 %collective-permute-start.3 = (bf16[256,128]{1,0:T(8,128)(2,1)S(1)}, bf16[256,128]{1,0:T(8,128)(2,1)S(1)}, u32[]{:S(2)}, u32[]{:S(2)}) collective-permute-start(bf16[256,128]{1,0:T(8,128)(2,1)S(1)} %get-tuple-element.26), channel_id=1, source_target_pairs={{0,16},{1,17},{2,18},{3,19},{4,20},{5,21},{6,22},{7,23},{8,24},{9,... | collective-permute-start | bytes 196616 | tf_op jit(solution)/shard_map/ppermute | solution.py:252
  24.9 4.7 %collective-permute-start.2 = (bf16[256,128]{1,0:T(8,128)(2,1)S(1)}, bf16[256,128]{1,0:T(8,128)(2,1)S(1)}, u32[]{:S(2)}, u32[]{:S(2)}) collective-permute-start(bf16[256,128]{1,0:T(8,128)(2,1)S(1)} %get-tuple-element.26), channel_id=1, source_target_pairs={{1,4},{3,6},{5,8},{7,10},{9,12},{11,14},{13,16},{15,18},{17,20},{1... | collective-permute-start | bytes 196616 | tf_op jit(solution)/shard_map/ppermute | solution.py:252
  29.6 2.6 %collective-permute-done.2.third = bf16[256,128]{1,0:T(8,128)(2,1)S(1)} collective-permute-done((bf16[256,128]{1,0:T(8,128)(2,1)S(1)}, bf16[256,128]{1,0:T(8,128)(2,1)S(1)}, u32[]{:S(2)}, u32[]{:S(2)}) %collective-permute-start.2) | collective-permute-done | bytes 65568 | tf_op jit(solution)/shard_map/ppermute | solution.py:252
  33.0 3.6 %collective-permute-start.4 = (bf16[512,128]{1,0:T(8,128)(2,1)S(1)}, bf16[512,128]{1,0:T(8,128)(2,1)S(1)}, u32[]{:S(2)}, u32[]{:S(2)}) collective-permute-start(bf16[512,128]{1,0:T(8,128)(2,1)S(1)} %get-tuple-element.35), channel_id=1, source_target_pairs={{0,32},{32,64},{64,96},{96,128},{128,160},{160,192},{192,224},{224... | collective-permute-start | bytes 393224 | tf_op jit(solution)/shard_map/ppermute | solution.py:275
  36.6 3.3 %collective-permute-done.4 = bf16[512,128]{1,0:T(8,128)(2,1)S(1)} collective-permute-done((bf16[512,128]{1,0:T(8,128)(2,1)S(1)}, bf16[512,128]{1,0:T(8,128)(2,1)S(1)}, u32[]{:S(2)}, u32[]{:S(2)}) %collective-permute-start.4) | collective-permute-done | bytes 131104 | tf_op jit(solution)/shard_map/ppermute | solution.py:275
  39.9 7.8 %all_gather.25.both = bf16[1024,128]{1,0:T(8,128)(2,1)S(1)} all-gather(bf16[512,128]{1,0:T(8,128)(2,1)S(1)} %collective-permute-done.4), channel_id=1, replica_groups={{0,1},{2,3},{4,5},{6,7},{8,9},{10,11},{12,13},{14,15},{16,17},{18,19},{..., dimensions={0}, use_global_device_ids=true | all-gather | bytes 393216 | tf_op jit(solution)/shard_map/all_gather | solution.py:248
  48.0 2.9 %collective-permute-start.6 = (bf16[256,128]{1,0:T(8,128)(2,1)S(1)}, bf16[256,128]{1,0:T(8,128)(2,1)S(1)}, u32[]{:S(2)}, u32[]{:S(2)}) collective-permute-start(bf16[256,128]{1,0:T(8,128)(2,1)S(1)} %slice.19), channel_id=1, source_target_pairs={{0,16},{1,17},{2,18},{3,19},{4,20},{5,21},{6,22},{7,23},{8,24},{9,... | collective-permute-start | bytes 196616 | tf_op jit(solution)/shard_map/ppermute | solution.py:252
  50.9 1.9 %collective-permute-start.5 = (bf16[256,128]{1,0:T(8,128)(2,1)S(1)}, bf16[256,128]{1,0:T(8,128)(2,1)S(1)}, u32[]{:S(2)}, u32[]{:S(2)}) collective-permute-start(bf16[256,128]{1,0:T(8,128)(2,1)S(1)} %slice.19), channel_id=1, source_target_pairs={{1,4},{3,6},{5,8},{7,10},{9,12},{11,14},{13,16},{15,18},{17,20},{1... | collective-permute-start | bytes 196616 | tf_op jit(solution)/shard_map/ppermute | solution.py:252
  52.8 5.1 %all_gather.26.beside = bf16[1024,128]{1,0:T(8,128)(2,1)S(1)} all-gather(bf16[512,128]{1,0:T(8,128)(2,1)S(1)} %get-tuple-element.36.own), channel_id=1, replica_groups={{1,2},{3,4},{5,6},{7,8},{9,10},{11,12},{13,14},{15,16},{17,18},{19,20},..., dimensions={0}, use_global_device_ids=true | all-gather | bytes 393216 | tf_op jit(solution)/shard_map/all_gather | solution.py:248
  58.4 1.0 partial.5
  59.4 1.9 %collective-permute-start.7 = (bf16[512,128]{1,0:T(8,128)(2,1)S(1)}, bf16[512,128]{1,0:T(8,128)(2,1)S(1)}, u32[]{:S(2)}, u32[]{:S(2)}) collective-permute-start(bf16[512,128]{1,0:T(8,128)(2,1)S(1)} %get-tuple-element.39), channel_id=1, source_target_pairs={{0,32},{32,64},{64,96},{96,128},{128,160},{160,192},{192,224},{224... | collective-permute-start | bytes 393224 | tf_op jit(solution)/shard_map/ppermute | solution.py:275
  61.3 5.0 %collective-permute-done.7 = bf16[512,128]{1,0:T(8,128)(2,1)S(1)} collective-permute-done((bf16[512,128]{1,0:T(8,128)(2,1)S(1)}, bf16[512,128]{1,0:T(8,128)(2,1)S(1)}, u32[]{:S(2)}, u32[]{:S(2)}) %collective-permute-start.7) | collective-permute-done | bytes 131104 | tf_op jit(solution)/shard_map/ppermute | solution.py:275
  66.3 7.7 %all_gather.27.both = bf16[1024,128]{1,0:T(8,128)(2,1)S(1)} all-gather(bf16[512,128]{1,0:T(8,128)(2,1)S(1)} %collective-permute-done.7), channel_id=1, replica_groups={{0,1},{2,3},{4,5},{6,7},{8,9},{10,11},{12,13},{14,15},{16,17},{18,19},{..., dimensions={0}, use_global_device_ids=true | all-gather | bytes 393216 | tf_op jit(solution)/shard_map/all_gather | solution.py:248
  74.3 1.9 %collective-permute-start.9 = (bf16[256,128]{1,0:T(8,128)(2,1)S(1)}, bf16[256,128]{1,0:T(8,128)(2,1)S(1)}, u32[]{:S(2)}, u32[]{:S(2)}) collective-permute-start(bf16[256,128]{1,0:T(8,128)(2,1)S(1)} %slice.20), channel_id=1, source_target_pairs={{0,16},{1,17},{2,18},{3,19},{4,20},{5,21},{6,22},{7,23},{8,24},{9,... | collective-permute-start | bytes 196616 | tf_op jit(solution)/shard_map/ppermute | solution.py:252
  76.2 2.9 %collective-permute-start.8 = (bf16[256,128]{1,0:T(8,128)(2,1)S(1)}, bf16[256,128]{1,0:T(8,128)(2,1)S(1)}, u32[]{:S(2)}, u32[]{:S(2)}) collective-permute-start(bf16[256,128]{1,0:T(8,128)(2,1)S(1)} %slice.20), channel_id=1, source_target_pairs={{1,4},{3,6},{5,8},{7,10},{9,12},{11,14},{13,16},{15,18},{17,20},{1... | collective-permute-start | bytes 196616 | tf_op jit(solution)/shard_map/ppermute | solution.py:252
  79.1 5.4 %all_gather.28.beside = bf16[1024,128]{1,0:T(8,128)(2,1)S(1)} all-gather(bf16[512,128]{1,0:T(8,128)(2,1)S(1)} %get-tuple-element.40.own), channel_id=1, replica_groups={{1,2},{3,4},{5,6},{7,8},{9,10},{11,12},{13,14},{15,16},{17,18},{19,20},..., dimensions={0}, use_global_device_ids=true | all-gather | bytes 393216 | tf_op jit(solution)/shard_map/all_gather | solution.py:248
  84.5 1.0 partial.6
  85.4 1.9 %collective-permute-start.10 = (bf16[512,128]{1,0:T(8,128)(2,1)S(1)}, bf16[512,128]{1,0:T(8,128)(2,1)S(1)}, u32[]{:S(2)}, u32[]{:S(2)}) collective-permute-start(bf16[512,128]{1,0:T(8,128)(2,1)S(1)} %get-tuple-element.43), channel_id=1, source_target_pairs={{0,32},{32,64},{64,96},{96,128},{128,160},{160,192},{192,224},{224... | collective-permute-start | bytes 393224 | tf_op jit(solution)/shard_map/ppermute | solution.py:275
  87.4 5.0 %collective-permute-done.10 = bf16[512,128]{1,0:T(8,128)(2,1)S(1)} collective-permute-done((bf16[512,128]{1,0:T(8,128)(2,1)S(1)}, bf16[512,128]{1,0:T(8,128)(2,1)S(1)}, u32[]{:S(2)}, u32[]{:S(2)}) %collective-permute-start.10) | collective-permute-done | bytes 131104 | tf_op jit(solution)/shard_map/ppermute | solution.py:275
  92.4 6.1 %all_gather.29.both = bf16[1024,128]{1,0:T(8,128)(2,1)S(1)} all-gather(bf16[512,128]{1,0:T(8,128)(2,1)S(1)} %collective-permute-done.10), channel_id=1, replica_groups={{0,1},{2,3},{4,5},{6,7},{8,9},{10,11},{12,13},{14,15},{16,17},{18,19},{..., dimensions={0}, use_global_device_ids=true | all-gather | bytes 393216 | tf_op jit(solution)/shard_map/all_gather | solution.py:248
  98.8 3.3 %collective-permute-start.12 = (bf16[256,128]{1,0:T(8,128)(2,1)S(1)}, bf16[256,128]{1,0:T(8,128)(2,1)S(1)}, u32[]{:S(2)}, u32[]{:S(2)}) collective-permute-start(bf16[256,128]{1,0:T(8,128)(2,1)S(1)} %slice.21), channel_id=1, source_target_pairs={{0,16},{1,17},{2,18},{3,19},{4,20},{5,21},{6,22},{7,23},{8,24},{9,... | collective-permute-start | bytes 196616 | tf_op jit(solution)/shard_map/ppermute | solution.py:252
  102.1 2.8 %collective-permute-start.11 = (bf16[256,128]{1,0:T(8,128)(2,1)S(1)}, bf16[256,128]{1,0:T(8,128)(2,1)S(1)}, u32[]{:S(2)}, u32[]{:S(2)}) collective-permute-start(bf16[256,128]{1,0:T(8,128)(2,1)S(1)} %slice.21), channel_id=1, source_target_pairs={{1,4},{3,6},{5,8},{7,10},{9,12},{11,14},{13,16},{15,18},{17,20},{1... | collective-permute-start | bytes 196616 | tf_op jit(solution)/shard_map/ppermute | solution.py:252
  104.8 5.4 %all_gather.30.beside = bf16[1024,128]{1,0:T(8,128)(2,1)S(1)} all-gather(bf16[512,128]{1,0:T(8,128)(2,1)S(1)} %get-tuple-element.44.own), channel_id=1, replica_groups={{1,2},{3,4},{5,6},{7,8},{9,10},{11,12},{13,14},{15,16},{17,18},{19,20},..., dimensions={0}, use_global_device_ids=true | all-gather | bytes 393216 | tf_op jit(solution)/shard_map/all_gather | solution.py:248
  110.9 5.3 %all_gather.31.both = bf16[512,128]{1,0:T(8,128)(2,1)S(1)} all-gather(bf16[256,128]{1,0:T(8,128)(2,1)S(1)} %get-tuple-element.49), channel_id=1, replica_groups={{0,1},{2,3},{4,5},{6,7},{8,9},{10,11},{12,13},{14,15},{16,17},{18,19},{..., dimensions={0}, use_global_device_ids=true | all-gather | bytes 196608 | tf_op jit(solution)/shard_map/all_gather | solution.py:248
  (36 shorter events, 6.6 us)
Async XLA Ops:
  1.3 1.0 copy-start
  2.3 0.9 copy-start.3
  3.2 0.9 copy-start.7
  7.1 1.0 copy-start.1
  8.2 0.9 copy-start.4
  9.1 1.9 %copy-start.6 = (bf16[1,24,256,256]{3,2,1,0:T(8,128)(2,1)S(1)}, bf16[1,24,256,256]{3,2,1,0:T(8,128)(2,1)}, u32[]{:S(2)}) copy-start(bf16[1,24,256,256]{3,2,1,0:T(8,128)(2,1)} %blocks) | copy-start | bytes 9437188
  11.0 0.7 copy-start.8
  11.6 36.1 %copy-start.2 = (f32[4,256,128]{2,1,0:T(8,128)S(1)}, f32[4,256,128]{2,1,0:T(8,128)}, u32[]{:S(2)}) copy-start(f32[4,256,128]{2,1,0:T(8,128)} %right.8) | copy-start | bytes 1572868
  11.6 36.1 %copy-start.5 = (bf16[256,256]{1,0:T(8,128)(2,1)S(1)}, bf16[256,256]{1,0:T(8,128)(2,1)}, u32[]{:S(2)}) copy-start(bf16[256,256]{1,0:T(8,128)(2,1)} %inverse.8) | copy-start | bytes 393220
  13.3 19.0 %collective-permute-start = (bf16[1792,256]{1,0:T(8,128)(2,1)S(1)}, bf16[1792,256]{1,0:T(8,128)(2,1)S(1)}, u32[]{:S(2)}, u32[]{:S(2)}) collective-permute-start(bf16[1792,256]{1,0:T(8,128)(2,1)S(1)} %get-tuple-element.33), channel_id=1, source_target_pairs={{0,1},{2,3},{4,5},{6,7},{8,9},{10,11},{12,13},{14,15},{16,17},{18,... | collective-permute-start | bytes 2752520 | tf_op jit(solution)/shard_map/ppermute | solution.py:252
  15.2 14.4 %collective-permute-start.1 = (bf16[512,128]{1,0:T(8,128)(2,1)S(1)}, bf16[512,128]{1,0:T(8,128)(2,1)S(1)}, u32[]{:S(2)}, u32[]{:S(2)}) collective-permute-start(bf16[512,128]{1,0:T(8,128)(2,1)S(1)} %maximum_select_fusion.own), channel_id=1, source_target_pairs={{1,2},{3,4},{5,6},{7,8},{9,10},{11,12},{13,14},{15,16},{17,18},{19... | collective-permute-start | bytes 393224 | tf_op jit(solution)/shard_map/ppermute | solution.py:252
  19.8 9.8 %collective-permute-start.3 = (bf16[256,128]{1,0:T(8,128)(2,1)S(1)}, bf16[256,128]{1,0:T(8,128)(2,1)S(1)}, u32[]{:S(2)}, u32[]{:S(2)}) collective-permute-start(bf16[256,128]{1,0:T(8,128)(2,1)S(1)} %get-tuple-element.26), channel_id=1, source_target_pairs={{0,16},{1,17},{2,18},{3,19},{4,20},{5,21},{6,22},{7,23},{8,24},{9,... | collective-permute-start | bytes 196616 | tf_op jit(solution)/shard_map/ppermute | solution.py:252
  24.9 7.4 %collective-permute-start.2 = (bf16[256,128]{1,0:T(8,128)(2,1)S(1)}, bf16[256,128]{1,0:T(8,128)(2,1)S(1)}, u32[]{:S(2)}, u32[]{:S(2)}) collective-permute-start(bf16[256,128]{1,0:T(8,128)(2,1)S(1)} %get-tuple-element.26), channel_id=1, source_target_pairs={{1,4},{3,6},{5,8},{7,10},{9,12},{11,14},{13,16},{15,18},{17,20},{1... | collective-permute-start | bytes 196616 | tf_op jit(solution)/shard_map/ppermute | solution.py:252
  33.0 6.9 %collective-permute-start.4 = (bf16[512,128]{1,0:T(8,128)(2,1)S(1)}, bf16[512,128]{1,0:T(8,128)(2,1)S(1)}, u32[]{:S(2)}, u32[]{:S(2)}) collective-permute-start(bf16[512,128]{1,0:T(8,128)(2,1)S(1)} %get-tuple-element.35), channel_id=1, source_target_pairs={{0,32},{32,64},{64,96},{96,128},{128,160},{160,192},{192,224},{224... | collective-permute-start | bytes 393224 | tf_op jit(solution)/shard_map/ppermute | solution.py:275
  48.0 9.9 %collective-permute-start.6 = (bf16[256,128]{1,0:T(8,128)(2,1)S(1)}, bf16[256,128]{1,0:T(8,128)(2,1)S(1)}, u32[]{:S(2)}, u32[]{:S(2)}) collective-permute-start(bf16[256,128]{1,0:T(8,128)(2,1)S(1)} %slice.19), channel_id=1, source_target_pairs={{0,16},{1,17},{2,18},{3,19},{4,20},{5,21},{6,22},{7,23},{8,24},{9,... | collective-permute-start | bytes 196616 | tf_op jit(solution)/shard_map/ppermute | solution.py:252
  50.9 7.5 %collective-permute-start.5 = (bf16[256,128]{1,0:T(8,128)(2,1)S(1)}, bf16[256,128]{1,0:T(8,128)(2,1)S(1)}, u32[]{:S(2)}, u32[]{:S(2)}) collective-permute-start(bf16[256,128]{1,0:T(8,128)(2,1)S(1)} %slice.19), channel_id=1, source_target_pairs={{1,4},{3,6},{5,8},{7,10},{9,12},{11,14},{13,16},{15,18},{17,20},{1... | collective-permute-start | bytes 196616 | tf_op jit(solution)/shard_map/ppermute | solution.py:252
  59.4 6.9 %collective-permute-start.7 = (bf16[512,128]{1,0:T(8,128)(2,1)S(1)}, bf16[512,128]{1,0:T(8,128)(2,1)S(1)}, u32[]{:S(2)}, u32[]{:S(2)}) collective-permute-start(bf16[512,128]{1,0:T(8,128)(2,1)S(1)} %get-tuple-element.39), channel_id=1, source_target_pairs={{0,32},{32,64},{64,96},{96,128},{128,160},{160,192},{192,224},{224... | collective-permute-start | bytes 393224 | tf_op jit(solution)/shard_map/ppermute | solution.py:275
  74.3 10.2 %collective-permute-start.9 = (bf16[256,128]{1,0:T(8,128)(2,1)S(1)}, bf16[256,128]{1,0:T(8,128)(2,1)S(1)}, u32[]{:S(2)}, u32[]{:S(2)}) collective-permute-start(bf16[256,128]{1,0:T(8,128)(2,1)S(1)} %slice.20), channel_id=1, source_target_pairs={{0,16},{1,17},{2,18},{3,19},{4,20},{5,21},{6,22},{7,23},{8,24},{9,... | collective-permute-start | bytes 196616 | tf_op jit(solution)/shard_map/ppermute | solution.py:252
  76.2 8.3 %collective-permute-start.8 = (bf16[256,128]{1,0:T(8,128)(2,1)S(1)}, bf16[256,128]{1,0:T(8,128)(2,1)S(1)}, u32[]{:S(2)}, u32[]{:S(2)}) collective-permute-start(bf16[256,128]{1,0:T(8,128)(2,1)S(1)} %slice.20), channel_id=1, source_target_pairs={{1,4},{3,6},{5,8},{7,10},{9,12},{11,14},{13,16},{15,18},{17,20},{1... | collective-permute-start | bytes 196616 | tf_op jit(solution)/shard_map/ppermute | solution.py:252
  85.4 6.9 %collective-permute-start.10 = (bf16[512,128]{1,0:T(8,128)(2,1)S(1)}, bf16[512,128]{1,0:T(8,128)(2,1)S(1)}, u32[]{:S(2)}, u32[]{:S(2)}) collective-permute-start(bf16[512,128]{1,0:T(8,128)(2,1)S(1)} %get-tuple-element.43), channel_id=1, source_target_pairs={{0,32},{32,64},{64,96},{96,128},{128,160},{160,192},{192,224},{224... | collective-permute-start | bytes 393224 | tf_op jit(solution)/shard_map/ppermute | solution.py:275
  98.8 11.4 %collective-permute-start.12 = (bf16[256,128]{1,0:T(8,128)(2,1)S(1)}, bf16[256,128]{1,0:T(8,128)(2,1)S(1)}, u32[]{:S(2)}, u32[]{:S(2)}) collective-permute-start(bf16[256,128]{1,0:T(8,128)(2,1)S(1)} %slice.21), channel_id=1, source_target_pairs={{0,16},{1,17},{2,18},{3,19},{4,20},{5,21},{6,22},{7,23},{8,24},{9,... | collective-permute-start | bytes 196616 | tf_op jit(solution)/shard_map/ppermute | solution.py:252
  102.1 8.1 %collective-permute-start.11 = (bf16[256,128]{1,0:T(8,128)(2,1)S(1)}, bf16[256,128]{1,0:T(8,128)(2,1)S(1)}, u32[]{:S(2)}, u32[]{:S(2)}) collective-permute-start(bf16[256,128]{1,0:T(8,128)(2,1)S(1)} %slice.21), channel_id=1, source_target_pairs={{1,4},{3,6},{5,8},{7,10},{9,12},{11,14},{13,16},{15,18},{17,20},{1... | collective-permute-start | bytes 196616 | tf_op jit(solution)/shard_map/ppermute | solution.py:252

commit v3 on v2

v3 whole, which is shorter than its diff:
```python
import functools

import jax
import jax.numpy as jnp
from jax import lax
from jax.experimental import pallas as pl
from jax.experimental.pallas import tpu as pltpu
from jax.sharding import PartitionSpec as P

F32 = jnp.float32
BF16 = jnp.bfloat16
VMEM = pl.BlockSpec(memory_space=pltpu.VMEM)
HBM = pl.BlockSpec(memory_space=pltpu.HBM)
LIMIT = 20 * 1024 * 1024


def params():
    return pltpu.CompilerParams(vmem_limit_bytes=LIMIT)


def mm(a, b):
    return jnp.dot(a, b, preferred_element_type=F32)


def combine_kernel(around, listed, blocks, inverse, right, kept, handed, listed_here, landing, sums, arrived, small):
    block = inverse.shape[0]
    copy = pltpu.make_async_copy(listed, listed_here, small)
    copy.start()
    own = lax.axis_index("blk")
    sign = 2 * lax.rem(own, 2) - 1

    def copy_of(k):
        return pltpu.make_async_copy(blocks.at[0, k], landing.at[k], arrived.at[k])

    copy.wait()
    live = listed_here[0, blocks.shape[1]]

    def begin(k, carry):
        copy_of(k).start()
        return carry

    lax.fori_loop(0, live, begin, 0)
    sums[...] = jnp.zeros_like(sums)
    handed[4 * block : 5 * block, :] = inverse[...]
    for tick in range(right.shape[0]):
        value = right[tick]
        high = value.astype(BF16)
        rows = pl.ds((5 + tick) * block, block)
        handed[rows, 0 : value.shape[1]] = high
        handed[rows, value.shape[1] :] = (value - high.astype(F32)).astype(BF16)

    def add(k, carry):
        copy_of(k).wait()
        offset = lax.rem(listed_here[0, k] - own + 3 + around, around) - 3
        turned = offset * sign
        slot = jnp.where(k == 0, 4, jnp.where(turned >= 0, 3 - turned, 8 + turned))
        sums[slot] = sums[slot] + landing[k].astype(F32)
        return carry

    lax.fori_loop(0, live, add, 0)
    for i in range(5):
        kept[i] = sums[i].astype(BF16)
    for i in range(3):
        handed[i * block : (i + 1) * block, :] = sums[5 + i].astype(BF16)
    handed[3 * block : 4 * block, :] = sums[4].astype(BF16)


def in_hbm(value):
    return pltpu.with_memory_space_constraint(value, pltpu.HBM)


def combine(around, sources, counts, factor_blocks, inverse, right):
    slots, block = factor_blocks.shape[1], factor_blocks.shape[2]
    ticks = right.shape[0]
    listed = jnp.concatenate([sources, counts[:, None]], 1)
    return pl.pallas_call(
        functools.partial(combine_kernel, around),
        out_shape=(
            jax.ShapeDtypeStruct((5, block, block), BF16),
            jax.ShapeDtypeStruct(((5 + ticks) * block, block), BF16),
        ),
        in_specs=[HBM, HBM, VMEM, VMEM],
        out_specs=(VMEM, VMEM),
        scratch_shapes=[
            pltpu.SMEM(listed.shape, jnp.int32),
            pltpu.VMEM((slots, block, block), BF16),
            pltpu.VMEM((8, block, block), F32),
            pltpu.SemaphoreType.DMA((slots,)),
            pltpu.SemaphoreType.DMA,
        ],
        compiler_params=params(),
        cost_estimate=pl.CostEstimate(flops=4_000_000, bytes_accessed=10_000_000, transcendentals=0),
        name="combine",
    )(in_hbm(listed), in_hbm(factor_blocks), inverse, right)


def first_kernel(right, incoming, inverse, solved, outgoing, inverse_here, later_here, right_here, incoming_here, arrived):
    copies = (
        pltpu.make_async_copy(right.at[0], right_here, arrived.at[0]),
        pltpu.make_async_copy(incoming, incoming_here, arrived.at[1]),
        pltpu.make_async_copy(inverse, inverse_here, arrived.at[2]),
        pltpu.make_async_copy(right.at[pl.ds(1, later_here.shape[0])], later_here, arrived.at[3]),
    )
    for copy in copies:
        copy.start()
    for copy in copies[:3]:
        copy.wait()
    value = mm(inverse_here[...], (right_here[...] - incoming_here[...]).astype(BF16))
    solved[...] = value
    outgoing[...] = value.astype(BF16)
    copies[3].wait()


def first_solve(right_side, carry_in, inverse_diag):
    ticks, block, columns = right_side.shape
    return pl.pallas_call(
        first_kernel,
        out_shape=(
            jax.ShapeDtypeStruct((block, columns), F32),
            jax.ShapeDtypeStruct((block, columns), BF16),
            jax.ShapeDtypeStruct((block, block), BF16),
            jax.ShapeDtypeStruct((ticks - 1, block, columns), F32),
        ),
        in_specs=[HBM, HBM, HBM],
        out_specs=(VMEM, VMEM, VMEM, VMEM),
        scratch_shapes=[
            pltpu.VMEM((block, columns), F32),
            pltpu.VMEM((block, columns), F32),
            pltpu.SemaphoreType.DMA((4,)),
        ],
        compiler_params=params(),
        name="first",
    )(in_hbm(right_side), in_hbm(carry_in), in_hbm(inverse_diag))


def pair_kernel(tick, both, right, inverse, given, *refs):
    far = refs[:-2]
    solved, outgoing = refs[-2:]
    block, columns = solved.shape
    odd = lax.rem(lax.axis_index("blk"), 2)
    mine = odd * (2 * block)
    theirs = (1 - odd) * (2 * block)

    def part(at):
        return both[pl.ds(pl.multiple_of(at, block), block), :].astype(F32)

    incoming = part(mine) + part(theirs + block)
    other = part(mine + block) + part(theirs)
    for ref in far:
        incoming += ref[0:block].astype(F32)
        other += ref[block:].astype(F32)
    value = mm(inverse[...], (right[tick - 1] - incoming).astype(BF16))
    solved[...] = value
    outgoing[0:block] = value.astype(BF16)
    rows = pl.ds((4 + tick) * block, block)
    other_right = given[rows, 0:columns].astype(F32) + given[rows, columns:].astype(F32)
    value = mm(given[4 * block : 5 * block, :], (other_right - other).astype(BF16))
    outgoing[block:] = value.astype(BF16)


def pair_solve(tick, both, right, inverse, given, far):
    block, columns = right.shape[1:]
    operands = [both, right, inverse, given] + ([] if far is None else [far])
    return pl.pallas_call(
        functools.partial(pair_kernel, tick),
        out_shape=(
            jax.ShapeDtypeStruct((block, columns), F32),
            jax.ShapeDtypeStruct((2 * block, columns), BF16),
        ),
        in_specs=[VMEM] * len(operands),
        out_specs=(VMEM, VMEM),
        compiler_params=params(),
        name="solve",
    )(*operands)


def products(kept, given, own, beside, third, opposite):
    block = third.shape[0]
    near = lax.rem(lax.axis_index("blk"), 2) * (2 * block)

    def part(at):
        return beside[pl.ds(pl.multiple_of(at, block), block), :]

    odd_one, same_one = part(near), part(near + block)
    self_one = own[0:block]
    value = mm(kept[3], self_one)
    value += mm(kept[1], same_one)
    value += mm(kept[2], odd_one)
    value += mm(kept[0], third[...])
    if opposite is not None:
        value += mm(kept[4], opposite[...])
    other = mm(given[0:block, :], same_one)
    other += mm(given[block : 2 * block, :], odd_one)
    other += mm(given[2 * block : 3 * block, :], self_one)
    return value, other


def partial_kernel(kept, given, own, beside, third, opposite, sums):
    block = third.shape[0]
    value, other = products(kept, given, own, beside, third, opposite)
    sums[0:block] = value.astype(BF16)
    sums[block:] = other.astype(BF16)


def far_kernel(kept, given, own, beside, third, far_sums, sums, leaving):
    block = third.shape[0]
    value, other = products(kept, given, own, beside, third, None)
    sums[0:block] = value.astype(BF16)
    sums[block:] = other.astype(BF16)
    leaving[0:block] = mm(far_sums[0:block, :], own[0:block]).astype(BF16)
    leaving[block:] = mm(far_sums[block:, :], own[block:]).astype(BF16)


def last_kernel(ticks, kept, given, own, beside, third, opposite, *refs):
    solved = refs[:ticks]
    exact, sums, outputs, left = refs[ticks:]
    copies = [pltpu.make_async_copy(solved[t], outputs.at[t], left.at[t]) for t in range(ticks)]
    for copy in copies:
        copy.start()
    value, other = products(kept, given, own, beside, third, opposite)
    exact[...] = value
    sums[...] = other.astype(BF16)
    for copy in copies:
        copy.wait()


def partial_sums(kernel, operands, pairs_out):
    block, columns = operands[4].shape
    return pl.pallas_call(
        kernel,
        out_shape=(jax.ShapeDtypeStruct((2 * block, columns), BF16),) * pairs_out,
        in_specs=[VMEM] * len(operands),
        out_specs=(VMEM,) * pairs_out,
        compiler_params=params(),
        name="partial",
    )(*operands)


def last_sums(operands, solved):
    block, columns = operands[4].shape
    ticks = len(solved)
    return pl.pallas_call(
        functools.partial(last_kernel, ticks),
        out_shape=(
            jax.ShapeDtypeStruct((block, columns), F32),
            jax.ShapeDtypeStruct((block, columns), BF16),
            jax.ShapeDtypeStruct((ticks, block, columns), F32),
        ),
        in_specs=[VMEM] * (len(operands) + ticks),
        out_specs=(VMEM, VMEM, HBM),
        scratch_shapes=[pltpu.SemaphoreType.DMA((ticks,))],
        compiler_params=params(),
        name="last",
    )(*operands, *solved)


def carry_kernel(exact, both, carry):
    block = exact.shape[0]
    odd = lax.rem(lax.axis_index("blk"), 2)
    theirs = pl.multiple_of((1 - odd) * block, block)
    carry[...] = exact[...] + both[pl.ds(theirs, block), :].astype(F32)


def carry_sum(exact, both):
    return pl.pallas_call(
        carry_kernel,
        out_shape=jax.ShapeDtypeStruct(exact.shape, F32),
        in_specs=[VMEM, VMEM],
        out_specs=VMEM,
        compiler_params=params(),
        name="carry",
    )(exact, both)


def shards(right_side, inverse_diag, factor_blocks, sources, counts, carry_in):
    ticks, block = right_side.shape[0], right_side.shape[1]
    groups, around = lax.axis_size("grp"), lax.axis_size("blk")
    chips = around // 2
    at = lax.axis_index("blk").astype(jnp.int32)
    odd = lax.rem(at, 2)
    chip_pairs = [[2 * c, 2 * c + 1] for c in range(chips)]
    next_pairs = [[2 * c + 1, (2 * c + 2) % around] for c in range(chips)]
    third_pairs = [[2 * c + 1, (2 * c + 4) % around] for c in range(chips)]
    opposite_pairs = [[b, b + chips] for b in range(chips)]

    def paired(value, pairs):
        return lax.all_gather(value, "blk", axis=0, tiled=True, axis_index_groups=pairs)

    def swapped(value, pairs):
        partner = [(a, b) for a, b in pairs] + [(b, a) for a, b in pairs]
        return lax.ppermute(value, "blk", partner)

    solved, own, inverse, right = first_solve(right_side, carry_in, inverse_diag)
    finished = [solved]
    far_sums = None
    forward = [(g * around + (b + chips) % around, (g + 1) * around + b) for g in range(groups - 1) for b in range(around)]
    for tick in range(ticks):
        last = tick + 1 == ticks
        near_form = tick == 0 or last
        mine = own[0:block]
        third = swapped(mine, third_pairs)
        opposite = swapped(mine, opposite_pairs) if near_form else None
        if tick == 0:
            chip = paired(own, chip_pairs)
            own = jnp.where(odd == 0, chip, jnp.roll(chip, block, 0))
            near = swapped(own, next_pairs)
            held = (own, third, opposite, sources, counts, factor_blocks, inverse, right)
            own, third, opposite, *held = lax.optimization_barrier(held)
            kept, handed = combine(around, *held)
            near, handed = lax.optimization_barrier((near, handed))
            given = swapped(handed, chip_pairs)
            beside = jnp.concatenate([near, near], 0)
        else:
            beside = paired(own, next_pairs)
        operands = [kept, given, own, beside, third]
        if last:
            exact, crossing, outputs = last_sums(operands + [opposite], finished)
            carry = carry_sum(exact, paired(crossing, chip_pairs))
            return (outputs, carry)
        far = None
        if near_form:
            (sums,) = partial_sums(partial_kernel, operands + [opposite], 1)
            own_far, pair_far = lax.optimization_barrier((sums, kept[4], given[3 * block : 4 * block]))[1:]
            far_sums = swapped(jnp.concatenate([own_far, pair_far], 0), opposite_pairs)
        else:
            sums, leaving = partial_sums(far_kernel, operands + [far_sums], 2)
            far = lax.ppermute(leaving, ("grp", "blk"), forward)
        moved = lax.ppermute(sums, "grp", [(g, g + 1) for g in range(groups - 1)])
        both = paired(moved, chip_pairs)
        solved, own = pair_solve(tick + 1, both, right, inverse, given, far)
        finished.append(solved)


def solution(mesh):
    placed = (
        P(None, ("grp", "blk"), None),
        P(("grp", "blk"), None),
        P(("grp", "blk"), None, None, None),
        P(("grp", "blk"), None),
        P(("grp", "blk")),
        P(("grp", "blk"), None),
    )
    return jax.shard_map(
        shards,
        mesh=mesh,
        in_specs=placed,
        out_specs=(P(None, ("grp", "blk"), None), P(("grp", "blk"), None)),
        check_vma=False,
    )
```

time: 118 us -> 107 us (0.907)
  the two profiles are of different devices: /device:TPU:257 before, /device:TPU:97 now
where the time goes in v3:
time: 107 us
  starting transfers between devices  55.4 us (52%)
  blocking collectives  38.2 us (36%)
  Pallas kernels  7.38 us (7%)
  waiting for transfers between devices  2.74 us (3%)
  between operations  1.58 us (1%)
  other arithmetic  1.32 us (1%)
    all_gather x8, blocking collectives, paired(): lax.all_gather(value, 'blk', axis=0, tiled=True, axis_index_groups=pairs)  38.2 us
    ppermute x9, starting transfers between devices, swapped(): return lax.ppermute(value, 'blk', partner)  35.1 us
    ppermute x3, starting transfers between devices, shards(): moved = lax.ppermute(sums, 'grp', [(g, g + 1) for g in range(groups - 1)])  14.7 us
    ppermute x2, starting transfers between devices, shards(): far = lax.ppermute(leaving, ('grp', 'blk'), forward)  5.57 us
    pallas_call x1, Pallas kernels, combine(): pl.pallas_call(functools.partial(combine_kernel, around), out_shape=(jax....  2.31 us
    ppermute x9, waiting for transfers between devices, swapped(): return lax.ppermute(value, 'blk', partner)  2.24 us
  transfers between devices with their start and end apart: 14, of which 2 were waited for; matrix products, arithmetic and copies ran while one was open for 1% of the time, Pallas kernels for 2%

profile of v3, /device:TPU:97, one launch (start us, length us, event | category | flops | bytes accessed | tf_op | source)
XLA Modules:
  0.0 106.7 jit_solution(14592560707263046806)
XLA Ops:
  0.6 1.2 %first.1 = (f32[256,128]{1,0:T(8,128)S(1)}, bf16[256,128]{1,0:T(8,128)(2,1)S(1)}, bf16[256,256]{1,0:T(8,128)(2,1)S(1)}, f32[3,256,128]{2,1,0:T(8,128)S(1)}) custom-call(f32[4,256,128]{2,1,0:T(8,128)} %right.1, f32[256,128]{1,0:T(8,128)} %incoming.1, bf16[256,256]{1,0:T(8,128)(2,1)} %inverse.1), custom_call_target="tpu_custom_call" | custom-call | tf_op jit(solution)/shard_map/first/pallas_call | solution.py:116
  1.9 5.2 %collective-permute-start = (bf16[256,128]{1,0:T(8,128)(2,1)S(1)}, bf16[256,128]{1,0:T(8,128)(2,1)S(1)}, u32[]{:S(2)}, u32[]{:S(2)}) collective-permute-start(bf16[256,128]{1,0:T(8,128)(2,1)S(1)} %get-tuple-element.33), channel_id=1, source_target_pairs={{1,4},{3,6},{5,8},{7,10},{9,12},{11,14},{13,16},{15,18},{17,20},{1... | collective-permute-start | bytes 196616 | tf_op jit(solution)/shard_map/ppermute | solution.py:291
  7.1 4.8 %collective-permute-start.1 = (bf16[256,128]{1,0:T(8,128)(2,1)S(1)}, bf16[256,128]{1,0:T(8,128)(2,1)S(1)}, u32[]{:S(2)}, u32[]{:S(2)}) collective-permute-start(bf16[256,128]{1,0:T(8,128)(2,1)S(1)} %get-tuple-element.33), channel_id=1, source_target_pairs={{0,16},{1,17},{2,18},{3,19},{4,20},{5,21},{6,22},{7,23},{8,24},{9,... | collective-permute-start | bytes 196616 | tf_op jit(solution)/shard_map/ppermute | solution.py:291
  11.9 1.9 %all_gather.24 = bf16[512,128]{1,0:T(8,128)(2,1)S(1)} all-gather(bf16[256,128]{1,0:T(8,128)(2,1)S(1)} %get-tuple-element.33), channel_id=1, replica_groups={{0,1},{2,3},{4,5},{6,7},{8,9},{10,11},{12,13},{14,15},{16,17},{18,19},{..., dimensions={0}, use_global_device_ids=true | all-gather | bytes 196608 | tf_op jit(solution)/shard_map/all_gather | solution.py:287
  13.9 2.3 %collective-permute-start.2 = (bf16[512,128]{1,0:T(8,128)(2,1)S(1)}, bf16[512,128]{1,0:T(8,128)(2,1)S(1)}, u32[]{:S(2)}, u32[]{:S(2)}) collective-permute-start(bf16[512,128]{1,0:T(8,128)(2,1)S(1)} %maximum_select_fusion.own), channel_id=1, source_target_pairs={{1,2},{3,4},{5,6},{7,8},{9,10},{11,12},{13,14},{15,16},{17,18},{19... | collective-permute-start | bytes 393224 | tf_op jit(solution)/shard_map/ppermute | solution.py:291
  16.8 1.2 %pad_add_fusion.listed = s32[1,25]{1,0:T(1,128)} fusion(s32[1,1]{1,0:T(1,128)} %bitcast.3, s32[1,24]{1,0:T(1,128)} %param.9), kind=kLoop, calls=%fused_computation.4 | loop fusion | flops 25 | bytes 200 | tf_op jit(solution)/shard_map/concatenate | solution.py:75
  18.1 2.3 %combine.1 = (bf16[5,256,256]{2,1,0:T(8,128)(2,1)S(1)}, bf16[2048,256]{1,0:T(8,128)(2,1)S(1)}) custom-call(s32[1,25]{1,0:T(1,128)} %pad_add_fusion.listed, bf16[1,24,256,256]{3,2,1,0:T(8,128)(2,1)} %blocks, bf16[256,256]{1,0:T(8,128)(2,1)S(1)} %get-tuple-element.39.inverse, f32[3,256,128]{2,1,0:T(8,128)S(1)} %get-tuple-element.40.right), custom_call_target="tpu_custom_call" | custom-call | flops 4000000 | bytes 10000000 | tf_op jit(solution)/shard_map/combine/pallas_call | solution.py:76
  20.4 5.2 %collective-permute-start.3 = (bf16[2048,256]{1,0:T(8,128)(2,1)S(1)}, bf16[2048,256]{1,0:T(8,128)(2,1)S(1)}, u32[]{:S(2)}, u32[]{:S(2)}) collective-permute-start(bf16[2048,256]{1,0:T(8,128)(2,1)S(1)} %get-tuple-element.43), channel_id=1, source_target_pairs={{0,1},{2,3},{4,5},{6,7},{8,9},{10,11},{12,13},{14,15},{16,17},{18,... | collective-permute-start | bytes 3145736 | tf_op jit(solution)/shard_map/ppermute | solution.py:291
  25.6 2.2 %collective-permute-done.3.given = bf16[2048,256]{1,0:T(8,128)(2,1)S(1)} collective-permute-done((bf16[2048,256]{1,0:T(8,128)(2,1)S(1)}, bf16[2048,256]{1,0:T(8,128)(2,1)S(1)}, u32[]{:S(2)}, u32[]{:S(2)}) %collective-permute-start.3) | collective-permute-done | bytes 1048608 | tf_op jit(solution)/shard_map/ppermute | solution.py:291
  27.8 0.4 partial.3
  28.3 4.8 %collective-permute-start.4 = (bf16[512,128]{1,0:T(8,128)(2,1)S(1)}, bf16[512,128]{1,0:T(8,128)(2,1)S(1)}, u32[]{:S(2)}, u32[]{:S(2)}) collective-permute-start(bf16[512,128]{1,0:T(8,128)(2,1)S(1)} %partial.3), channel_id=1, source_target_pairs={{0,32},{32,64},{64,96},{96,128},{128,160},{160,192},{192,224},{224... | collective-permute-start | bytes 393224 | tf_op jit(solution)/shard_map/ppermute | solution.py:328
  33.1 3.2 %collective-permute-start.6 = (bf16[512,256]{1,0:T(8,128)(2,1)S(1)}, bf16[512,256]{1,0:T(8,128)(2,1)S(1)}, u32[]{:S(2)}, u32[]{:S(2)}) collective-permute-start(bf16[512,256]{1,0:T(8,128)(2,1)S(1)} %pad_maximum_fusion.1), channel_id=1, source_target_pairs={{0,16},{1,17},{2,18},{3,19},{4,20},{5,21},{6,22},{7,23},{8,24},{9,... | collective-permute-start | bytes 786440 | tf_op jit(solution)/shard_map/ppermute | solution.py:291
  36.3 2.6 %all_gather.25.both = bf16[1024,128]{1,0:T(8,128)(2,1)S(1)} all-gather(bf16[512,128]{1,0:T(8,128)(2,1)S(1)} %collective-permute-done.4), channel_id=1, replica_groups={{0,1},{2,3},{4,5},{6,7},{8,9},{10,11},{12,13},{14,15},{16,17},{18,19},{..., dimensions={0}, use_global_device_ids=true | all-gather | bytes 393216 | tf_op jit(solution)/shard_map/all_gather | solution.py:287
  39.1 2.4 %collective-permute-start.5 = (bf16[256,128]{1,0:T(8,128)(2,1)S(1)}, bf16[256,128]{1,0:T(8,128)(2,1)S(1)}, u32[]{:S(2)}, u32[]{:S(2)}) collective-permute-start(bf16[256,128]{1,0:T(8,128)(2,1)S(1)} %slice.25), channel_id=1, source_target_pairs={{1,4},{3,6},{5,8},{7,10},{9,12},{11,14},{13,16},{15,18},{17,20},{1... | collective-permute-start | bytes 196616 | tf_op jit(solution)/shard_map/ppermute | solution.py:291
  41.5 6.0 %all_gather.26.beside = bf16[1024,128]{1,0:T(8,128)(2,1)S(1)} all-gather(bf16[512,128]{1,0:T(8,128)(2,1)S(1)} %get-tuple-element.48.own), channel_id=1, replica_groups={{1,2},{3,4},{5,6},{7,8},{9,10},{11,12},{13,14},{15,16},{17,18},{19,20},..., dimensions={0}, use_global_device_ids=true | all-gather | bytes 393216 | tf_op jit(solution)/shard_map/all_gather | solution.py:287
  47.6 0.5 partial.4
  48.1 5.3 %collective-permute-start.7 = (bf16[512,128]{1,0:T(8,128)(2,1)S(1)}, bf16[512,128]{1,0:T(8,128)(2,1)S(1)}, u32[]{:S(2)}, u32[]{:S(2)}) collective-permute-start(bf16[512,128]{1,0:T(8,128)(2,1)S(1)} %get-tuple-element.51), channel_id=1, source_target_pairs={{0,32},{32,64},{64,96},{96,128},{128,160},{160,192},{192,224},{224... | collective-permute-start | bytes 393224 | tf_op jit(solution)/shard_map/ppermute | solution.py:328
  53.4 2.9 %collective-permute-start.8 = (bf16[512,128]{1,0:T(8,128)(2,1)S(1)}, bf16[512,128]{1,0:T(8,128)(2,1)S(1)}, u32[]{:S(2)}, u32[]{:S(2)}) collective-permute-start(bf16[512,128]{1,0:T(8,128)(2,1)S(1)} %get-tuple-element.52), channel_id=1, source_target_pairs={{16,32},{17,33},{18,34},{19,35},{20,36},{21,37},{22,38},{23,39},{2... | collective-permute-start | bytes 393224 | tf_op jit(solution)/shard_map/ppermute | solution.py:327
  56.3 4.7 %all_gather.27.both = bf16[1024,128]{1,0:T(8,128)(2,1)S(1)} all-gather(bf16[512,128]{1,0:T(8,128)(2,1)S(1)} %collective-permute-done.7), channel_id=1, replica_groups={{0,1},{2,3},{4,5},{6,7},{8,9},{10,11},{12,13},{14,15},{16,17},{18,19},{..., dimensions={0}, use_global_device_ids=true | all-gather | bytes 393216 | tf_op jit(solution)/shard_map/all_gather | solution.py:287
  61.0 0.5 collective-permute-done.8.refs_0_
  61.8 4.8 %collective-permute-start.9 = (bf16[256,128]{1,0:T(8,128)(2,1)S(1)}, bf16[256,128]{1,0:T(8,128)(2,1)S(1)}, u32[]{:S(2)}, u32[]{:S(2)}) collective-permute-start(bf16[256,128]{1,0:T(8,128)(2,1)S(1)} %slice.28), channel_id=1, source_target_pairs={{1,4},{3,6},{5,8},{7,10},{9,12},{11,14},{13,16},{15,18},{17,20},{1... | collective-permute-start | bytes 196616 | tf_op jit(solution)/shard_map/ppermute | solution.py:291
  66.6 6.0 %all_gather.28.beside = bf16[1024,128]{1,0:T(8,128)(2,1)S(1)} all-gather(bf16[512,128]{1,0:T(8,128)(2,1)S(1)} %get-tuple-element.53.own), channel_id=1, replica_groups={{1,2},{3,4},{5,6},{7,8},{9,10},{11,12},{13,14},{15,16},{17,18},{19,20},..., dimensions={0}, use_global_device_ids=true | all-gather | bytes 393216 | tf_op jit(solution)/shard_map/all_gather | solution.py:287
  72.6 0.5 partial.5
  73.1 4.6 %collective-permute-start.10 = (bf16[512,128]{1,0:T(8,128)(2,1)S(1)}, bf16[512,128]{1,0:T(8,128)(2,1)S(1)}, u32[]{:S(2)}, u32[]{:S(2)}) collective-permute-start(bf16[512,128]{1,0:T(8,128)(2,1)S(1)} %get-tuple-element.54), channel_id=1, source_target_pairs={{0,32},{32,64},{64,96},{96,128},{128,160},{160,192},{192,224},{224... | collective-permute-start | bytes 393224 | tf_op jit(solution)/shard_map/ppermute | solution.py:328
  77.7 2.7 %collective-permute-start.11 = (bf16[512,128]{1,0:T(8,128)(2,1)S(1)}, bf16[512,128]{1,0:T(8,128)(2,1)S(1)}, u32[]{:S(2)}, u32[]{:S(2)}) collective-permute-start(bf16[512,128]{1,0:T(8,128)(2,1)S(1)} %get-tuple-element.55), channel_id=1, source_target_pairs={{16,32},{17,33},{18,34},{19,35},{20,36},{21,37},{22,38},{23,39},{2... | collective-permute-start | bytes 393224 | tf_op jit(solution)/shard_map/ppermute | solution.py:327
  80.5 6.2 %all_gather.29.both = bf16[1024,128]{1,0:T(8,128)(2,1)S(1)} all-gather(bf16[512,128]{1,0:T(8,128)(2,1)S(1)} %collective-permute-done.10), channel_id=1, replica_groups={{0,1},{2,3},{4,5},{6,7},{8,9},{10,11},{12,13},{14,15},{16,17},{18,19},{..., dimensions={0}, use_global_device_ids=true | all-gather | bytes 393216 | tf_op jit(solution)/shard_map/all_gather | solution.py:287
  86.9 3.9 %collective-permute-start.12 = (bf16[256,128]{1,0:T(8,128)(2,1)S(1)}, bf16[256,128]{1,0:T(8,128)(2,1)S(1)}, u32[]{:S(2)}, u32[]{:S(2)}) collective-permute-start(bf16[256,128]{1,0:T(8,128)(2,1)S(1)} %slice.29), channel_id=1, source_target_pairs={{1,4},{3,6},{5,8},{7,10},{9,12},{11,14},{13,16},{15,18},{17,20},{1... | collective-permute-start | bytes 196616 | tf_op jit(solution)/shard_map/ppermute | solution.py:291
  90.8 3.5 %collective-permute-start.13 = (bf16[256,128]{1,0:T(8,128)(2,1)S(1)}, bf16[256,128]{1,0:T(8,128)(2,1)S(1)}, u32[]{:S(2)}, u32[]{:S(2)}) collective-permute-start(bf16[256,128]{1,0:T(8,128)(2,1)S(1)} %slice.29), channel_id=1, source_target_pairs={{0,16},{1,17},{2,18},{3,19},{4,20},{5,21},{6,22},{7,23},{8,24},{9,... | collective-permute-start | bytes 196616 | tf_op jit(solution)/shard_map/ppermute | solution.py:291
  94.3 5.9 %all_gather.30.beside = bf16[1024,128]{1,0:T(8,128)(2,1)S(1)} all-gather(bf16[512,128]{1,0:T(8,128)(2,1)S(1)} %get-tuple-element.56.own), channel_id=1, replica_groups={{1,2},{3,4},{5,6},{7,8},{9,10},{11,12},{13,14},{15,16},{17,18},{19,20},..., dimensions={0}, use_global_device_ids=true | all-gather | bytes 393216 | tf_op jit(solution)/shard_map/all_gather | solution.py:287
  100.2 1.0 last.1
  101.2 4.8 %all_gather.31.both = bf16[512,128]{1,0:T(8,128)(2,1)S(1)} all-gather(bf16[256,128]{1,0:T(8,128)(2,1)S(1)} %get-tuple-element.63), channel_id=1, replica_groups={{0,1},{2,3},{4,5},{6,7},{8,9},{10,11},{12,13},{14,15},{16,17},{18,19},{..., dimensions={0}, use_global_device_ids=true | all-gather | bytes 196608 | tf_op jit(solution)/shard_map/all_gather | solution.py:287
  106.0 0.7 carry.1
  (24 shorter events, 0.9 us)
Async XLA Ops:
  1.9 14.9 %collective-permute-start = (bf16[256,128]{1,0:T(8,128)(2,1)S(1)}, bf16[256,128]{1,0:T(8,128)(2,1)S(1)}, u32[]{:S(2)}, u32[]{:S(2)}) collective-permute-start(bf16[256,128]{1,0:T(8,128)(2,1)S(1)} %get-tuple-element.33), channel_id=1, source_target_pairs={{1,4},{3,6},{5,8},{7,10},{9,12},{11,14},{13,16},{15,18},{17,20},{1... | collective-permute-start | bytes 196616 | tf_op jit(solution)/shard_map/ppermute | solution.py:291
  7.1 9.7 %collective-permute-start.1 = (bf16[256,128]{1,0:T(8,128)(2,1)S(1)}, bf16[256,128]{1,0:T(8,128)(2,1)S(1)}, u32[]{:S(2)}, u32[]{:S(2)}) collective-permute-start(bf16[256,128]{1,0:T(8,128)(2,1)S(1)} %get-tuple-element.33), channel_id=1, source_target_pairs={{0,16},{1,17},{2,18},{3,19},{4,20},{5,21},{6,22},{7,23},{8,24},{9,... | collective-permute-start | bytes 196616 | tf_op jit(solution)/shard_map/ppermute | solution.py:291
  13.9 6.5 %collective-permute-start.2 = (bf16[512,128]{1,0:T(8,128)(2,1)S(1)}, bf16[512,128]{1,0:T(8,128)(2,1)S(1)}, u32[]{:S(2)}, u32[]{:S(2)}) collective-permute-start(bf16[512,128]{1,0:T(8,128)(2,1)S(1)} %maximum_select_fusion.own), channel_id=1, source_target_pairs={{1,2},{3,4},{5,6},{7,8},{9,10},{11,12},{13,14},{15,16},{17,18},{19... | collective-permute-start | bytes 393224 | tf_op jit(solution)/shard_map/ppermute | solution.py:291
  20.4 7.4 %collective-permute-start.3 = (bf16[2048,256]{1,0:T(8,128)(2,1)S(1)}, bf16[2048,256]{1,0:T(8,128)(2,1)S(1)}, u32[]{:S(2)}, u32[]{:S(2)}) collective-permute-start(bf16[2048,256]{1,0:T(8,128)(2,1)S(1)} %get-tuple-element.43), channel_id=1, source_target_pairs={{0,1},{2,3},{4,5},{6,7},{8,9},{10,11},{12,13},{14,15},{16,17},{18,... | collective-permute-start | bytes 3145736 | tf_op jit(solution)/shard_map/ppermute | solution.py:291
  28.3 8.0 %collective-permute-start.4 = (bf16[512,128]{1,0:T(8,128)(2,1)S(1)}, bf16[512,128]{1,0:T(8,128)(2,1)S(1)}, u32[]{:S(2)}, u32[]{:S(2)}) collective-permute-start(bf16[512,128]{1,0:T(8,128)(2,1)S(1)} %partial.3), channel_id=1, source_target_pairs={{0,32},{32,64},{64,96},{96,128},{128,160},{160,192},{192,224},{224... | collective-permute-start | bytes 393224 | tf_op jit(solution)/shard_map/ppermute | solution.py:328
  33.1 14.5 %collective-permute-start.6 = (bf16[512,256]{1,0:T(8,128)(2,1)S(1)}, bf16[512,256]{1,0:T(8,128)(2,1)S(1)}, u32[]{:S(2)}, u32[]{:S(2)}) collective-permute-start(bf16[512,256]{1,0:T(8,128)(2,1)S(1)} %pad_maximum_fusion.1), channel_id=1, source_target_pairs={{0,16},{1,17},{2,18},{3,19},{4,20},{5,21},{6,22},{7,23},{8,24},{9,... | collective-permute-start | bytes 786440 | tf_op jit(solution)/shard_map/ppermute | solution.py:291
  39.1 8.5 %collective-permute-start.5 = (bf16[256,128]{1,0:T(8,128)(2,1)S(1)}, bf16[256,128]{1,0:T(8,128)(2,1)S(1)}, u32[]{:S(2)}, u32[]{:S(2)}) collective-permute-start(bf16[256,128]{1,0:T(8,128)(2,1)S(1)} %slice.25), channel_id=1, source_target_pairs={{1,4},{3,6},{5,8},{7,10},{9,12},{11,14},{13,16},{15,18},{17,20},{1... | collective-permute-start | bytes 196616 | tf_op jit(solution)/shard_map/ppermute | solution.py:291
  48.1 8.2 %collective-permute-start.7 = (bf16[512,128]{1,0:T(8,128)(2,1)S(1)}, bf16[512,128]{1,0:T(8,128)(2,1)S(1)}, u32[]{:S(2)}, u32[]{:S(2)}) collective-permute-start(bf16[512,128]{1,0:T(8,128)(2,1)S(1)} %get-tuple-element.51), channel_id=1, source_target_pairs={{0,32},{32,64},{64,96},{96,128},{128,160},{160,192},{192,224},{224... | collective-permute-start | bytes 393224 | tf_op jit(solution)/shard_map/ppermute | solution.py:328
  53.4 8.1 %collective-permute-start.8 = (bf16[512,128]{1,0:T(8,128)(2,1)S(1)}, bf16[512,128]{1,0:T(8,128)(2,1)S(1)}, u32[]{:S(2)}, u32[]{:S(2)}) collective-permute-start(bf16[512,128]{1,0:T(8,128)(2,1)S(1)} %get-tuple-element.52), channel_id=1, source_target_pairs={{16,32},{17,33},{18,34},{19,35},{20,36},{21,37},{22,38},{23,39},{2... | collective-permute-start | bytes 393224 | tf_op jit(solution)/shard_map/ppermute | solution.py:327
  61.8 10.8 %collective-permute-start.9 = (bf16[256,128]{1,0:T(8,128)(2,1)S(1)}, bf16[256,128]{1,0:T(8,128)(2,1)S(1)}, u32[]{:S(2)}, u32[]{:S(2)}) collective-permute-start(bf16[256,128]{1,0:T(8,128)(2,1)S(1)} %slice.28), channel_id=1, source_target_pairs={{1,4},{3,6},{5,8},{7,10},{9,12},{11,14},{13,16},{15,18},{17,20},{1... | collective-permute-start | bytes 196616 | tf_op jit(solution)/shard_map/ppermute | solution.py:291
  73.1 7.4 %collective-permute-start.10 = (bf16[512,128]{1,0:T(8,128)(2,1)S(1)}, bf16[512,128]{1,0:T(8,128)(2,1)S(1)}, u32[]{:S(2)}, u32[]{:S(2)}) collective-permute-start(bf16[512,128]{1,0:T(8,128)(2,1)S(1)} %get-tuple-element.54), channel_id=1, source_target_pairs={{0,32},{32,64},{64,96},{96,128},{128,160},{160,192},{192,224},{224... | collective-permute-start | bytes 393224 | tf_op jit(solution)/shard_map/ppermute | solution.py:328
  77.7 8.9 %collective-permute-start.11 = (bf16[512,128]{1,0:T(8,128)(2,1)S(1)}, bf16[512,128]{1,0:T(8,128)(2,1)S(1)}, u32[]{:S(2)}, u32[]{:S(2)}) collective-permute-start(bf16[512,128]{1,0:T(8,128)(2,1)S(1)} %get-tuple-element.55), channel_id=1, source_target_pairs={{16,32},{17,33},{18,34},{19,35},{20,36},{21,37},{22,38},{23,39},{2... | collective-permute-start | bytes 393224 | tf_op jit(solution)/shard_map/ppermute | solution.py:327
  86.9 13.3 %collective-permute-start.12 = (bf16[256,128]{1,0:T(8,128)(2,1)S(1)}, bf16[256,128]{1,0:T(8,128)(2,1)S(1)}, u32[]{:S(2)}, u32[]{:S(2)}) collective-permute-start(bf16[256,128]{1,0:T(8,128)(2,1)S(1)} %slice.29), channel_id=1, source_target_pairs={{1,4},{3,6},{5,8},{7,10},{9,12},{11,14},{13,16},{15,18},{17,20},{1... | collective-permute-start | bytes 196616 | tf_op jit(solution)/shard_map/ppermute | solution.py:291
  90.8 9.4 %collective-permute-start.13 = (bf16[256,128]{1,0:T(8,128)(2,1)S(1)}, bf16[256,128]{1,0:T(8,128)(2,1)S(1)}, u32[]{:S(2)}, u32[]{:S(2)}) collective-permute-start(bf16[256,128]{1,0:T(8,128)(2,1)S(1)} %slice.29), channel_id=1, source_target_pairs={{0,16},{1,17},{2,18},{3,19},{4,20},{5,21},{6,22},{7,23},{8,24},{9,... | collective-permute-start | bytes 196616 | tf_op jit(solution)/shard_map/ppermute | solution.py:291

commit v4 on v3

--- a/solution.py
+++ b/solution.py
@@ -10,6 +10,7 @@
 F32 = jnp.float32
 BF16 = jnp.bfloat16
 VMEM = pl.BlockSpec(memory_space=pltpu.VMEM)
+SMEM = pl.BlockSpec(memory_space=pltpu.SMEM)
 HBM = pl.BlockSpec(memory_space=pltpu.HBM)
 LIMIT = 20 * 1024 * 1024
 
@@ -22,9 +23,9 @@
     return jnp.dot(a, b, preferred_element_type=F32)
 
 
-def combine_kernel(around, listed, blocks, inverse, right, kept, handed, listed_here, landing, sums, arrived, small):
+def combine_kernel(around, count, source_list, blocks, inverse, right, kept, handed, source_here, landing, sums, arrived, small):
     block = inverse.shape[0]
-    copy = pltpu.make_async_copy(listed, listed_here, small)
+    copy = pltpu.make_async_copy(source_list, source_here, small)
     copy.start()
     own = lax.axis_index("blk")
     sign = 2 * lax.rem(own, 2) - 1
@@ -32,8 +33,7 @@
     def copy_of(k):
         return pltpu.make_async_copy(blocks.at[0, k], landing.at[k], arrived.at[k])
 
-    copy.wait()
-    live = listed_here[0, blocks.shape[1]]
+    live = count[0]
 
     def begin(k, carry):
         copy_of(k).start()
@@ -48,10 +48,11 @@
         rows = pl.ds((5 + tick) * block, block)
         handed[rows, 0 : value.shape[1]] = high
         handed[rows, value.shape[1] :] = (value - high.astype(F32)).astype(BF16)
+    copy.wait()
 
     def add(k, carry):
         copy_of(k).wait()
-        offset = lax.rem(listed_here[0, k] - own + 3 + around, around) - 3
+        offset = lax.rem(source_here[0, k] - own + 3 + around, around) - 3
         turned = offset * sign
         slot = jnp.where(k == 0, 4, jnp.where(turned >= 0, 3 - turned, 8 + turned))
         sums[slot] = sums[slot] + landing[k].astype(F32)
@@ -72,17 +73,16 @@
 def combine(around, sources, counts, factor_blocks, inverse, right):
     slots, block = factor_blocks.shape[1], factor_blocks.shape[2]
     ticks = right.shape[0]
-    listed = jnp.concatenate([sources, counts[:, None]], 1)
     return pl.pallas_call(
         functools.partial(combine_kernel, around),
         out_shape=(
             jax.ShapeDtypeStruct((5, block, block), BF16),
             jax.ShapeDtypeStruct(((5 + ticks) * block, block), BF16),
         ),
-        in_specs=[HBM, HBM, VMEM, VMEM],
+        in_specs=[SMEM, HBM, HBM, VMEM, VMEM],
         out_specs=(VMEM, VMEM),
         scratch_shapes=[
-            pltpu.SMEM(listed.shape, jnp.int32),
+            pltpu.SMEM(sources.shape, jnp.int32),
             pltpu.VMEM((slots, block, block), BF16),
             pltpu.VMEM((8, block, block), F32),
             pltpu.SemaphoreType.DMA((slots,)),
@@ -91,7 +91,7 @@
         compiler_params=params(),
         cost_estimate=pl.CostEstimate(flops=4_000_000, bytes_accessed=10_000_000, transcendentals=0),
         name="combine",
-    )(in_hbm(listed), in_hbm(factor_blocks), inverse, right)
+    )(counts, in_hbm(sources), in_hbm(factor_blocks), inverse, right)
 
 
 def first_kernel(right, incoming, inverse, solved, outgoing, inverse_here, later_here, right_here, incoming_here, arrived):
@@ -176,12 +176,7 @@
 
 def products(kept, given, own, beside, third, opposite):
     block = third.shape[0]
-    near = lax.rem(lax.axis_index("blk"), 2) * (2 * block)
-
-    def part(at):
-        return beside[pl.ds(pl.multiple_of(at, block), block), :]
-
-    odd_one, same_one = part(near), part(near + block)
+    odd_one, same_one = beside[0:block], beside[block:]
     self_one = own[0:block]
     value = mm(kept[3], self_one)
     value += mm(kept[1], same_one)
@@ -303,15 +298,14 @@
         if tick == 0:
             chip = paired(own, chip_pairs)
             own = jnp.where(odd == 0, chip, jnp.roll(chip, block, 0))
-            near = swapped(own, next_pairs)
+            beside = swapped(own, next_pairs)
             held = (own, third, opposite, sources, counts, factor_blocks, inverse, right)
             own, third, opposite, *held = lax.optimization_barrier(held)
             kept, handed = combine(around, *held)
-            near, handed = lax.optimization_barrier((near, handed))
+            beside, handed = lax.optimization_barrier((beside, handed))
             given = swapped(handed, chip_pairs)
-            beside = jnp.concatenate([near, near], 0)
         else:
-            beside = paired(own, next_pairs)
+            beside = swapped(own, next_pairs)
         operands = [kept, given, own, beside, third]
         if last:
             exact, crossing, outputs = last_sums(operands + [opposite], finished)

time: 107 us -> 114 us (1.065)
  the two profiles are of different devices: /device:TPU:97 before, /device:TPU:99 now
where the time goes in v4:
time: 114 us
  starting transfers between devices  63.1 us (55%)
  blocking collectives  26.4 us (23%)
  waiting for transfers between devices  16.1 us (14%)
  Pallas kernels  6.48 us (6%)
  between operations  1.59 us (1%)
    ppermute x12, starting transfers between devices, swapped(): return lax.ppermute(value, 'blk', partner)  42 us
    all_gather x5, blocking collectives, paired(): lax.all_gather(value, 'blk', axis=0, tiled=True, axis_index_groups=pairs)  26.4 us
    ppermute x12, waiting for transfers between devices, swapped(): return lax.ppermute(value, 'blk', partner)  16.1 us
    ppermute x3, starting transfers between devices, shards(): moved = lax.ppermute(sums, 'grp', [(g, g + 1) for g in range(groups - 1)])  12.5 us
    ppermute x2, starting transfers between devices, shards(): far = lax.ppermute(leaving, ('grp', 'blk'), forward)  8.59 us
  transfers between devices with their start and end apart: 17, of which 6 were waited for; matrix products, arithmetic and copies ran while one was open for 0% of the time, Pallas kernels for 2%

profile of v4, /device:TPU:99, one launch (start us, length us, event | category | flops | bytes accessed | tf_op | source)
XLA Modules:
  0.0 113.8 jit_solution(7371521665746776621)
XLA Ops:
  0.6 1.2 %first.1 = (f32[256,128]{1,0:T(8,128)S(1)}, bf16[256,128]{1,0:T(8,128)(2,1)S(1)}, bf16[256,256]{1,0:T(8,128)(2,1)S(1)}, f32[3,256,128]{2,1,0:T(8,128)S(1)}) custom-call(f32[4,256,128]{2,1,0:T(8,128)} %right.1, f32[256,128]{1,0:T(8,128)} %incoming.1, bf16[256,256]{1,0:T(8,128)(2,1)} %inverse.1), custom_call_target="tpu_custom_call" | custom-call | tf_op jit(solution)/shard_map/first/pallas_call | solution.py:116
  1.9 2.2 %all_gather.15 = bf16[512,128]{1,0:T(8,128)(2,1)S(1)} all-gather(bf16[256,128]{1,0:T(8,128)(2,1)S(1)} %get-tuple-element.33), channel_id=1, replica_groups={{0,1},{2,3},{4,5},{6,7},{8,9},{10,11},{12,13},{14,15},{16,17},{18,19},{..., dimensions={0}, use_global_device_ids=true | all-gather | bytes 196608 | tf_op jit(solution)/shard_map/all_gather | solution.py:282
  4.2 3.4 %collective-permute-start.2 = (bf16[512,128]{1,0:T(8,128)(2,1)S(1)}, bf16[512,128]{1,0:T(8,128)(2,1)S(1)}, u32[]{:S(2)}, u32[]{:S(2)}) collective-permute-start(bf16[512,128]{1,0:T(8,128)(2,1)S(1)} %maximum_select_fusion.own), channel_id=1, source_target_pairs={{1,2},{3,4},{5,6},{7,8},{9,10},{11,12},{13,14},{15,16},{17,18},{19... | collective-permute-start | bytes 393224 | tf_op jit(solution)/shard_map/ppermute | solution.py:286
  7.5 3.1 %collective-permute-start = (bf16[256,128]{1,0:T(8,128)(2,1)S(1)}, bf16[256,128]{1,0:T(8,128)(2,1)S(1)}, u32[]{:S(2)}, u32[]{:S(2)}) collective-permute-start(bf16[256,128]{1,0:T(8,128)(2,1)S(1)} %get-tuple-element.33), channel_id=1, source_target_pairs={{1,4},{3,6},{5,8},{7,10},{9,12},{11,14},{13,16},{15,18},{17,20},{1... | collective-permute-start | bytes 196616 | tf_op jit(solution)/shard_map/ppermute | solution.py:286
  10.7 4.8 %collective-permute-start.1 = (bf16[256,128]{1,0:T(8,128)(2,1)S(1)}, bf16[256,128]{1,0:T(8,128)(2,1)S(1)}, u32[]{:S(2)}, u32[]{:S(2)}) collective-permute-start(bf16[256,128]{1,0:T(8,128)(2,1)S(1)} %get-tuple-element.33), channel_id=1, source_target_pairs={{0,16},{1,17},{2,18},{3,19},{4,20},{5,21},{6,22},{7,23},{8,24},{9,... | collective-permute-start | bytes 196616 | tf_op jit(solution)/shard_map/ppermute | solution.py:286
  16.2 1.0 collective-permute-done.1.opposite
  17.2 1.6 %combine.1 = (bf16[5,256,256]{2,1,0:T(8,128)(2,1)S(1)}, bf16[2048,256]{1,0:T(8,128)(2,1)S(1)}) custom-call(s32[1]{0:T(128)S(6)} %copy.8.count, s32[1,24]{1,0:T(1,128)} %source_list, bf16[1,24,256,256]{3,2,1,0:T(8,128)(2,1)} %blocks, bf16[256,256]{1,0:T(8,128)(2,1)S(1)} %get-tuple-element.39.inverse, f32[3,256,128]{2,1,0:T(8,128)S(1)} %get-tuple-element.40.right), custom_call_target="tpu_custom_call" | custom-call | flops 4000000 | bytes 10000000 | tf_op jit(solution)/shard_map/combine/pallas_call | solution.py:76
  18.8 5.3 %collective-permute-start.3 = (bf16[2048,256]{1,0:T(8,128)(2,1)S(1)}, bf16[2048,256]{1,0:T(8,128)(2,1)S(1)}, u32[]{:S(2)}, u32[]{:S(2)}) collective-permute-start(bf16[2048,256]{1,0:T(8,128)(2,1)S(1)} %get-tuple-element.43), channel_id=1, source_target_pairs={{0,1},{2,3},{4,5},{6,7},{8,9},{10,11},{12,13},{14,15},{16,17},{18,... | collective-permute-start | bytes 3145736 | tf_op jit(solution)/shard_map/ppermute | solution.py:286
  24.2 2.2 %collective-permute-done.3.given = bf16[2048,256]{1,0:T(8,128)(2,1)S(1)} collective-permute-done((bf16[2048,256]{1,0:T(8,128)(2,1)S(1)}, bf16[2048,256]{1,0:T(8,128)(2,1)S(1)}, u32[]{:S(2)}, u32[]{:S(2)}) %collective-permute-start.3) | collective-permute-done | bytes 1048608 | tf_op jit(solution)/shard_map/ppermute | solution.py:286
  26.9 4.8 %collective-permute-start.4 = (bf16[512,128]{1,0:T(8,128)(2,1)S(1)}, bf16[512,128]{1,0:T(8,128)(2,1)S(1)}, u32[]{:S(2)}, u32[]{:S(2)}) collective-permute-start(bf16[512,128]{1,0:T(8,128)(2,1)S(1)} %partial.3), channel_id=1, source_target_pairs={{0,32},{32,64},{64,96},{96,128},{128,160},{160,192},{192,224},{224... | collective-permute-start | bytes 393224 | tf_op jit(solution)/shard_map/ppermute | solution.py:322
  31.7 3.5 %collective-permute-start.7 = (bf16[512,256]{1,0:T(8,128)(2,1)S(1)}, bf16[512,256]{1,0:T(8,128)(2,1)S(1)}, u32[]{:S(2)}, u32[]{:S(2)}) collective-permute-start(bf16[512,256]{1,0:T(8,128)(2,1)S(1)} %pad_maximum_fusion), channel_id=1, source_target_pairs={{0,16},{1,17},{2,18},{3,19},{4,20},{5,21},{6,22},{7,23},{8,24},{9,... | collective-permute-start | bytes 786440 | tf_op jit(solution)/shard_map/ppermute | solution.py:286
  35.2 2.6 %all_gather.16.both = bf16[1024,128]{1,0:T(8,128)(2,1)S(1)} all-gather(bf16[512,128]{1,0:T(8,128)(2,1)S(1)} %collective-permute-done.4), channel_id=1, replica_groups={{0,1},{2,3},{4,5},{6,7},{8,9},{10,11},{12,13},{14,15},{16,17},{18,19},{..., dimensions={0}, use_global_device_ids=true | all-gather | bytes 393216 | tf_op jit(solution)/shard_map/all_gather | solution.py:282
  38.1 3.2 %collective-permute-start.5 = (bf16[512,128]{1,0:T(8,128)(2,1)S(1)}, bf16[512,128]{1,0:T(8,128)(2,1)S(1)}, u32[]{:S(2)}, u32[]{:S(2)}) collective-permute-start(bf16[512,128]{1,0:T(8,128)(2,1)S(1)} %get-tuple-element.48.own), channel_id=1, source_target_pairs={{1,2},{3,4},{5,6},{7,8},{9,10},{11,12},{13,14},{15,16},{17,18},{19... | collective-permute-start | bytes 393224 | tf_op jit(solution)/shard_map/ppermute | solution.py:286
  41.2 3.1 %collective-permute-start.6 = (bf16[256,128]{1,0:T(8,128)(2,1)S(1)}, bf16[256,128]{1,0:T(8,128)(2,1)S(1)}, u32[]{:S(2)}, u32[]{:S(2)}) collective-permute-start(bf16[256,128]{1,0:T(8,128)(2,1)S(1)} %slice.25), channel_id=1, source_target_pairs={{1,4},{3,6},{5,8},{7,10},{9,12},{11,14},{13,16},{15,18},{17,20},{1... | collective-permute-start | bytes 196616 | tf_op jit(solution)/shard_map/ppermute | solution.py:286
  44.4 4.2 %collective-permute-done.6.third = bf16[256,128]{1,0:T(8,128)(2,1)S(1)} collective-permute-done((bf16[256,128]{1,0:T(8,128)(2,1)S(1)}, bf16[256,128]{1,0:T(8,128)(2,1)S(1)}, u32[]{:S(2)}, u32[]{:S(2)}) %collective-permute-start.6) | collective-permute-done | bytes 65568 | tf_op jit(solution)/shard_map/ppermute | solution.py:286
  49.1 3.3 %collective-permute-start.8 = (bf16[512,128]{1,0:T(8,128)(2,1)S(1)}, bf16[512,128]{1,0:T(8,128)(2,1)S(1)}, u32[]{:S(2)}, u32[]{:S(2)}) collective-permute-start(bf16[512,128]{1,0:T(8,128)(2,1)S(1)} %get-tuple-element.51), channel_id=1, source_target_pairs={{0,32},{32,64},{64,96},{96,128},{128,160},{160,192},{192,224},{224... | collective-permute-start | bytes 393224 | tf_op jit(solution)/shard_map/ppermute | solution.py:322
  52.4 5.3 %collective-permute-start.9 = (bf16[512,128]{1,0:T(8,128)(2,1)S(1)}, bf16[512,128]{1,0:T(8,128)(2,1)S(1)}, u32[]{:S(2)}, u32[]{:S(2)}) collective-permute-start(bf16[512,128]{1,0:T(8,128)(2,1)S(1)} %get-tuple-element.52), channel_id=1, source_target_pairs={{16,32},{17,33},{18,34},{19,35},{20,36},{21,37},{22,38},{23,39},{2... | collective-permute-start | bytes 393224 | tf_op jit(solution)/shard_map/ppermute | solution.py:321
  57.7 4.3 %all_gather.17.both = bf16[1024,128]{1,0:T(8,128)(2,1)S(1)} all-gather(bf16[512,128]{1,0:T(8,128)(2,1)S(1)} %collective-permute-done.8), channel_id=1, replica_groups={{0,1},{2,3},{4,5},{6,7},{8,9},{10,11},{12,13},{14,15},{16,17},{18,19},{..., dimensions={0}, use_global_device_ids=true | all-gather | bytes 393216 | tf_op jit(solution)/shard_map/all_gather | solution.py:282
  62.3 3.7 %collective-permute-start.10 = (bf16[512,128]{1,0:T(8,128)(2,1)S(1)}, bf16[512,128]{1,0:T(8,128)(2,1)S(1)}, u32[]{:S(2)}, u32[]{:S(2)}) collective-permute-start(bf16[512,128]{1,0:T(8,128)(2,1)S(1)} %get-tuple-element.53.own), channel_id=1, source_target_pairs={{1,2},{3,4},{5,6},{7,8},{9,10},{11,12},{13,14},{15,16},{17,18},{19... | collective-permute-start | bytes 393224 | tf_op jit(solution)/shard_map/ppermute | solution.py:286
  66.0 2.1 %collective-permute-start.11 = (bf16[256,128]{1,0:T(8,128)(2,1)S(1)}, bf16[256,128]{1,0:T(8,128)(2,1)S(1)}, u32[]{:S(2)}, u32[]{:S(2)}) collective-permute-start(bf16[256,128]{1,0:T(8,128)(2,1)S(1)} %slice.28), channel_id=1, source_target_pairs={{1,4},{3,6},{5,8},{7,10},{9,12},{11,14},{13,16},{15,18},{17,20},{1... | collective-permute-start | bytes 196616 | tf_op jit(solution)/shard_map/ppermute | solution.py:286
  68.1 5.4 %collective-permute-done.11.third = bf16[256,128]{1,0:T(8,128)(2,1)S(1)} collective-permute-done((bf16[256,128]{1,0:T(8,128)(2,1)S(1)}, bf16[256,128]{1,0:T(8,128)(2,1)S(1)}, u32[]{:S(2)}, u32[]{:S(2)}) %collective-permute-start.11) | collective-permute-done | bytes 65568 | tf_op jit(solution)/shard_map/ppermute | solution.py:286
  74.0 4.4 %collective-permute-start.12 = (bf16[512,128]{1,0:T(8,128)(2,1)S(1)}, bf16[512,128]{1,0:T(8,128)(2,1)S(1)}, u32[]{:S(2)}, u32[]{:S(2)}) collective-permute-start(bf16[512,128]{1,0:T(8,128)(2,1)S(1)} %get-tuple-element.54), channel_id=1, source_target_pairs={{0,32},{32,64},{64,96},{96,128},{128,160},{160,192},{192,224},{224... | collective-permute-start | bytes 393224 | tf_op jit(solution)/shard_map/ppermute | solution.py:322
  78.4 3.3 %collective-permute-start.13 = (bf16[512,128]{1,0:T(8,128)(2,1)S(1)}, bf16[512,128]{1,0:T(8,128)(2,1)S(1)}, u32[]{:S(2)}, u32[]{:S(2)}) collective-permute-start(bf16[512,128]{1,0:T(8,128)(2,1)S(1)} %get-tuple-element.55), channel_id=1, source_target_pairs={{16,32},{17,33},{18,34},{19,35},{20,36},{21,37},{22,38},{23,39},{2... | collective-permute-start | bytes 393224 | tf_op jit(solution)/shard_map/ppermute | solution.py:321
  81.7 5.3 %all_gather.18.both = bf16[1024,128]{1,0:T(8,128)(2,1)S(1)} all-gather(bf16[512,128]{1,0:T(8,128)(2,1)S(1)} %collective-permute-done.12), channel_id=1, replica_groups={{0,1},{2,3},{4,5},{6,7},{8,9},{10,11},{12,13},{14,15},{16,17},{18,19},{..., dimensions={0}, use_global_device_ids=true | all-gather | bytes 393216 | tf_op jit(solution)/shard_map/all_gather | solution.py:282
  87.3 3.8 %collective-permute-start.14 = (bf16[512,128]{1,0:T(8,128)(2,1)S(1)}, bf16[512,128]{1,0:T(8,128)(2,1)S(1)}, u32[]{:S(2)}, u32[]{:S(2)}) collective-permute-start(bf16[512,128]{1,0:T(8,128)(2,1)S(1)} %get-tuple-element.56.own), channel_id=1, source_target_pairs={{1,2},{3,4},{5,6},{7,8},{9,10},{11,12},{13,14},{15,16},{17,18},{19... | collective-permute-start | bytes 393224 | tf_op jit(solution)/shard_map/ppermute | solution.py:286
  91.1 1.9 %collective-permute-start.15 = (bf16[256,128]{1,0:T(8,128)(2,1)S(1)}, bf16[256,128]{1,0:T(8,128)(2,1)S(1)}, u32[]{:S(2)}, u32[]{:S(2)}) collective-permute-start(bf16[256,128]{1,0:T(8,128)(2,1)S(1)} %slice.29), channel_id=1, source_target_pairs={{1,4},{3,6},{5,8},{7,10},{9,12},{11,14},{13,16},{15,18},{17,20},{1... | collective-permute-start | bytes 196616 | tf_op jit(solution)/shard_map/ppermute | solution.py:286
  93.0 4.0 %collective-permute-start.16 = (bf16[256,128]{1,0:T(8,128)(2,1)S(1)}, bf16[256,128]{1,0:T(8,128)(2,1)S(1)}, u32[]{:S(2)}, u32[]{:S(2)}) collective-permute-start(bf16[256,128]{1,0:T(8,128)(2,1)S(1)} %slice.29), channel_id=1, source_target_pairs={{0,16},{1,17},{2,18},{3,19},{4,20},{5,21},{6,22},{7,23},{8,24},{9,... | collective-permute-start | bytes 196616 | tf_op jit(solution)/shard_map/ppermute | solution.py:286
  97.1 1.7 %collective-permute-done.15.third = bf16[256,128]{1,0:T(8,128)(2,1)S(1)} collective-permute-done((bf16[256,128]{1,0:T(8,128)(2,1)S(1)}, bf16[256,128]{1,0:T(8,128)(2,1)S(1)}, u32[]{:S(2)}, u32[]{:S(2)}) %collective-permute-start.15) | collective-permute-done | bytes 65568 | tf_op jit(solution)/shard_map/ppermute | solution.py:286
  98.7 1.5 %collective-permute-done.16.opposite = bf16[256,128]{1,0:T(8,128)(2,1)S(1)} collective-permute-done((bf16[256,128]{1,0:T(8,128)(2,1)S(1)}, bf16[256,128]{1,0:T(8,128)(2,1)S(1)}, u32[]{:S(2)}, u32[]{:S(2)}) %collective-permute-start.16) | collective-permute-done | bytes 65568 | tf_op jit(solution)/shard_map/ppermute | solution.py:286
  100.3 0.8 last.1
  101.1 12.0 %all_gather.19.both = bf16[512,128]{1,0:T(8,128)(2,1)S(1)} all-gather(bf16[256,128]{1,0:T(8,128)(2,1)S(1)} %get-tuple-element.63), channel_id=1, replica_groups={{0,1},{2,3},{4,5},{6,7},{8,9},{10,11},{12,13},{14,15},{16,17},{18,19},{..., dimensions={0}, use_global_device_ids=true | all-gather | bytes 196608 | tf_op jit(solution)/shard_map/all_gather | solution.py:282
  113.1 0.7 carry.1
  (25 shorter events, 2.3 us)
Async XLA Ops:
  4.2 14.7 %collective-permute-start.2 = (bf16[512,128]{1,0:T(8,128)(2,1)S(1)}, bf16[512,128]{1,0:T(8,128)(2,1)S(1)}, u32[]{:S(2)}, u32[]{:S(2)}) collective-permute-start(bf16[512,128]{1,0:T(8,128)(2,1)S(1)} %maximum_select_fusion.own), channel_id=1, source_target_pairs={{1,2},{3,4},{5,6},{7,8},{9,10},{11,12},{13,14},{15,16},{17,18},{19... | collective-permute-start | bytes 393224 | tf_op jit(solution)/shard_map/ppermute | solution.py:286
  7.5 8.6 %collective-permute-start = (bf16[256,128]{1,0:T(8,128)(2,1)S(1)}, bf16[256,128]{1,0:T(8,128)(2,1)S(1)}, u32[]{:S(2)}, u32[]{:S(2)}) collective-permute-start(bf16[256,128]{1,0:T(8,128)(2,1)S(1)} %get-tuple-element.33), channel_id=1, source_target_pairs={{1,4},{3,6},{5,8},{7,10},{9,12},{11,14},{13,16},{15,18},{17,20},{1... | collective-permute-start | bytes 196616 | tf_op jit(solution)/shard_map/ppermute | solution.py:286
  10.7 6.5 %collective-permute-start.1 = (bf16[256,128]{1,0:T(8,128)(2,1)S(1)}, bf16[256,128]{1,0:T(8,128)(2,1)S(1)}, u32[]{:S(2)}, u32[]{:S(2)}) collective-permute-start(bf16[256,128]{1,0:T(8,128)(2,1)S(1)} %get-tuple-element.33), channel_id=1, source_target_pairs={{0,16},{1,17},{2,18},{3,19},{4,20},{5,21},{6,22},{7,23},{8,24},{9,... | collective-permute-start | bytes 196616 | tf_op jit(solution)/shard_map/ppermute | solution.py:286
  18.8 7.6 %collective-permute-start.3 = (bf16[2048,256]{1,0:T(8,128)(2,1)S(1)}, bf16[2048,256]{1,0:T(8,128)(2,1)S(1)}, u32[]{:S(2)}, u32[]{:S(2)}) collective-permute-start(bf16[2048,256]{1,0:T(8,128)(2,1)S(1)} %get-tuple-element.43), channel_id=1, source_target_pairs={{0,1},{2,3},{4,5},{6,7},{8,9},{10,11},{12,13},{14,15},{16,17},{18,... | collective-permute-start | bytes 3145736 | tf_op jit(solution)/shard_map/ppermute | solution.py:286
  26.9 8.4 %collective-permute-start.4 = (bf16[512,128]{1,0:T(8,128)(2,1)S(1)}, bf16[512,128]{1,0:T(8,128)(2,1)S(1)}, u32[]{:S(2)}, u32[]{:S(2)}) collective-permute-start(bf16[512,128]{1,0:T(8,128)(2,1)S(1)} %partial.3), channel_id=1, source_target_pairs={{0,32},{32,64},{64,96},{96,128},{128,160},{160,192},{192,224},{224... | collective-permute-start | bytes 393224 | tf_op jit(solution)/shard_map/ppermute | solution.py:322
  31.7 16.9 %collective-permute-start.7 = (bf16[512,256]{1,0:T(8,128)(2,1)S(1)}, bf16[512,256]{1,0:T(8,128)(2,1)S(1)}, u32[]{:S(2)}, u32[]{:S(2)}) collective-permute-start(bf16[512,256]{1,0:T(8,128)(2,1)S(1)} %pad_maximum_fusion), channel_id=1, source_target_pairs={{0,16},{1,17},{2,18},{3,19},{4,20},{5,21},{6,22},{7,23},{8,24},{9,... | collective-permute-start | bytes 786440 | tf_op jit(solution)/shard_map/ppermute | solution.py:286
  38.1 10.5 %collective-permute-start.5 = (bf16[512,128]{1,0:T(8,128)(2,1)S(1)}, bf16[512,128]{1,0:T(8,128)(2,1)S(1)}, u32[]{:S(2)}, u32[]{:S(2)}) collective-permute-start(bf16[512,128]{1,0:T(8,128)(2,1)S(1)} %get-tuple-element.48.own), channel_id=1, source_target_pairs={{1,2},{3,4},{5,6},{7,8},{9,10},{11,12},{13,14},{15,16},{17,18},{19... | collective-permute-start | bytes 393224 | tf_op jit(solution)/shard_map/ppermute | solution.py:286
  41.2 7.4 %collective-permute-start.6 = (bf16[256,128]{1,0:T(8,128)(2,1)S(1)}, bf16[256,128]{1,0:T(8,128)(2,1)S(1)}, u32[]{:S(2)}, u32[]{:S(2)}) collective-permute-start(bf16[256,128]{1,0:T(8,128)(2,1)S(1)} %slice.25), channel_id=1, source_target_pairs={{1,4},{3,6},{5,8},{7,10},{9,12},{11,14},{13,16},{15,18},{17,20},{1... | collective-permute-start | bytes 196616 | tf_op jit(solution)/shard_map/ppermute | solution.py:286
  49.1 8.6 %collective-permute-start.8 = (bf16[512,128]{1,0:T(8,128)(2,1)S(1)}, bf16[512,128]{1,0:T(8,128)(2,1)S(1)}, u32[]{:S(2)}, u32[]{:S(2)}) collective-permute-start(bf16[512,128]{1,0:T(8,128)(2,1)S(1)} %get-tuple-element.51), channel_id=1, source_target_pairs={{0,32},{32,64},{64,96},{96,128},{128,160},{160,192},{192,224},{224... | collective-permute-start | bytes 393224 | tf_op jit(solution)/shard_map/ppermute | solution.py:322
  52.4 9.6 %collective-permute-start.9 = (bf16[512,128]{1,0:T(8,128)(2,1)S(1)}, bf16[512,128]{1,0:T(8,128)(2,1)S(1)}, u32[]{:S(2)}, u32[]{:S(2)}) collective-permute-start(bf16[512,128]{1,0:T(8,128)(2,1)S(1)} %get-tuple-element.52), channel_id=1, source_target_pairs={{16,32},{17,33},{18,34},{19,35},{20,36},{21,37},{22,38},{23,39},{2... | collective-permute-start | bytes 393224 | tf_op jit(solution)/shard_map/ppermute | solution.py:321
  62.3 11.2 %collective-permute-start.10 = (bf16[512,128]{1,0:T(8,128)(2,1)S(1)}, bf16[512,128]{1,0:T(8,128)(2,1)S(1)}, u32[]{:S(2)}, u32[]{:S(2)}) collective-permute-start(bf16[512,128]{1,0:T(8,128)(2,1)S(1)} %get-tuple-element.53.own), channel_id=1, source_target_pairs={{1,2},{3,4},{5,6},{7,8},{9,10},{11,12},{13,14},{15,16},{17,18},{19... | collective-permute-start | bytes 393224 | tf_op jit(solution)/shard_map/ppermute | solution.py:286
  66.0 7.5 %collective-permute-start.11 = (bf16[256,128]{1,0:T(8,128)(2,1)S(1)}, bf16[256,128]{1,0:T(8,128)(2,1)S(1)}, u32[]{:S(2)}, u32[]{:S(2)}) collective-permute-start(bf16[256,128]{1,0:T(8,128)(2,1)S(1)} %slice.28), channel_id=1, source_target_pairs={{1,4},{3,6},{5,8},{7,10},{9,12},{11,14},{13,16},{15,18},{17,20},{1... | collective-permute-start | bytes 196616 | tf_op jit(solution)/shard_map/ppermute | solution.py:286
  74.0 7.7 %collective-permute-start.12 = (bf16[512,128]{1,0:T(8,128)(2,1)S(1)}, bf16[512,128]{1,0:T(8,128)(2,1)S(1)}, u32[]{:S(2)}, u32[]{:S(2)}) collective-permute-start(bf16[512,128]{1,0:T(8,128)(2,1)S(1)} %get-tuple-element.54), channel_id=1, source_target_pairs={{0,32},{32,64},{64,96},{96,128},{128,160},{160,192},{192,224},{224... | collective-permute-start | bytes 393224 | tf_op jit(solution)/shard_map/ppermute | solution.py:322
  78.4 8.6 %collective-permute-start.13 = (bf16[512,128]{1,0:T(8,128)(2,1)S(1)}, bf16[512,128]{1,0:T(8,128)(2,1)S(1)}, u32[]{:S(2)}, u32[]{:S(2)}) collective-permute-start(bf16[512,128]{1,0:T(8,128)(2,1)S(1)} %get-tuple-element.55), channel_id=1, source_target_pairs={{16,32},{17,33},{18,34},{19,35},{20,36},{21,37},{22,38},{23,39},{2... | collective-permute-start | bytes 393224 | tf_op jit(solution)/shard_map/ppermute | solution.py:321
  87.3 13.0 %collective-permute-start.14 = (bf16[512,128]{1,0:T(8,128)(2,1)S(1)}, bf16[512,128]{1,0:T(8,128)(2,1)S(1)}, u32[]{:S(2)}, u32[]{:S(2)}) collective-permute-start(bf16[512,128]{1,0:T(8,128)(2,1)S(1)} %get-tuple-element.56.own), channel_id=1, source_target_pairs={{1,2},{3,4},{5,6},{7,8},{9,10},{11,12},{13,14},{15,16},{17,18},{19... | collective-permute-start | bytes 393224 | tf_op jit(solution)/shard_map/ppermute | solution.py:286
  91.1 7.6 %collective-permute-start.15 = (bf16[256,128]{1,0:T(8,128)(2,1)S(1)}, bf16[256,128]{1,0:T(8,128)(2,1)S(1)}, u32[]{:S(2)}, u32[]{:S(2)}) collective-permute-start(bf16[256,128]{1,0:T(8,128)(2,1)S(1)} %slice.29), channel_id=1, source_target_pairs={{1,4},{3,6},{5,8},{7,10},{9,12},{11,14},{13,16},{15,18},{17,20},{1... | collective-permute-start | bytes 196616 | tf_op jit(solution)/shard_map/ppermute | solution.py:286
  93.0 7.2 %collective-permute-start.16 = (bf16[256,128]{1,0:T(8,128)(2,1)S(1)}, bf16[256,128]{1,0:T(8,128)(2,1)S(1)}, u32[]{:S(2)}, u32[]{:S(2)}) collective-permute-start(bf16[256,128]{1,0:T(8,128)(2,1)S(1)} %slice.29), channel_id=1, source_target_pairs={{0,16},{1,17},{2,18},{3,19},{4,20},{5,21},{6,22},{7,23},{8,24},{9,... | collective-permute-start | bytes 196616 | tf_op jit(solution)/shard_map/ppermute | solution.py:286

commit v5 on v4

--- a/solution.py
+++ b/solution.py
@@ -63,7 +63,8 @@
         kept[i] = sums[i].astype(BF16)
     for i in range(3):
         handed[i * block : (i + 1) * block, :] = sums[5 + i].astype(BF16)
-    handed[3 * block : 4 * block, :] = sums[4].astype(BF16)
+    odd = lax.rem(own, 2) == 1
+    handed[3 * block : 4 * block, :] = jnp.where(odd, sums[3], sums[4]).astype(BF16)
 
 
 def in_hbm(value):
@@ -133,9 +134,7 @@
     )(in_hbm(right_side), in_hbm(carry_in), in_hbm(inverse_diag))
 
 
-def pair_kernel(tick, both, right, inverse, given, *refs):
-    far = refs[:-2]
-    solved, outgoing = refs[-2:]
+def pair_kernel(tick, both, right, inverse, given, solved, outgoing):
     block, columns = solved.shape
     odd = lax.rem(lax.axis_index("blk"), 2)
     mine = odd * (2 * block)
@@ -146,9 +145,6 @@
 
     incoming = part(mine) + part(theirs + block)
     other = part(mine + block) + part(theirs)
-    for ref in far:
-        incoming += ref[0:block].astype(F32)
-        other += ref[block:].astype(F32)
     value = mm(inverse[...], (right[tick - 1] - incoming).astype(BF16))
     solved[...] = value
     outgoing[0:block] = value.astype(BF16)
@@ -158,9 +154,9 @@
     outgoing[block:] = value.astype(BF16)
 
 
-def pair_solve(tick, both, right, inverse, given, far):
+def pair_solve(tick, both, right, inverse, given):
     block, columns = right.shape[1:]
-    operands = [both, right, inverse, given] + ([] if far is None else [far])
+    operands = [both, right, inverse, given]
     return pl.pallas_call(
         functools.partial(pair_kernel, tick),
         out_shape=(
@@ -176,14 +172,18 @@
 
 def products(kept, given, own, beside, third, opposite):
     block = third.shape[0]
-    odd_one, same_one = beside[0:block], beside[block:]
+    near = lax.rem(lax.axis_index("blk"), 2) * (2 * block)
+
+    def part(at):
+        return beside[pl.ds(pl.multiple_of(at, block), block), :]
+
+    odd_one, same_one = part(near), part(near + block)
     self_one = own[0:block]
     value = mm(kept[3], self_one)
     value += mm(kept[1], same_one)
     value += mm(kept[2], odd_one)
     value += mm(kept[0], third[...])
-    if opposite is not None:
-        value += mm(kept[4], opposite[...])
+    value += mm(kept[4], opposite[...])
     other = mm(given[0:block, :], same_one)
     other += mm(given[block : 2 * block, :], odd_one)
     other += mm(given[2 * block : 3 * block, :], self_one)
@@ -197,13 +197,68 @@
     sums[block:] = other.astype(BF16)
 
 
-def far_kernel(kept, given, own, beside, third, far_sums, sums, leaving):
+def pack_kernel(kept, handed, given, packed):
+    block = packed.shape[1]
+    odd = lax.rem(lax.axis_index("blk"), 2)
+    for i in range(3):
+        packed[i * block : (i + 1) * block, :] = kept[i]
+    packed[3 * block : 5 * block, :] = given[0 : 2 * block, :]
+    packed[8 * block :, :] = given[3 * block : 4 * block, :]
+
+    @pl.when(odd == 0)
+    def _():
+        packed[5 * block : 6 * block, :] = kept[3]
+        packed[6 * block : 7 * block, :] = handed[2 * block : 3 * block, :]
+        packed[7 * block : 8 * block, :] = given[2 * block : 3 * block, :]
+
+    @pl.when(odd == 1)
+    def _():
+        packed[5 * block : 6 * block, :] = kept[4]
+        packed[6 * block : 8 * block, :] = jnp.zeros((2 * block, block), BF16)
+
+
+def pack(kept, handed, given):
+    block = kept.shape[1]
+    return pl.pallas_call(
+        pack_kernel,
+        out_shape=jax.ShapeDtypeStruct((9 * block, block), BF16),
+        in_specs=[VMEM] * 3,
+        out_specs=VMEM,
+        compiler_params=params(),
+        name="pack",
+    )(kept, handed, given)
+
+
+def landed_kernel(packed, beside, third, level, sums):
     block = third.shape[0]
-    value, other = products(kept, given, own, beside, third, None)
+
+    def factor(i):
+        return packed[i * block : (i + 1) * block, :]
+
+    odd_one, same_one = beside[0:block], beside[block:]
+    first, second = level[0:block], level[block:]
+    value = mm(factor(1), same_one)
+    value += mm(factor(2), odd_one)
+    value += mm(factor(5), first)
+    value += mm(factor(6), second)
+    value += mm(factor(0), third[...])
+    other = mm(factor(3), same_one)
+    other += mm(factor(4), odd_one)
+    other += mm(factor(7), first)
+    other += mm(factor(8), second)
     sums[0:block] = value.astype(BF16)
     sums[block:] = other.astype(BF16)
-    leaving[0:block] = mm(far_sums[0:block, :], own[0:block]).astype(BF16)
-    leaving[block:] = mm(far_sums[block:, :], own[block:]).astype(BF16)
+
+
+def landed_sums(packed, beside, third, level):
+    return pl.pallas_call(
+        landed_kernel,
+        out_shape=jax.ShapeDtypeStruct(beside.shape, BF16),
+        in_specs=[VMEM] * 4,
+        out_specs=VMEM,
+        compiler_params=params(),
+        name="landed",
+    )(packed, beside, third, level)
 
 
 def last_kernel(ticks, kept, given, own, beside, third, opposite, *refs):
@@ -219,13 +274,13 @@
         copy.wait()
 
 
-def partial_sums(kernel, operands, pairs_out):
+def partial_sums(operands):
     block, columns = operands[4].shape
     return pl.pallas_call(
-        kernel,
-        out_shape=(jax.ShapeDtypeStruct((2 * block, columns), BF16),) * pairs_out,
+        partial_kernel,
+        out_shape=jax.ShapeDtypeStruct((2 * block, columns), BF16),
         in_specs=[VMEM] * len(operands),
-        out_specs=(VMEM,) * pairs_out,
+        out_specs=VMEM,
         compiler_params=params(),
         name="partial",
     )(*operands)
@@ -287,42 +342,49 @@
 
     solved, own, inverse, right = first_solve(right_side, carry_in, inverse_diag)
     finished = [solved]
-    far_sums = None
-    forward = [(g * around + (b + chips) % around, (g + 1) * around + b) for g in range(groups - 1) for b in range(around)]
-    for tick in range(ticks):
-        last = tick + 1 == ticks
-        near_form = tick == 0 or last
+
+    def swapped_pairs(pairs):
+        return {a: b for a, b in pairs} | {b: a for a, b in pairs}
+
+    def forward(value, source_of):
+        pairs = [
+            (g * around + source_of[b], (g + 1) * around + b) for g in range(groups - 1) for b in range(around)
+        ]
+        return lax.ppermute(value, ("grp", "blk"), pairs)
+
+    level_of = {b: b if b % 2 == 0 else (b + chips) % around for b in range(around)}
+
+    def exchanged(own):
         mine = own[0:block]
-        third = swapped(mine, third_pairs)
-        opposite = swapped(mine, opposite_pairs) if near_form else None
-        if tick == 0:
-            chip = paired(own, chip_pairs)
-            own = jnp.where(odd == 0, chip, jnp.roll(chip, block, 0))
-            beside = swapped(own, next_pairs)
-            held = (own, third, opposite, sources, counts, factor_blocks, inverse, right)
-            own, third, opposite, *held = lax.optimization_barrier(held)
-            kept, handed = combine(around, *held)
-            beside, handed = lax.optimization_barrier((beside, handed))
-            given = swapped(handed, chip_pairs)
-        else:
-            beside = swapped(own, next_pairs)
-        operands = [kept, given, own, beside, third]
-        if last:
-            exact, crossing, outputs = last_sums(operands + [opposite], finished)
-            carry = carry_sum(exact, paired(crossing, chip_pairs))
-            return (outputs, carry)
-        far = None
-        if near_form:
-            (sums,) = partial_sums(partial_kernel, operands + [opposite], 1)
-            own_far, pair_far = lax.optimization_barrier((sums, kept[4], given[3 * block : 4 * block]))[1:]
-            far_sums = swapped(jnp.concatenate([own_far, pair_far], 0), opposite_pairs)
-        else:
-            sums, leaving = partial_sums(far_kernel, operands + [far_sums], 2)
-            far = lax.ppermute(leaving, ("grp", "blk"), forward)
-        moved = lax.ppermute(sums, "grp", [(g, g + 1) for g in range(groups - 1)])
-        both = paired(moved, chip_pairs)
-        solved, own = pair_solve(tick + 1, both, right, inverse, given, far)
+        return swapped(mine, third_pairs), swapped(mine, opposite_pairs)
+
+    third, opposite = exchanged(own)
+    chip = paired(own, chip_pairs)
+    own = jnp.where(odd == 0, chip, jnp.roll(chip, block, 0))
+    near = swapped(own, next_pairs)
+    held = (own, third, opposite, sources, counts, factor_blocks, inverse, right)
+    own, third, opposite, *held = lax.optimization_barrier(held)
+    kept, handed = combine(around, *held)
+    near, leaving = lax.optimization_barrier((near, handed))
+    given = swapped(leaving, chip_pairs)
+    beside = jnp.concatenate([near, near], 0)
+    sums = partial_sums([kept, given, own, beside, third, opposite])
+    sums = lax.ppermute(sums, "grp", [(g, g + 1) for g in range(groups - 1)])
+    sums, *held = lax.optimization_barrier((sums, kept, handed, given))
+    packed = forward(pack(*held), {b: b for b in range(around)})
+    for tick in range(1, ticks):
+        solved, own = pair_solve(tick, paired(sums, chip_pairs), right, inverse, given)
         finished.append(solved)
+        if tick + 1 < ticks:
+            beside = forward(own, swapped_pairs(next_pairs))
+            third = forward(own[0:block], swapped_pairs(third_pairs))
+            level = forward(own, level_of)
+            sums = landed_sums(packed, beside, third, level)
+    third, opposite = exchanged(own)
+    beside = paired(own, next_pairs)
+    exact, crossing, outputs = last_sums([kept, given, own, beside, third, opposite], finished)
+    carry = carry_sum(exact, paired(crossing, chip_pairs))
+    return (outputs, carry)
 
 
 def solution(mesh):

time: 114 us -> 120 us (1.053)
  the two profiles are of different devices: /device:TPU:99 before, /device:TPU:65 now
where the time goes in v5:
time: 120 us
  starting transfers between devices  55 us (46%)
  blocking collectives  28.5 us (24%)
  waiting for transfers between devices  28.2 us (24%)
  Pallas kernels  6.63 us (6%)
  between operations  1.53 us (1%)
    ppermute x7, starting transfers between devices, forward(): return lax.ppermute(value, ('grp', 'blk'), pairs)  29 us
    all_gather x6, blocking collectives, paired(): lax.all_gather(value, 'blk', axis=0, tiled=True, axis_index_groups=pairs)  28.5 us
    ppermute x6, starting transfers between devices, swapped(): return lax.ppermute(value, 'blk', partner)  22.8 us
    ppermute x7, waiting for transfers between devices, forward(): return lax.ppermute(value, ('grp', 'blk'), pairs)  21.5 us
    ppermute x1, waiting for transfers between devices, shards(): sums = lax.ppermute(sums, 'grp', [(g, g + 1) for g in range(groups - 1)])  3.37 us
    ppermute x6, waiting for transfers between devices, swapped(): return lax.ppermute(value, 'blk', partner)  3.27 us
    ppermute x1, starting transfers between devices, shards(): sums = lax.ppermute(sums, 'grp', [(g, g + 1) for g in range(groups - 1)])  3.23 us
  transfers between devices with their start and end apart: 14, of which 5 were waited for; matrix products, arithmetic and copies ran while one was open for 0% of the time, Pallas kernels for 1%

profile of v5, /device:TPU:65, one launch (start us, length us, event | category | flops | bytes accessed | tf_op | source)
XLA Modules:
  0.0 119.9 jit_solution(13752624563859283719)
XLA Ops:
  0.6 1.2 %first.1 = (f32[256,128]{1,0:T(8,128)S(1)}, bf16[256,128]{1,0:T(8,128)(2,1)S(1)}, bf16[256,256]{1,0:T(8,128)(2,1)S(1)}, f32[3,256,128]{2,1,0:T(8,128)S(1)}) custom-call(f32[4,256,128]{2,1,0:T(8,128)} %right.1, f32[256,128]{1,0:T(8,128)} %incoming.1, bf16[256,256]{1,0:T(8,128)(2,1)} %inverse.1), custom_call_target="tpu_custom_call" | custom-call | tf_op jit(solution)/shard_map/first/pallas_call | solution.py:117
  1.9 2.2 %all_gather.18 = bf16[512,128]{1,0:T(8,128)(2,1)S(1)} all-gather(bf16[256,128]{1,0:T(8,128)(2,1)S(1)} %get-tuple-element.31), channel_id=1, replica_groups={{0,1},{2,3},{4,5},{6,7},{8,9},{10,11},{12,13},{14,15},{16,17},{18,19},{..., dimensions={0}, use_global_device_ids=true | all-gather | bytes 196608 | tf_op jit(solution)/shard_map/all_gather | solution.py:337
  4.2 3.4 %collective-permute-start.2 = (bf16[512,128]{1,0:T(8,128)(2,1)S(1)}, bf16[512,128]{1,0:T(8,128)(2,1)S(1)}, u32[]{:S(2)}, u32[]{:S(2)}) collective-permute-start(bf16[512,128]{1,0:T(8,128)(2,1)S(1)} %maximum_select_fusion.own), channel_id=1, source_target_pairs={{1,2},{3,4},{5,6},{7,8},{9,10},{11,12},{13,14},{15,16},{17,18},{19... | collective-permute-start | bytes 393224 | tf_op jit(solution)/shard_map/ppermute | solution.py:341
  7.5 3.7 %collective-permute-start = (bf16[256,128]{1,0:T(8,128)(2,1)S(1)}, bf16[256,128]{1,0:T(8,128)(2,1)S(1)}, u32[]{:S(2)}, u32[]{:S(2)}) collective-permute-start(bf16[256,128]{1,0:T(8,128)(2,1)S(1)} %get-tuple-element.31), channel_id=1, source_target_pairs={{1,4},{3,6},{5,8},{7,10},{9,12},{11,14},{13,16},{15,18},{17,20},{1... | collective-permute-start | bytes 196616 | tf_op jit(solution)/shard_map/ppermute | solution.py:341
  11.3 4.8 %collective-permute-start.1 = (bf16[256,128]{1,0:T(8,128)(2,1)S(1)}, bf16[256,128]{1,0:T(8,128)(2,1)S(1)}, u32[]{:S(2)}, u32[]{:S(2)}) collective-permute-start(bf16[256,128]{1,0:T(8,128)(2,1)S(1)} %get-tuple-element.31), channel_id=1, source_target_pairs={{0,16},{1,17},{2,18},{3,19},{4,20},{5,21},{6,22},{7,23},{8,24},{9,... | collective-permute-start | bytes 196616 | tf_op jit(solution)/shard_map/ppermute | solution.py:341
  16.8 1.0 collective-permute-done.1.opposite
  17.8 1.5 %combine.1 = (bf16[5,256,256]{2,1,0:T(8,128)(2,1)S(1)}, bf16[2048,256]{1,0:T(8,128)(2,1)S(1)}) custom-call(s32[1]{0:T(128)S(6)} %copy.8.count, s32[1,24]{1,0:T(1,128)} %source_list, bf16[1,24,256,256]{3,2,1,0:T(8,128)(2,1)} %blocks, bf16[256,256]{1,0:T(8,128)(2,1)S(1)} %get-tuple-element.37.inverse, f32[3,256,128]{2,1,0:T(8,128)S(1)} %get-tuple-element.38.right), custom_call_target="tpu_custom_call" | custom-call | flops 4000000 | bytes 10000000 | tf_op jit(solution)/shard_map/combine/pallas_call | solution.py:77
  19.4 6.9 %collective-permute-start.3 = (bf16[2048,256]{1,0:T(8,128)(2,1)S(1)}, bf16[2048,256]{1,0:T(8,128)(2,1)S(1)}, u32[]{:S(2)}, u32[]{:S(2)}) collective-permute-start(bf16[2048,256]{1,0:T(8,128)(2,1)S(1)} %get-tuple-element.47.handed), channel_id=1, source_target_pairs={{0,1},{2,3},{4,5},{6,7},{8,9},{10,11},{12,13},{14,15},{16,17},{18,... | collective-permute-start | bytes 3145736 | tf_op jit(solution)/shard_map/ppermute | solution.py:341
  26.3 2.2 %collective-permute-done.3.given = bf16[2048,256]{1,0:T(8,128)(2,1)S(1)} collective-permute-done((bf16[2048,256]{1,0:T(8,128)(2,1)S(1)}, bf16[2048,256]{1,0:T(8,128)(2,1)S(1)}, u32[]{:S(2)}, u32[]{:S(2)}) %collective-permute-start.3) | collective-permute-done | bytes 1048608 | tf_op jit(solution)/shard_map/ppermute | solution.py:341
  28.5 0.4 partial.1
  29.0 3.2 %collective-permute-start.4 = (bf16[512,128]{1,0:T(8,128)(2,1)S(1)}, bf16[512,128]{1,0:T(8,128)(2,1)S(1)}, u32[]{:S(2)}, u32[]{:S(2)}) collective-permute-start(bf16[512,128]{1,0:T(8,128)(2,1)S(1)} %partial.1), channel_id=1, source_target_pairs={{0,32},{32,64},{64,96},{96,128},{128,160},{160,192},{192,224},{224... | collective-permute-start | bytes 393224 | tf_op jit(solution)/shard_map/ppermute | solution.py:372
  32.2 3.4 %collective-permute-done.4 = bf16[512,128]{1,0:T(8,128)(2,1)S(1)} collective-permute-done((bf16[512,128]{1,0:T(8,128)(2,1)S(1)}, bf16[512,128]{1,0:T(8,128)(2,1)S(1)}, u32[]{:S(2)}, u32[]{:S(2)}) %collective-permute-start.4) | collective-permute-done | bytes 131104 | tf_op jit(solution)/shard_map/ppermute | solution.py:372
  35.7 3.9 %collective-permute-start.5 = (bf16[2304,256]{1,0:T(8,128)(2,1)S(1)}, bf16[2304,256]{1,0:T(8,128)(2,1)S(1)}, u32[]{:S(2)}, u32[]{:S(2)}) collective-permute-start(bf16[2304,256]{1,0:T(8,128)(2,1)S(1)} %pack.1), channel_id=1, source_target_pairs={{0,32},{1,33},{2,34},{3,35},{4,36},{5,37},{6,38},{7,39},{8,40},{9,... | collective-permute-start | bytes 3538952 | tf_op jit(solution)/shard_map/ppermute | solution.py:353
  39.5 3.1 %all_gather.19.both = bf16[1024,128]{1,0:T(8,128)(2,1)S(1)} all-gather(bf16[512,128]{1,0:T(8,128)(2,1)S(1)} %collective-permute-done.4), channel_id=1, replica_groups={{0,1},{2,3},{4,5},{6,7},{8,9},{10,11},{12,13},{14,15},{16,17},{18,19},{..., dimensions={0}, use_global_device_ids=true | all-gather | bytes 393216 | tf_op jit(solution)/shard_map/all_gather | solution.py:337
  42.9 4.8 %collective-permute-start.6 = (bf16[512,128]{1,0:T(8,128)(2,1)S(1)}, bf16[512,128]{1,0:T(8,128)(2,1)S(1)}, u32[]{:S(2)}, u32[]{:S(2)}) collective-permute-start(bf16[512,128]{1,0:T(8,128)(2,1)S(1)} %get-tuple-element.50), channel_id=1, source_target_pairs={{31,32},{2,33},{1,34},{4,35},{3,36},{6,37},{5,38},{8,39},{7,40},{1... | collective-permute-start | bytes 393224 | tf_op jit(solution)/shard_map/ppermute | solution.py:353
  47.7 3.8 %collective-permute-start.8 = (bf16[512,128]{1,0:T(8,128)(2,1)S(1)}, bf16[512,128]{1,0:T(8,128)(2,1)S(1)}, u32[]{:S(2)}, u32[]{:S(2)}) collective-permute-start(bf16[512,128]{1,0:T(8,128)(2,1)S(1)} %get-tuple-element.50), channel_id=1, source_target_pairs={{0,32},{17,33},{2,34},{19,35},{4,36},{21,37},{6,38},{23,39},{8,40}... | collective-permute-start | bytes 393224 | tf_op jit(solution)/shard_map/ppermute | solution.py:353
  51.5 3.7 %collective-permute-start.7 = (bf16[256,128]{1,0:T(8,128)(2,1)S(1)}, bf16[256,128]{1,0:T(8,128)(2,1)S(1)}, u32[]{:S(2)}, u32[]{:S(2)}) collective-permute-start(bf16[256,128]{1,0:T(8,128)(2,1)S(1)} %slice.19), channel_id=1, source_target_pairs={{29,32},{4,33},{31,34},{6,35},{1,36},{8,37},{3,38},{10,39},{5,40},... | collective-permute-start | bytes 196616 | tf_op jit(solution)/shard_map/ppermute | solution.py:353
  55.3 15.8 %collective-permute-done.7.third = bf16[256,128]{1,0:T(8,128)(2,1)S(1)} collective-permute-done((bf16[256,128]{1,0:T(8,128)(2,1)S(1)}, bf16[256,128]{1,0:T(8,128)(2,1)S(1)}, u32[]{:S(2)}, u32[]{:S(2)}) %collective-permute-start.7) | collective-permute-done | bytes 65568 | tf_op jit(solution)/shard_map/ppermute | solution.py:353
  71.0 0.5 landed.2
  71.5 4.2 %all_gather.20.both = bf16[1024,128]{1,0:T(8,128)(2,1)S(1)} all-gather(bf16[512,128]{1,0:T(8,128)(2,1)S(1)} %landed.2), channel_id=1, replica_groups={{0,1},{2,3},{4,5},{6,7},{8,9},{10,11},{12,13},{14,15},{16,17},{18,19},{..., dimensions={0}, use_global_device_ids=true | all-gather | bytes 393216 | tf_op jit(solution)/shard_map/all_gather | solution.py:337
  76.0 3.9 %collective-permute-start.9 = (bf16[512,128]{1,0:T(8,128)(2,1)S(1)}, bf16[512,128]{1,0:T(8,128)(2,1)S(1)}, u32[]{:S(2)}, u32[]{:S(2)}) collective-permute-start(bf16[512,128]{1,0:T(8,128)(2,1)S(1)} %get-tuple-element.51), channel_id=1, source_target_pairs={{31,32},{2,33},{1,34},{4,35},{3,36},{6,37},{5,38},{8,39},{7,40},{1... | collective-permute-start | bytes 393224 | tf_op jit(solution)/shard_map/ppermute | solution.py:353
  79.9 6.7 %collective-permute-start.11 = (bf16[512,128]{1,0:T(8,128)(2,1)S(1)}, bf16[512,128]{1,0:T(8,128)(2,1)S(1)}, u32[]{:S(2)}, u32[]{:S(2)}) collective-permute-start(bf16[512,128]{1,0:T(8,128)(2,1)S(1)} %get-tuple-element.51), channel_id=1, source_target_pairs={{0,32},{17,33},{2,34},{19,35},{4,36},{21,37},{6,38},{23,39},{8,40}... | collective-permute-start | bytes 393224 | tf_op jit(solution)/shard_map/ppermute | solution.py:353
  86.6 2.2 %collective-permute-start.10 = (bf16[256,128]{1,0:T(8,128)(2,1)S(1)}, bf16[256,128]{1,0:T(8,128)(2,1)S(1)}, u32[]{:S(2)}, u32[]{:S(2)}) collective-permute-start(bf16[256,128]{1,0:T(8,128)(2,1)S(1)} %slice.20), channel_id=1, source_target_pairs={{29,32},{4,33},{31,34},{6,35},{1,36},{8,37},{3,38},{10,39},{5,40},... | collective-permute-start | bytes 196616 | tf_op jit(solution)/shard_map/ppermute | solution.py:353
  88.8 5.7 %collective-permute-done.10.third = bf16[256,128]{1,0:T(8,128)(2,1)S(1)} collective-permute-done((bf16[256,128]{1,0:T(8,128)(2,1)S(1)}, bf16[256,128]{1,0:T(8,128)(2,1)S(1)}, u32[]{:S(2)}, u32[]{:S(2)}) %collective-permute-start.10) | collective-permute-done | bytes 65568 | tf_op jit(solution)/shard_map/ppermute | solution.py:353
  94.6 0.5 landed.3
  95.1 6.7 %all_gather.21.both = bf16[1024,128]{1,0:T(8,128)(2,1)S(1)} all-gather(bf16[512,128]{1,0:T(8,128)(2,1)S(1)} %landed.3), channel_id=1, replica_groups={{0,1},{2,3},{4,5},{6,7},{8,9},{10,11},{12,13},{14,15},{16,17},{18,19},{..., dimensions={0}, use_global_device_ids=true | all-gather | bytes 393216 | tf_op jit(solution)/shard_map/all_gather | solution.py:337
  102.0 1.9 %collective-permute-start.12 = (bf16[256,128]{1,0:T(8,128)(2,1)S(1)}, bf16[256,128]{1,0:T(8,128)(2,1)S(1)}, u32[]{:S(2)}, u32[]{:S(2)}) collective-permute-start(bf16[256,128]{1,0:T(8,128)(2,1)S(1)} %slice.21), channel_id=1, source_target_pairs={{1,4},{3,6},{5,8},{7,10},{9,12},{11,14},{13,16},{15,18},{17,20},{1... | collective-permute-start | bytes 196616 | tf_op jit(solution)/shard_map/ppermute | solution.py:341
  103.9 2.0 %collective-permute-start.13 = (bf16[256,128]{1,0:T(8,128)(2,1)S(1)}, bf16[256,128]{1,0:T(8,128)(2,1)S(1)}, u32[]{:S(2)}, u32[]{:S(2)}) collective-permute-start(bf16[256,128]{1,0:T(8,128)(2,1)S(1)} %slice.21), channel_id=1, source_target_pairs={{0,16},{1,17},{2,18},{3,19},{4,20},{5,21},{6,22},{7,23},{8,24},{9,... | collective-permute-start | bytes 196616 | tf_op jit(solution)/shard_map/ppermute | solution.py:341
  105.9 8.4 %all_gather.22.beside = bf16[1024,128]{1,0:T(8,128)(2,1)S(1)} all-gather(bf16[512,128]{1,0:T(8,128)(2,1)S(1)} %get-tuple-element.52.own), channel_id=1, replica_groups={{1,2},{3,4},{5,6},{7,8},{9,10},{11,12},{13,14},{15,16},{17,18},{19,20},..., dimensions={0}, use_global_device_ids=true | all-gather | bytes 393216 | tf_op jit(solution)/shard_map/all_gather | solution.py:337
  114.3 1.0 last.1
  115.3 3.9 %all_gather.23.both = bf16[512,128]{1,0:T(8,128)(2,1)S(1)} all-gather(bf16[256,128]{1,0:T(8,128)(2,1)S(1)} %get-tuple-element.59), channel_id=1, replica_groups={{0,1},{2,3},{4,5},{6,7},{8,9},{10,11},{12,13},{14,15},{16,17},{18,19},{..., dimensions={0}, use_global_device_ids=true | all-gather | bytes 196608 | tf_op jit(solution)/shard_map/all_gather | solution.py:337
  119.2 0.7 carry.1
  (19 shorter events, 0.9 us)
Async XLA Ops:
  4.2 15.2 %collective-permute-start.2 = (bf16[512,128]{1,0:T(8,128)(2,1)S(1)}, bf16[512,128]{1,0:T(8,128)(2,1)S(1)}, u32[]{:S(2)}, u32[]{:S(2)}) collective-permute-start(bf16[512,128]{1,0:T(8,128)(2,1)S(1)} %maximum_select_fusion.own), channel_id=1, source_target_pairs={{1,2},{3,4},{5,6},{7,8},{9,10},{11,12},{13,14},{15,16},{17,18},{19... | collective-permute-start | bytes 393224 | tf_op jit(solution)/shard_map/ppermute | solution.py:341
  7.5 9.2 %collective-permute-start = (bf16[256,128]{1,0:T(8,128)(2,1)S(1)}, bf16[256,128]{1,0:T(8,128)(2,1)S(1)}, u32[]{:S(2)}, u32[]{:S(2)}) collective-permute-start(bf16[256,128]{1,0:T(8,128)(2,1)S(1)} %get-tuple-element.31), channel_id=1, source_target_pairs={{1,4},{3,6},{5,8},{7,10},{9,12},{11,14},{13,16},{15,18},{17,20},{1... | collective-permute-start | bytes 196616 | tf_op jit(solution)/shard_map/ppermute | solution.py:341
  11.3 6.5 %collective-permute-start.1 = (bf16[256,128]{1,0:T(8,128)(2,1)S(1)}, bf16[256,128]{1,0:T(8,128)(2,1)S(1)}, u32[]{:S(2)}, u32[]{:S(2)}) collective-permute-start(bf16[256,128]{1,0:T(8,128)(2,1)S(1)} %get-tuple-element.31), channel_id=1, source_target_pairs={{0,16},{1,17},{2,18},{3,19},{4,20},{5,21},{6,22},{7,23},{8,24},{9,... | collective-permute-start | bytes 196616 | tf_op jit(solution)/shard_map/ppermute | solution.py:341
  19.4 9.2 %collective-permute-start.3 = (bf16[2048,256]{1,0:T(8,128)(2,1)S(1)}, bf16[2048,256]{1,0:T(8,128)(2,1)S(1)}, u32[]{:S(2)}, u32[]{:S(2)}) collective-permute-start(bf16[2048,256]{1,0:T(8,128)(2,1)S(1)} %get-tuple-element.47.handed), channel_id=1, source_target_pairs={{0,1},{2,3},{4,5},{6,7},{8,9},{10,11},{12,13},{14,15},{16,17},{18,... | collective-permute-start | bytes 3145736 | tf_op jit(solution)/shard_map/ppermute | solution.py:341
  29.0 6.6 %collective-permute-start.4 = (bf16[512,128]{1,0:T(8,128)(2,1)S(1)}, bf16[512,128]{1,0:T(8,128)(2,1)S(1)}, u32[]{:S(2)}, u32[]{:S(2)}) collective-permute-start(bf16[512,128]{1,0:T(8,128)(2,1)S(1)} %partial.1), channel_id=1, source_target_pairs={{0,32},{32,64},{64,96},{96,128},{128,160},{160,192},{192,224},{224... | collective-permute-start | bytes 393224 | tf_op jit(solution)/shard_map/ppermute | solution.py:372
  35.7 35.4 %collective-permute-start.5 = (bf16[2304,256]{1,0:T(8,128)(2,1)S(1)}, bf16[2304,256]{1,0:T(8,128)(2,1)S(1)}, u32[]{:S(2)}, u32[]{:S(2)}) collective-permute-start(bf16[2304,256]{1,0:T(8,128)(2,1)S(1)} %pack.1), channel_id=1, source_target_pairs={{0,32},{1,33},{2,34},{3,35},{4,36},{5,37},{6,38},{7,39},{8,40},{9,... | collective-permute-start | bytes 3538952 | tf_op jit(solution)/shard_map/ppermute | solution.py:353
  42.9 28.1 %collective-permute-start.6 = (bf16[512,128]{1,0:T(8,128)(2,1)S(1)}, bf16[512,128]{1,0:T(8,128)(2,1)S(1)}, u32[]{:S(2)}, u32[]{:S(2)}) collective-permute-start(bf16[512,128]{1,0:T(8,128)(2,1)S(1)} %get-tuple-element.50), channel_id=1, source_target_pairs={{31,32},{2,33},{1,34},{4,35},{3,36},{6,37},{5,38},{8,39},{7,40},{1... | collective-permute-start | bytes 393224 | tf_op jit(solution)/shard_map/ppermute | solution.py:353
  47.7 23.3 %collective-permute-start.8 = (bf16[512,128]{1,0:T(8,128)(2,1)S(1)}, bf16[512,128]{1,0:T(8,128)(2,1)S(1)}, u32[]{:S(2)}, u32[]{:S(2)}) collective-permute-start(bf16[512,128]{1,0:T(8,128)(2,1)S(1)} %get-tuple-element.50), channel_id=1, source_target_pairs={{0,32},{17,33},{2,34},{19,35},{4,36},{21,37},{6,38},{23,39},{8,40}... | collective-permute-start | bytes 393224 | tf_op jit(solution)/shard_map/ppermute | solution.py:353
  51.5 19.5 %collective-permute-start.7 = (bf16[256,128]{1,0:T(8,128)(2,1)S(1)}, bf16[256,128]{1,0:T(8,128)(2,1)S(1)}, u32[]{:S(2)}, u32[]{:S(2)}) collective-permute-start(bf16[256,128]{1,0:T(8,128)(2,1)S(1)} %slice.19), channel_id=1, source_target_pairs={{29,32},{4,33},{31,34},{6,35},{1,36},{8,37},{3,38},{10,39},{5,40},... | collective-permute-start | bytes 196616 | tf_op jit(solution)/shard_map/ppermute | solution.py:353
  76.0 18.6 %collective-permute-start.9 = (bf16[512,128]{1,0:T(8,128)(2,1)S(1)}, bf16[512,128]{1,0:T(8,128)(2,1)S(1)}, u32[]{:S(2)}, u32[]{:S(2)}) collective-permute-start(bf16[512,128]{1,0:T(8,128)(2,1)S(1)} %get-tuple-element.51), channel_id=1, source_target_pairs={{31,32},{2,33},{1,34},{4,35},{3,36},{6,37},{5,38},{8,39},{7,40},{1... | collective-permute-start | bytes 393224 | tf_op jit(solution)/shard_map/ppermute | solution.py:353
  79.9 14.7 %collective-permute-start.11 = (bf16[512,128]{1,0:T(8,128)(2,1)S(1)}, bf16[512,128]{1,0:T(8,128)(2,1)S(1)}, u32[]{:S(2)}, u32[]{:S(2)}) collective-permute-start(bf16[512,128]{1,0:T(8,128)(2,1)S(1)} %get-tuple-element.51), channel_id=1, source_target_pairs={{0,32},{17,33},{2,34},{19,35},{4,36},{21,37},{6,38},{23,39},{8,40}... | collective-permute-start | bytes 393224 | tf_op jit(solution)/shard_map/ppermute | solution.py:353
  86.6 8.0 %collective-permute-start.10 = (bf16[256,128]{1,0:T(8,128)(2,1)S(1)}, bf16[256,128]{1,0:T(8,128)(2,1)S(1)}, u32[]{:S(2)}, u32[]{:S(2)}) collective-permute-start(bf16[256,128]{1,0:T(8,128)(2,1)S(1)} %slice.20), channel_id=1, source_target_pairs={{29,32},{4,33},{31,34},{6,35},{1,36},{8,37},{3,38},{10,39},{5,40},... | collective-permute-start | bytes 196616 | tf_op jit(solution)/shard_map/ppermute | solution.py:353
  102.0 12.3 %collective-permute-start.12 = (bf16[256,128]{1,0:T(8,128)(2,1)S(1)}, bf16[256,128]{1,0:T(8,128)(2,1)S(1)}, u32[]{:S(2)}, u32[]{:S(2)}) collective-permute-start(bf16[256,128]{1,0:T(8,128)(2,1)S(1)} %slice.21), channel_id=1, source_target_pairs={{1,4},{3,6},{5,8},{7,10},{9,12},{11,14},{13,16},{15,18},{17,20},{1... | collective-permute-start | bytes 196616 | tf_op jit(solution)/shard_map/ppermute | solution.py:341
  103.9 10.4 %collective-permute-start.13 = (bf16[256,128]{1,0:T(8,128)(2,1)S(1)}, bf16[256,128]{1,0:T(8,128)(2,1)S(1)}, u32[]{:S(2)}, u32[]{:S(2)}) collective-permute-start(bf16[256,128]{1,0:T(8,128)(2,1)S(1)} %slice.21), channel_id=1, source_target_pairs={{0,16},{1,17},{2,18},{3,19},{4,20},{5,21},{6,22},{7,23},{8,24},{9,... | collective-permute-start | bytes 196616 | tf_op jit(solution)/shard_map/ppermute | solution.py:341

commit v6 on v4

--- a/solution.py
+++ b/solution.py
@@ -176,7 +176,12 @@
 
 def products(kept, given, own, beside, third, opposite):
     block = third.shape[0]
-    odd_one, same_one = beside[0:block], beside[block:]
+    near = lax.rem(lax.axis_index("blk"), 2) * (2 * block)
+
+    def part(at):
+        return beside[pl.ds(pl.multiple_of(at, block), block), :]
+
+    odd_one, same_one = part(near), part(near + block)
     self_one = own[0:block]
     value = mm(kept[3], self_one)
     value += mm(kept[1], same_one)
@@ -298,14 +303,11 @@
         if tick == 0:
             chip = paired(own, chip_pairs)
             own = jnp.where(odd == 0, chip, jnp.roll(chip, block, 0))
-            beside = swapped(own, next_pairs)
             held = (own, third, opposite, sources, counts, factor_blocks, inverse, right)
             own, third, opposite, *held = lax.optimization_barrier(held)
             kept, handed = combine(around, *held)
-            beside, handed = lax.optimization_barrier((beside, handed))
             given = swapped(handed, chip_pairs)
-        else:
-            beside = swapped(own, next_pairs)
+        beside = paired(own, next_pairs)
         operands = [kept, given, own, beside, third]
         if last:
             exact, crossing, outputs = last_sums(operands + [opposite], finished)

time: 114 us -> 107 us (0.939)
  the two profiles are of different devices: /device:TPU:99 before, /device:TPU:97 now
where the time goes in v6:
time: 107 us; the launch traced here: 106 us
  starting transfers between devices  53.3 us (50%)
  blocking collectives  44.2 us (41%)
  Pallas kernels  6.34 us (6%)
  between operations  1.56 us (1%)
    all_gather x9, blocking collectives, paired(): lax.all_gather(value, 'blk', axis=0, tiled=True, axis_index_groups=pairs)  44.2 us
    ppermute x8, starting transfers between devices, swapped(): return lax.ppermute(value, 'blk', partner)  32.3 us
    ppermute x3, starting transfers between devices, shards(): moved = lax.ppermute(sums, 'grp', [(g, g + 1) for g in range(groups - 1)])  13.3 us
    ppermute x2, starting transfers between devices, shards(): far = lax.ppermute(leaving, ('grp', 'blk'), forward)  7.65 us
  transfers between devices with their start and end apart: 13, of which 1 were waited for; matrix products, arithmetic and copies ran while one was open for 0% of the time, Pallas kernels for 0%

profile of v6, /device:TPU:97, one launch (start us, length us, event | category | flops | bytes accessed | tf_op | source)
XLA Modules:
  0.0 106.0 jit_solution(14690224264588358181)
XLA Ops:
  0.6 1.2 %first.1 = (f32[256,128]{1,0:T(8,128)S(1)}, bf16[256,128]{1,0:T(8,128)(2,1)S(1)}, bf16[256,256]{1,0:T(8,128)(2,1)S(1)}, f32[3,256,128]{2,1,0:T(8,128)S(1)}) custom-call(f32[4,256,128]{2,1,0:T(8,128)} %right.1, f32[256,128]{1,0:T(8,128)} %incoming.1, bf16[256,256]{1,0:T(8,128)(2,1)} %inverse.1), custom_call_target="tpu_custom_call" | custom-call | tf_op jit(solution)/shard_map/first/pallas_call | solution.py:116
  1.9 5.2 %collective-permute-start = (bf16[256,128]{1,0:T(8,128)(2,1)S(1)}, bf16[256,128]{1,0:T(8,128)(2,1)S(1)}, u32[]{:S(2)}, u32[]{:S(2)}) collective-permute-start(bf16[256,128]{1,0:T(8,128)(2,1)S(1)} %get-tuple-element.31), channel_id=1, source_target_pairs={{1,4},{3,6},{5,8},{7,10},{9,12},{11,14},{13,16},{15,18},{17,20},{1... | collective-permute-start | bytes 196616 | tf_op jit(solution)/shard_map/ppermute | solution.py:291
  7.1 4.8 %collective-permute-start.1 = (bf16[256,128]{1,0:T(8,128)(2,1)S(1)}, bf16[256,128]{1,0:T(8,128)(2,1)S(1)}, u32[]{:S(2)}, u32[]{:S(2)}) collective-permute-start(bf16[256,128]{1,0:T(8,128)(2,1)S(1)} %get-tuple-element.31), channel_id=1, source_target_pairs={{0,16},{1,17},{2,18},{3,19},{4,20},{5,21},{6,22},{7,23},{8,24},{9,... | collective-permute-start | bytes 196616 | tf_op jit(solution)/shard_map/ppermute | solution.py:291
  11.9 1.9 %all_gather.27 = bf16[512,128]{1,0:T(8,128)(2,1)S(1)} all-gather(bf16[256,128]{1,0:T(8,128)(2,1)S(1)} %get-tuple-element.31), channel_id=1, replica_groups={{0,1},{2,3},{4,5},{6,7},{8,9},{10,11},{12,13},{14,15},{16,17},{18,19},{..., dimensions={0}, use_global_device_ids=true | all-gather | bytes 196608 | tf_op jit(solution)/shard_map/all_gather | solution.py:287
  14.6 1.3 %combine.1 = (bf16[5,256,256]{2,1,0:T(8,128)(2,1)S(1)}, bf16[2048,256]{1,0:T(8,128)(2,1)S(1)}) custom-call(s32[1]{0:T(128)S(6)} %copy.8.count, s32[1,24]{1,0:T(1,128)} %source_list, bf16[1,24,256,256]{3,2,1,0:T(8,128)(2,1)} %blocks, bf16[256,256]{1,0:T(8,128)(2,1)S(1)} %get-tuple-element.37.inverse, f32[3,256,128]{2,1,0:T(8,128)S(1)} %get-tuple-element.38.right), custom_call_target="tpu_custom_call" | custom-call | flops 4000000 | bytes 10000000 | tf_op jit(solution)/shard_map/combine/pallas_call | solution.py:76
  15.9 4.6 %collective-permute-start.2 = (bf16[2048,256]{1,0:T(8,128)(2,1)S(1)}, bf16[2048,256]{1,0:T(8,128)(2,1)S(1)}, u32[]{:S(2)}, u32[]{:S(2)}) collective-permute-start(bf16[2048,256]{1,0:T(8,128)(2,1)S(1)} %get-tuple-element.40), channel_id=1, source_target_pairs={{0,1},{2,3},{4,5},{6,7},{8,9},{10,11},{12,13},{14,15},{16,17},{18,... | collective-permute-start | bytes 3145736 | tf_op jit(solution)/shard_map/ppermute | solution.py:291
  20.5 5.4 %all_gather.28.beside = bf16[1024,128]{1,0:T(8,128)(2,1)S(1)} all-gather(bf16[512,128]{1,0:T(8,128)(2,1)S(1)} %maximum_select_fusion.own), channel_id=1, replica_groups={{1,2},{3,4},{5,6},{7,8},{9,10},{11,12},{13,14},{15,16},{17,18},{19,20},..., dimensions={0}, use_global_device_ids=true | all-gather | bytes 393216 | tf_op jit(solution)/shard_map/all_gather | solution.py:287
  25.9 0.4 partial.3
  26.3 4.9 %collective-permute-start.3 = (bf16[512,128]{1,0:T(8,128)(2,1)S(1)}, bf16[512,128]{1,0:T(8,128)(2,1)S(1)}, u32[]{:S(2)}, u32[]{:S(2)}) collective-permute-start(bf16[512,128]{1,0:T(8,128)(2,1)S(1)} %partial.3), channel_id=1, source_target_pairs={{0,32},{32,64},{64,96},{96,128},{128,160},{160,192},{192,224},{224... | collective-permute-start | bytes 393224 | tf_op jit(solution)/shard_map/ppermute | solution.py:324
  31.3 2.6 %collective-permute-start.5 = (bf16[512,256]{1,0:T(8,128)(2,1)S(1)}, bf16[512,256]{1,0:T(8,128)(2,1)S(1)}, u32[]{:S(2)}, u32[]{:S(2)}) collective-permute-start(bf16[512,256]{1,0:T(8,128)(2,1)S(1)} %pad_maximum_fusion), channel_id=1, source_target_pairs={{0,16},{1,17},{2,18},{3,19},{4,20},{5,21},{6,22},{7,23},{8,24},{9,... | collective-permute-start | bytes 786440 | tf_op jit(solution)/shard_map/ppermute | solution.py:291
  34.0 4.7 %all_gather.29.both = bf16[1024,128]{1,0:T(8,128)(2,1)S(1)} all-gather(bf16[512,128]{1,0:T(8,128)(2,1)S(1)} %collective-permute-done.3), channel_id=1, replica_groups={{0,1},{2,3},{4,5},{6,7},{8,9},{10,11},{12,13},{14,15},{16,17},{18,19},{..., dimensions={0}, use_global_device_ids=true | all-gather | bytes 393216 | tf_op jit(solution)/shard_map/all_gather | solution.py:287
  39.0 1.9 %collective-permute-start.4 = (bf16[256,128]{1,0:T(8,128)(2,1)S(1)}, bf16[256,128]{1,0:T(8,128)(2,1)S(1)}, u32[]{:S(2)}, u32[]{:S(2)}) collective-permute-start(bf16[256,128]{1,0:T(8,128)(2,1)S(1)} %slice.25), channel_id=1, source_target_pairs={{1,4},{3,6},{5,8},{7,10},{9,12},{11,14},{13,16},{15,18},{17,20},{1... | collective-permute-start | bytes 196616 | tf_op jit(solution)/shard_map/ppermute | solution.py:291
  40.9 5.4 %all_gather.30.beside = bf16[1024,128]{1,0:T(8,128)(2,1)S(1)} all-gather(bf16[512,128]{1,0:T(8,128)(2,1)S(1)} %get-tuple-element.44.own), channel_id=1, replica_groups={{1,2},{3,4},{5,6},{7,8},{9,10},{11,12},{13,14},{15,16},{17,18},{19,20},..., dimensions={0}, use_global_device_ids=true | all-gather | bytes 393216 | tf_op jit(solution)/shard_map/all_gather | solution.py:287
  46.3 0.5 collective-permute-done.4.third
  46.7 0.5 partial.4
  47.2 4.9 %collective-permute-start.6 = (bf16[512,128]{1,0:T(8,128)(2,1)S(1)}, bf16[512,128]{1,0:T(8,128)(2,1)S(1)}, u32[]{:S(2)}, u32[]{:S(2)}) collective-permute-start(bf16[512,128]{1,0:T(8,128)(2,1)S(1)} %get-tuple-element.47), channel_id=1, source_target_pairs={{0,32},{32,64},{64,96},{96,128},{128,160},{160,192},{192,224},{224... | collective-permute-start | bytes 393224 | tf_op jit(solution)/shard_map/ppermute | solution.py:324
  52.1 4.6 %collective-permute-start.7 = (bf16[512,128]{1,0:T(8,128)(2,1)S(1)}, bf16[512,128]{1,0:T(8,128)(2,1)S(1)}, u32[]{:S(2)}, u32[]{:S(2)}) collective-permute-start(bf16[512,128]{1,0:T(8,128)(2,1)S(1)} %get-tuple-element.48), channel_id=1, source_target_pairs={{16,32},{17,33},{18,34},{19,35},{20,36},{21,37},{22,38},{23,39},{2... | collective-permute-start | bytes 393224 | tf_op jit(solution)/shard_map/ppermute | solution.py:323
  56.8 4.2 %all_gather.31.both = bf16[1024,128]{1,0:T(8,128)(2,1)S(1)} all-gather(bf16[512,128]{1,0:T(8,128)(2,1)S(1)} %collective-permute-done.6), channel_id=1, replica_groups={{0,1},{2,3},{4,5},{6,7},{8,9},{10,11},{12,13},{14,15},{16,17},{18,19},{..., dimensions={0}, use_global_device_ids=true | all-gather | bytes 393216 | tf_op jit(solution)/shard_map/all_gather | solution.py:287
  61.0 0.3 solve.4
  61.3 5.5 %collective-permute-start.8 = (bf16[256,128]{1,0:T(8,128)(2,1)S(1)}, bf16[256,128]{1,0:T(8,128)(2,1)S(1)}, u32[]{:S(2)}, u32[]{:S(2)}) collective-permute-start(bf16[256,128]{1,0:T(8,128)(2,1)S(1)} %slice.28), channel_id=1, source_target_pairs={{1,4},{3,6},{5,8},{7,10},{9,12},{11,14},{13,16},{15,18},{17,20},{1... | collective-permute-start | bytes 196616 | tf_op jit(solution)/shard_map/ppermute | solution.py:291
  66.7 6.2 %all_gather.32.beside = bf16[1024,128]{1,0:T(8,128)(2,1)S(1)} all-gather(bf16[512,128]{1,0:T(8,128)(2,1)S(1)} %get-tuple-element.49.own), channel_id=1, replica_groups={{1,2},{3,4},{5,6},{7,8},{9,10},{11,12},{13,14},{15,16},{17,18},{19,20},..., dimensions={0}, use_global_device_ids=true | all-gather | bytes 393216 | tf_op jit(solution)/shard_map/all_gather | solution.py:287
  72.9 0.5 partial.5
  73.4 3.5 %collective-permute-start.9 = (bf16[512,128]{1,0:T(8,128)(2,1)S(1)}, bf16[512,128]{1,0:T(8,128)(2,1)S(1)}, u32[]{:S(2)}, u32[]{:S(2)}) collective-permute-start(bf16[512,128]{1,0:T(8,128)(2,1)S(1)} %get-tuple-element.50), channel_id=1, source_target_pairs={{0,32},{32,64},{64,96},{96,128},{128,160},{160,192},{192,224},{224... | collective-permute-start | bytes 393224 | tf_op jit(solution)/shard_map/ppermute | solution.py:324
  76.9 3.0 %collective-permute-start.10 = (bf16[512,128]{1,0:T(8,128)(2,1)S(1)}, bf16[512,128]{1,0:T(8,128)(2,1)S(1)}, u32[]{:S(2)}, u32[]{:S(2)}) collective-permute-start(bf16[512,128]{1,0:T(8,128)(2,1)S(1)} %get-tuple-element.51), channel_id=1, source_target_pairs={{16,32},{17,33},{18,34},{19,35},{20,36},{21,37},{22,38},{23,39},{2... | collective-permute-start | bytes 393224 | tf_op jit(solution)/shard_map/ppermute | solution.py:323
  80.0 6.1 %all_gather.33.both = bf16[1024,128]{1,0:T(8,128)(2,1)S(1)} all-gather(bf16[512,128]{1,0:T(8,128)(2,1)S(1)} %collective-permute-done.9), channel_id=1, replica_groups={{0,1},{2,3},{4,5},{6,7},{8,9},{10,11},{12,13},{14,15},{16,17},{18,19},{..., dimensions={0}, use_global_device_ids=true | all-gather | bytes 393216 | tf_op jit(solution)/shard_map/all_gather | solution.py:287
  86.0 0.3 solve.5
  86.3 3.7 %collective-permute-start.11 = (bf16[256,128]{1,0:T(8,128)(2,1)S(1)}, bf16[256,128]{1,0:T(8,128)(2,1)S(1)}, u32[]{:S(2)}, u32[]{:S(2)}) collective-permute-start(bf16[256,128]{1,0:T(8,128)(2,1)S(1)} %slice.29), channel_id=1, source_target_pairs={{1,4},{3,6},{5,8},{7,10},{9,12},{11,14},{13,16},{15,18},{17,20},{1... | collective-permute-start | bytes 196616 | tf_op jit(solution)/shard_map/ppermute | solution.py:291
  90.0 3.9 %collective-permute-start.12 = (bf16[256,128]{1,0:T(8,128)(2,1)S(1)}, bf16[256,128]{1,0:T(8,128)(2,1)S(1)}, u32[]{:S(2)}, u32[]{:S(2)}) collective-permute-start(bf16[256,128]{1,0:T(8,128)(2,1)S(1)} %slice.29), channel_id=1, source_target_pairs={{0,16},{1,17},{2,18},{3,19},{4,20},{5,21},{6,22},{7,23},{8,24},{9,... | collective-permute-start | bytes 196616 | tf_op jit(solution)/shard_map/ppermute | solution.py:291
  93.9 5.4 %all_gather.34.beside = bf16[1024,128]{1,0:T(8,128)(2,1)S(1)} all-gather(bf16[512,128]{1,0:T(8,128)(2,1)S(1)} %get-tuple-element.52.own), channel_id=1, replica_groups={{1,2},{3,4},{5,6},{7,8},{9,10},{11,12},{13,14},{15,16},{17,18},{19,20},..., dimensions={0}, use_global_device_ids=true | all-gather | bytes 393216 | tf_op jit(solution)/shard_map/all_gather | solution.py:287
  99.3 1.0 last.1
  100.3 5.0 %all_gather.35.both = bf16[512,128]{1,0:T(8,128)(2,1)S(1)} all-gather(bf16[256,128]{1,0:T(8,128)(2,1)S(1)} %get-tuple-element.59), channel_id=1, replica_groups={{0,1},{2,3},{4,5},{6,7},{8,9},{10,11},{12,13},{14,15},{16,17},{18,19},{..., dimensions={0}, use_global_device_ids=true | all-gather | bytes 196608 | tf_op jit(solution)/shard_map/all_gather | solution.py:287
  105.4 0.7 carry.1
  (21 shorter events, 0.4 us)
Async XLA Ops:
  1.9 12.7 %collective-permute-start = (bf16[256,128]{1,0:T(8,128)(2,1)S(1)}, bf16[256,128]{1,0:T(8,128)(2,1)S(1)}, u32[]{:S(2)}, u32[]{:S(2)}) collective-permute-start(bf16[256,128]{1,0:T(8,128)(2,1)S(1)} %get-tuple-element.31), channel_id=1, source_target_pairs={{1,4},{3,6},{5,8},{7,10},{9,12},{11,14},{13,16},{15,18},{17,20},{1... | collective-permute-start | bytes 196616 | tf_op jit(solution)/shard_map/ppermute | solution.py:291
  7.1 7.5 %collective-permute-start.1 = (bf16[256,128]{1,0:T(8,128)(2,1)S(1)}, bf16[256,128]{1,0:T(8,128)(2,1)S(1)}, u32[]{:S(2)}, u32[]{:S(2)}) collective-permute-start(bf16[256,128]{1,0:T(8,128)(2,1)S(1)} %get-tuple-element.31), channel_id=1, source_target_pairs={{0,16},{1,17},{2,18},{3,19},{4,20},{5,21},{6,22},{7,23},{8,24},{9,... | collective-permute-start | bytes 196616 | tf_op jit(solution)/shard_map/ppermute | solution.py:291
  15.9 10.0 %collective-permute-start.2 = (bf16[2048,256]{1,0:T(8,128)(2,1)S(1)}, bf16[2048,256]{1,0:T(8,128)(2,1)S(1)}, u32[]{:S(2)}, u32[]{:S(2)}) collective-permute-start(bf16[2048,256]{1,0:T(8,128)(2,1)S(1)} %get-tuple-element.40), channel_id=1, source_target_pairs={{0,1},{2,3},{4,5},{6,7},{8,9},{10,11},{12,13},{14,15},{16,17},{18,... | collective-permute-start | bytes 3145736 | tf_op jit(solution)/shard_map/ppermute | solution.py:291
  26.3 7.6 %collective-permute-start.3 = (bf16[512,128]{1,0:T(8,128)(2,1)S(1)}, bf16[512,128]{1,0:T(8,128)(2,1)S(1)}, u32[]{:S(2)}, u32[]{:S(2)}) collective-permute-start(bf16[512,128]{1,0:T(8,128)(2,1)S(1)} %partial.3), channel_id=1, source_target_pairs={{0,32},{32,64},{64,96},{96,128},{128,160},{160,192},{192,224},{224... | collective-permute-start | bytes 393224 | tf_op jit(solution)/shard_map/ppermute | solution.py:324
  31.3 15.4 %collective-permute-start.5 = (bf16[512,256]{1,0:T(8,128)(2,1)S(1)}, bf16[512,256]{1,0:T(8,128)(2,1)S(1)}, u32[]{:S(2)}, u32[]{:S(2)}) collective-permute-start(bf16[512,256]{1,0:T(8,128)(2,1)S(1)} %pad_maximum_fusion), channel_id=1, source_target_pairs={{0,16},{1,17},{2,18},{3,19},{4,20},{5,21},{6,22},{7,23},{8,24},{9,... | collective-permute-start | bytes 786440 | tf_op jit(solution)/shard_map/ppermute | solution.py:291
  39.0 7.8 %collective-permute-start.4 = (bf16[256,128]{1,0:T(8,128)(2,1)S(1)}, bf16[256,128]{1,0:T(8,128)(2,1)S(1)}, u32[]{:S(2)}, u32[]{:S(2)}) collective-permute-start(bf16[256,128]{1,0:T(8,128)(2,1)S(1)} %slice.25), channel_id=1, source_target_pairs={{1,4},{3,6},{5,8},{7,10},{9,12},{11,14},{13,16},{15,18},{17,20},{1... | collective-permute-start | bytes 196616 | tf_op jit(solution)/shard_map/ppermute | solution.py:291
  47.2 9.5 %collective-permute-start.6 = (bf16[512,128]{1,0:T(8,128)(2,1)S(1)}, bf16[512,128]{1,0:T(8,128)(2,1)S(1)}, u32[]{:S(2)}, u32[]{:S(2)}) collective-permute-start(bf16[512,128]{1,0:T(8,128)(2,1)S(1)} %get-tuple-element.47), channel_id=1, source_target_pairs={{0,32},{32,64},{64,96},{96,128},{128,160},{160,192},{192,224},{224... | collective-permute-start | bytes 393224 | tf_op jit(solution)/shard_map/ppermute | solution.py:324
  52.1 8.9 %collective-permute-start.7 = (bf16[512,128]{1,0:T(8,128)(2,1)S(1)}, bf16[512,128]{1,0:T(8,128)(2,1)S(1)}, u32[]{:S(2)}, u32[]{:S(2)}) collective-permute-start(bf16[512,128]{1,0:T(8,128)(2,1)S(1)} %get-tuple-element.48), channel_id=1, source_target_pairs={{16,32},{17,33},{18,34},{19,35},{20,36},{21,37},{22,38},{23,39},{2... | collective-permute-start | bytes 393224 | tf_op jit(solution)/shard_map/ppermute | solution.py:323
  61.3 11.7 %collective-permute-start.8 = (bf16[256,128]{1,0:T(8,128)(2,1)S(1)}, bf16[256,128]{1,0:T(8,128)(2,1)S(1)}, u32[]{:S(2)}, u32[]{:S(2)}) collective-permute-start(bf16[256,128]{1,0:T(8,128)(2,1)S(1)} %slice.28), channel_id=1, source_target_pairs={{1,4},{3,6},{5,8},{7,10},{9,12},{11,14},{13,16},{15,18},{17,20},{1... | collective-permute-start | bytes 196616 | tf_op jit(solution)/shard_map/ppermute | solution.py:291
  73.4 6.5 %collective-permute-start.9 = (bf16[512,128]{1,0:T(8,128)(2,1)S(1)}, bf16[512,128]{1,0:T(8,128)(2,1)S(1)}, u32[]{:S(2)}, u32[]{:S(2)}) collective-permute-start(bf16[512,128]{1,0:T(8,128)(2,1)S(1)} %get-tuple-element.50), channel_id=1, source_target_pairs={{0,32},{32,64},{64,96},{96,128},{128,160},{160,192},{192,224},{224... | collective-permute-start | bytes 393224 | tf_op jit(solution)/shard_map/ppermute | solution.py:324
  76.9 9.1 %collective-permute-start.10 = (bf16[512,128]{1,0:T(8,128)(2,1)S(1)}, bf16[512,128]{1,0:T(8,128)(2,1)S(1)}, u32[]{:S(2)}, u32[]{:S(2)}) collective-permute-start(bf16[512,128]{1,0:T(8,128)(2,1)S(1)} %get-tuple-element.51), channel_id=1, source_target_pairs={{16,32},{17,33},{18,34},{19,35},{20,36},{21,37},{22,38},{23,39},{2... | collective-permute-start | bytes 393224 | tf_op jit(solution)/shard_map/ppermute | solution.py:323
  86.3 13.0 %collective-permute-start.11 = (bf16[256,128]{1,0:T(8,128)(2,1)S(1)}, bf16[256,128]{1,0:T(8,128)(2,1)S(1)}, u32[]{:S(2)}, u32[]{:S(2)}) collective-permute-start(bf16[256,128]{1,0:T(8,128)(2,1)S(1)} %slice.29), channel_id=1, source_target_pairs={{1,4},{3,6},{5,8},{7,10},{9,12},{11,14},{13,16},{15,18},{17,20},{1... | collective-permute-start | bytes 196616 | tf_op jit(solution)/shard_map/ppermute | solution.py:291
  90.0 9.3 %collective-permute-start.12 = (bf16[256,128]{1,0:T(8,128)(2,1)S(1)}, bf16[256,128]{1,0:T(8,128)(2,1)S(1)}, u32[]{:S(2)}, u32[]{:S(2)}) collective-permute-start(bf16[256,128]{1,0:T(8,128)(2,1)S(1)} %slice.29), channel_id=1, source_target_pairs={{0,16},{1,17},{2,18},{3,19},{4,20},{5,21},{6,22},{7,23},{8,24},{9,... | collective-permute-start | bytes 196616 | tf_op jit(solution)/shard_map/ppermute | solution.py:291

commit v7 on v6

--- a/solution.py
+++ b/solution.py
@@ -133,22 +133,21 @@
     )(in_hbm(right_side), in_hbm(carry_in), in_hbm(inverse_diag))
 
 
-def pair_kernel(tick, both, right, inverse, given, *refs):
-    far = refs[:-2]
-    solved, outgoing = refs[-2:]
+def pair_kernel(tick, both, right, inverse, given, solved, outgoing):
     block, columns = solved.shape
     odd = lax.rem(lax.axis_index("blk"), 2)
-    mine = odd * (2 * block)
-    theirs = (1 - odd) * (2 * block)
+    rows = both.shape[0] // 2
+    mine = odd * rows
+    theirs = (1 - odd) * rows
 
     def part(at):
         return both[pl.ds(pl.multiple_of(at, block), block), :].astype(F32)
 
     incoming = part(mine) + part(theirs + block)
     other = part(mine + block) + part(theirs)
-    for ref in far:
-        incoming += ref[0:block].astype(F32)
-        other += ref[block:].astype(F32)
+    for i in range(2 * block, rows, 2 * block):
+        incoming += part(mine + i) + part(theirs + i + block)
+        other += part(mine + i + block) + part(theirs + i)
     value = mm(inverse[...], (right[tick - 1] - incoming).astype(BF16))
     solved[...] = value
     outgoing[0:block] = value.astype(BF16)
@@ -158,9 +157,9 @@
     outgoing[block:] = value.astype(BF16)
 
 
-def pair_solve(tick, both, right, inverse, given, far):
+def pair_solve(tick, both, right, inverse, given):
     block, columns = right.shape[1:]
-    operands = [both, right, inverse, given] + ([] if far is None else [far])
+    operands = [both, right, inverse, given]
     return pl.pallas_call(
         functools.partial(pair_kernel, tick),
         out_shape=(
@@ -188,10 +187,12 @@
     value += mm(kept[2], odd_one)
     value += mm(kept[0], third[...])
     if opposite is not None:
-        value += mm(kept[4], opposite[...])
+        value += mm(kept[4], opposite[0:block])
     other = mm(given[0:block, :], same_one)
     other += mm(given[block : 2 * block, :], odd_one)
     other += mm(given[2 * block : 3 * block, :], self_one)
+    if opposite is not None:
+        other += mm(given[3 * block : 4 * block, :], opposite[block:])
     return value, other
 
 
@@ -293,37 +294,37 @@
     solved, own, inverse, right = first_solve(right_side, carry_in, inverse_diag)
     finished = [solved]
     far_sums = None
-    forward = [(g * around + (b + chips) % around, (g + 1) * around + b) for g in range(groups - 1) for b in range(around)]
+    seconds = range(1, around, 2)
+    opposite_of = [(b, (b + chips) % around) for b in seconds]
+    forward = [(g * around + a, (g + 1) * around + b) for g in range(groups - 1) for a, b in opposite_of]
     for tick in range(ticks):
         last = tick + 1 == ticks
         near_form = tick == 0 or last
-        mine = own[0:block]
-        third = swapped(mine, third_pairs)
-        opposite = swapped(mine, opposite_pairs) if near_form else None
+        third = swapped(own[0:block], third_pairs)
         if tick == 0:
             chip = paired(own, chip_pairs)
             own = jnp.where(odd == 0, chip, jnp.roll(chip, block, 0))
-            held = (own, third, opposite, sources, counts, factor_blocks, inverse, right)
-            own, third, opposite, *held = lax.optimization_barrier(held)
+            held = lax.optimization_barrier((own, sources, counts, factor_blocks, inverse, right))[1:]
             kept, handed = combine(around, *held)
             given = swapped(handed, chip_pairs)
+        opposite = lax.ppermute(own, "blk", opposite_of) if near_form else None
         beside = paired(own, next_pairs)
         operands = [kept, given, own, beside, third]
         if last:
             exact, crossing, outputs = last_sums(operands + [opposite], finished)
             carry = carry_sum(exact, paired(crossing, chip_pairs))
             return (outputs, carry)
-        far = None
         if near_form:
             (sums,) = partial_sums(partial_kernel, operands + [opposite], 1)
             own_far, pair_far = lax.optimization_barrier((sums, kept[4], given[3 * block : 4 * block]))[1:]
-            far_sums = swapped(jnp.concatenate([own_far, pair_far], 0), opposite_pairs)
+            far_sums = lax.ppermute(jnp.concatenate([own_far, pair_far], 0), "blk", opposite_of)
         else:
             sums, leaving = partial_sums(far_kernel, operands + [far_sums], 2)
             far = lax.ppermute(leaving, ("grp", "blk"), forward)
-        moved = lax.ppermute(sums, "grp", [(g, g + 1) for g in range(groups - 1)])
-        both = paired(moved, chip_pairs)
-        solved, own = pair_solve(tick + 1, both, right, inverse, given, far)
+        sums = lax.ppermute(sums, "grp", [(g, g + 1) for g in range(groups - 1)])
+        if not near_form:
+            sums = jnp.concatenate([sums, far], 0)
+        solved, own = pair_solve(tick + 1, paired(sums, chip_pairs), right, inverse, given)
         finished.append(solved)
 
 

time: 107 us -> 107 us (level)
  the two profiles are of different devices: /device:TPU:97 before, /device:TPU:65 now
where the time goes in v7:
time: 107 us
  blocking collectives  49.2 us (46%)
  starting transfers between devices  43.6 us (41%)
  Pallas kernels  6.49 us (6%)
  waiting for transfers between devices  5.85 us (5%)
  between operations  1.55 us (1%)
    all_gather x9, blocking collectives, paired(): lax.all_gather(value, 'blk', axis=0, tiled=True, axis_index_groups=pairs)  49.2 us
    ppermute x3, starting transfers between devices, shards(): sums = lax.ppermute(sums, 'grp', [(g, g + 1) for g in range(groups - 1)])  12.7 us
    ppermute x5, starting transfers between devices, swapped(): return lax.ppermute(value, 'blk', partner)  12.2 us
    ppermute x2, starting transfers between devices, shards(): far = lax.ppermute(leaving, ('grp', 'blk'), forward)  8.24 us
    ppermute x2, starting transfers between devices, shards(): opposite = lax.ppermute(own, 'blk', opposite_of) if near_form else None  7.27 us
    ppermute x2, waiting for transfers between devices, shards(): far = lax.ppermute(leaving, ('grp', 'blk'), forward)  3.42 us
    ppermute x1, starting transfers between devices, shards(): lax.ppermute(jnp.concatenate([own_far, pair_far], 0), 'blk', opposite_of)  3.28 us
  transfers between devices with their start and end apart: 13, of which 3 were waited for; matrix products, arithmetic and copies ran while one was open for 0% of the time, Pallas kernels for 0%

profile of v7, /device:TPU:65, one launch (start us, length us, event | category | flops | bytes accessed | tf_op | source)
XLA Modules:
  0.0 106.8 jit_solution(3492146804962510459)
XLA Ops:
  0.6 1.2 %first.1 = (f32[256,128]{1,0:T(8,128)S(1)}, bf16[256,128]{1,0:T(8,128)(2,1)S(1)}, bf16[256,256]{1,0:T(8,128)(2,1)S(1)}, f32[3,256,128]{2,1,0:T(8,128)S(1)}) custom-call(f32[4,256,128]{2,1,0:T(8,128)} %right.1, f32[256,128]{1,0:T(8,128)} %incoming.1, bf16[256,256]{1,0:T(8,128)(2,1)} %inverse.1), custom_call_target="tpu_custom_call" | custom-call | tf_op jit(solution)/shard_map/first/pallas_call | solution.py:116
  1.9 2.2 %all_gather.27 = bf16[512,128]{1,0:T(8,128)(2,1)S(1)} all-gather(bf16[256,128]{1,0:T(8,128)(2,1)S(1)} %get-tuple-element.28), channel_id=1, replica_groups={{0,1},{2,3},{4,5},{6,7},{8,9},{10,11},{12,13},{14,15},{16,17},{18,19},{..., dimensions={0}, use_global_device_ids=true | all-gather | bytes 196608 | tf_op jit(solution)/shard_map/all_gather | solution.py:288
  4.8 1.3 %combine.1 = (bf16[5,256,256]{2,1,0:T(8,128)(2,1)S(1)}, bf16[2048,256]{1,0:T(8,128)(2,1)S(1)}) custom-call(s32[1]{0:T(128)S(6)} %copy.8.count, s32[1,24]{1,0:T(1,128)} %source_list, bf16[1,24,256,256]{3,2,1,0:T(8,128)(2,1)} %blocks, bf16[256,256]{1,0:T(8,128)(2,1)S(1)} %get-tuple-element.34.inverse, f32[3,256,128]{2,1,0:T(8,128)S(1)} %get-tuple-element.35.right), custom_call_target="tpu_custom_call" | custom-call | flops 4000000 | bytes 10000000 | tf_op jit(solution)/shard_map/combine/pallas_call | solution.py:76
  6.2 2.8 %collective-permute-start = (bf16[2048,256]{1,0:T(8,128)(2,1)S(1)}, bf16[2048,256]{1,0:T(8,128)(2,1)S(1)}, u32[]{:S(2)}, u32[]{:S(2)}) collective-permute-start(bf16[2048,256]{1,0:T(8,128)(2,1)S(1)} %get-tuple-element.37), channel_id=1, source_target_pairs={{0,1},{2,3},{4,5},{6,7},{8,9},{10,11},{12,13},{14,15},{16,17},{18,... | collective-permute-start | bytes 3145736 | tf_op jit(solution)/shard_map/ppermute | solution.py:292
  9.0 4.9 %collective-permute-start.2 = (bf16[512,128]{1,0:T(8,128)(2,1)S(1)}, bf16[512,128]{1,0:T(8,128)(2,1)S(1)}, u32[]{:S(2)}, u32[]{:S(2)}) collective-permute-start(bf16[512,128]{1,0:T(8,128)(2,1)S(1)} %maximum_select_fusion.own), channel_id=1, source_target_pairs={{1,17},{3,19},{5,21},{7,23},{9,25},{11,27},{13,29},{15,31},{17,1},... | collective-permute-start | bytes 393224 | tf_op jit(solution)/shard_map/ppermute | solution.py:310
  14.0 1.9 %collective-permute-start.1 = (bf16[256,128]{1,0:T(8,128)(2,1)S(1)}, bf16[256,128]{1,0:T(8,128)(2,1)S(1)}, u32[]{:S(2)}, u32[]{:S(2)}) collective-permute-start(bf16[256,128]{1,0:T(8,128)(2,1)S(1)} %get-tuple-element.28), channel_id=1, source_target_pairs={{1,4},{3,6},{5,8},{7,10},{9,12},{11,14},{13,16},{15,18},{17,20},{1... | collective-permute-start | bytes 196616 | tf_op jit(solution)/shard_map/ppermute | solution.py:292
  15.9 6.8 %all_gather.28.beside = bf16[1024,128]{1,0:T(8,128)(2,1)S(1)} all-gather(bf16[512,128]{1,0:T(8,128)(2,1)S(1)} %maximum_select_fusion.own), channel_id=1, replica_groups={{1,2},{3,4},{5,6},{7,8},{9,10},{11,12},{13,14},{15,16},{17,18},{19,20},..., dimensions={0}, use_global_device_ids=true | all-gather | bytes 393216 | tf_op jit(solution)/shard_map/all_gather | solution.py:288
  22.7 0.5 partial.3
  23.2 3.5 %collective-permute-start.3 = (bf16[512,128]{1,0:T(8,128)(2,1)S(1)}, bf16[512,128]{1,0:T(8,128)(2,1)S(1)}, u32[]{:S(2)}, u32[]{:S(2)}) collective-permute-start(bf16[512,128]{1,0:T(8,128)(2,1)S(1)} %partial.3), channel_id=1, source_target_pairs={{0,32},{32,64},{64,96},{96,128},{128,160},{160,192},{192,224},{224... | collective-permute-start | bytes 393224 | tf_op jit(solution)/shard_map/ppermute | solution.py:324
  26.7 3.3 %collective-permute-start.5 = (bf16[512,256]{1,0:T(8,128)(2,1)S(1)}, bf16[512,256]{1,0:T(8,128)(2,1)S(1)}, u32[]{:S(2)}, u32[]{:S(2)}) collective-permute-start(bf16[512,256]{1,0:T(8,128)(2,1)S(1)} %pad_maximum_fusion), channel_id=1, source_target_pairs={{1,17},{3,19},{5,21},{7,23},{9,25},{11,27},{13,29},{15,31},{17,1},... | collective-permute-start | bytes 786440 | tf_op jit(solution)/shard_map/ppermute | solution.py:320
  30.0 6.8 %all_gather.29.both = bf16[1024,128]{1,0:T(8,128)(2,1)S(1)} all-gather(bf16[512,128]{1,0:T(8,128)(2,1)S(1)} %collective-permute-done.3), channel_id=1, replica_groups={{0,1},{2,3},{4,5},{6,7},{8,9},{10,11},{12,13},{14,15},{16,17},{18,19},{..., dimensions={0}, use_global_device_ids=true | all-gather | bytes 393216 | tf_op jit(solution)/shard_map/all_gather | solution.py:288
  37.0 1.9 %collective-permute-start.4 = (bf16[256,128]{1,0:T(8,128)(2,1)S(1)}, bf16[256,128]{1,0:T(8,128)(2,1)S(1)}, u32[]{:S(2)}, u32[]{:S(2)}) collective-permute-start(bf16[256,128]{1,0:T(8,128)(2,1)S(1)} %slice.25), channel_id=1, source_target_pairs={{1,4},{3,6},{5,8},{7,10},{9,12},{11,14},{13,16},{15,18},{17,20},{1... | collective-permute-start | bytes 196616 | tf_op jit(solution)/shard_map/ppermute | solution.py:292
  38.9 5.4 %all_gather.30.beside = bf16[1024,128]{1,0:T(8,128)(2,1)S(1)} all-gather(bf16[512,128]{1,0:T(8,128)(2,1)S(1)} %get-tuple-element.38.own), channel_id=1, replica_groups={{1,2},{3,4},{5,6},{7,8},{9,10},{11,12},{13,14},{15,16},{17,18},{19,20},..., dimensions={0}, use_global_device_ids=true | all-gather | bytes 393216 | tf_op jit(solution)/shard_map/all_gather | solution.py:288
  44.3 0.5 collective-permute-done.4.third
  44.8 0.5 partial.4
  45.2 4.4 %collective-permute-start.6 = (bf16[512,128]{1,0:T(8,128)(2,1)S(1)}, bf16[512,128]{1,0:T(8,128)(2,1)S(1)}, u32[]{:S(2)}, u32[]{:S(2)}) collective-permute-start(bf16[512,128]{1,0:T(8,128)(2,1)S(1)} %get-tuple-element.41), channel_id=1, source_target_pairs={{0,32},{32,64},{64,96},{96,128},{128,160},{160,192},{192,224},{224... | collective-permute-start | bytes 393224 | tf_op jit(solution)/shard_map/ppermute | solution.py:324
  49.6 4.7 %collective-permute-start.7 = (bf16[512,128]{1,0:T(8,128)(2,1)S(1)}, bf16[512,128]{1,0:T(8,128)(2,1)S(1)}, u32[]{:S(2)}, u32[]{:S(2)}) collective-permute-start(bf16[512,128]{1,0:T(8,128)(2,1)S(1)} %get-tuple-element.42), channel_id=1, source_target_pairs={{1,49},{3,51},{5,53},{7,55},{9,57},{11,59},{13,61},{15,63},{17,33}... | collective-permute-start | bytes 393224 | tf_op jit(solution)/shard_map/ppermute | solution.py:323
  54.3 3.4 %collective-permute-done.7 = bf16[512,128]{1,0:T(8,128)(2,1)S(1)} collective-permute-done((bf16[512,128]{1,0:T(8,128)(2,1)S(1)}, bf16[512,128]{1,0:T(8,128)(2,1)S(1)}, u32[]{:S(2)}, u32[]{:S(2)}) %collective-permute-start.7) | collective-permute-done | bytes 131104 | tf_op jit(solution)/shard_map/ppermute | solution.py:323
  57.8 2.2 %all_gather.31.both = bf16[2048,128]{1,0:T(8,128)(2,1)S(1)} all-gather(bf16[1024,128]{1,0:T(8,128)(2,1)S(1)} %pad_maximum_fusion.1), channel_id=1, replica_groups={{0,1},{2,3},{4,5},{6,7},{8,9},{10,11},{12,13},{14,15},{16,17},{18,19},{..., dimensions={0}, use_global_device_ids=true | all-gather | bytes 786432 | tf_op jit(solution)/shard_map/all_gather | solution.py:288
  60.3 3.6 %collective-permute-start.8 = (bf16[256,128]{1,0:T(8,128)(2,1)S(1)}, bf16[256,128]{1,0:T(8,128)(2,1)S(1)}, u32[]{:S(2)}, u32[]{:S(2)}) collective-permute-start(bf16[256,128]{1,0:T(8,128)(2,1)S(1)} %slice.28), channel_id=1, source_target_pairs={{1,4},{3,6},{5,8},{7,10},{9,12},{11,14},{13,16},{15,18},{17,20},{1... | collective-permute-start | bytes 196616 | tf_op jit(solution)/shard_map/ppermute | solution.py:292
  63.8 7.0 %all_gather.32.beside = bf16[1024,128]{1,0:T(8,128)(2,1)S(1)} all-gather(bf16[512,128]{1,0:T(8,128)(2,1)S(1)} %get-tuple-element.43.own), channel_id=1, replica_groups={{1,2},{3,4},{5,6},{7,8},{9,10},{11,12},{13,14},{15,16},{17,18},{19,20},..., dimensions={0}, use_global_device_ids=true | all-gather | bytes 393216 | tf_op jit(solution)/shard_map/all_gather | solution.py:288
  70.8 0.5 partial.5
  71.3 3.6 %collective-permute-start.10 = (bf16[512,128]{1,0:T(8,128)(2,1)S(1)}, bf16[512,128]{1,0:T(8,128)(2,1)S(1)}, u32[]{:S(2)}, u32[]{:S(2)}) collective-permute-start(bf16[512,128]{1,0:T(8,128)(2,1)S(1)} %get-tuple-element.45), channel_id=1, source_target_pairs={{1,49},{3,51},{5,53},{7,55},{9,57},{11,59},{13,61},{15,63},{17,33}... | collective-permute-start | bytes 393224 | tf_op jit(solution)/shard_map/ppermute | solution.py:323
  74.9 4.8 %collective-permute-start.9 = (bf16[512,128]{1,0:T(8,128)(2,1)S(1)}, bf16[512,128]{1,0:T(8,128)(2,1)S(1)}, u32[]{:S(2)}, u32[]{:S(2)}) collective-permute-start(bf16[512,128]{1,0:T(8,128)(2,1)S(1)} %get-tuple-element.44), channel_id=1, source_target_pairs={{0,32},{32,64},{64,96},{96,128},{128,160},{160,192},{192,224},{224... | collective-permute-start | bytes 393224 | tf_op jit(solution)/shard_map/ppermute | solution.py:324
  79.7 1.9 %collective-permute-done.9 = bf16[512,128]{1,0:T(8,128)(2,1)S(1)} collective-permute-done((bf16[512,128]{1,0:T(8,128)(2,1)S(1)}, bf16[512,128]{1,0:T(8,128)(2,1)S(1)}, u32[]{:S(2)}, u32[]{:S(2)}) %collective-permute-start.9) | collective-permute-done | bytes 131104 | tf_op jit(solution)/shard_map/ppermute | solution.py:324
  81.6 5.1 %all_gather.33.both = bf16[2048,128]{1,0:T(8,128)(2,1)S(1)} all-gather(bf16[1024,128]{1,0:T(8,128)(2,1)S(1)} %pad_maximum_fusion.2), channel_id=1, replica_groups={{0,1},{2,3},{4,5},{6,7},{8,9},{10,11},{12,13},{14,15},{16,17},{18,19},{..., dimensions={0}, use_global_device_ids=true | all-gather | bytes 786432 | tf_op jit(solution)/shard_map/all_gather | solution.py:288
  87.1 2.3 %collective-permute-start.12 = (bf16[512,128]{1,0:T(8,128)(2,1)S(1)}, bf16[512,128]{1,0:T(8,128)(2,1)S(1)}, u32[]{:S(2)}, u32[]{:S(2)}) collective-permute-start(bf16[512,128]{1,0:T(8,128)(2,1)S(1)} %get-tuple-element.46.own), channel_id=1, source_target_pairs={{1,17},{3,19},{5,21},{7,23},{9,25},{11,27},{13,29},{15,31},{17,1},... | collective-permute-start | bytes 393224 | tf_op jit(solution)/shard_map/ppermute | solution.py:310
  89.4 1.9 %collective-permute-start.11 = (bf16[256,128]{1,0:T(8,128)(2,1)S(1)}, bf16[256,128]{1,0:T(8,128)(2,1)S(1)}, u32[]{:S(2)}, u32[]{:S(2)}) collective-permute-start(bf16[256,128]{1,0:T(8,128)(2,1)S(1)} %slice.29), channel_id=1, source_target_pairs={{1,4},{3,6},{5,8},{7,10},{9,12},{11,14},{13,16},{15,18},{17,20},{1... | collective-permute-start | bytes 196616 | tf_op jit(solution)/shard_map/ppermute | solution.py:292
  91.3 9.3 %all_gather.34.beside = bf16[1024,128]{1,0:T(8,128)(2,1)S(1)} all-gather(bf16[512,128]{1,0:T(8,128)(2,1)S(1)} %get-tuple-element.46.own), channel_id=1, replica_groups={{1,2},{3,4},{5,6},{7,8},{9,10},{11,12},{13,14},{15,16},{17,18},{19,20},..., dimensions={0}, use_global_device_ids=true | all-gather | bytes 393216 | tf_op jit(solution)/shard_map/all_gather | solution.py:288
  100.7 1.0 last.1
  101.7 4.4 %all_gather.35.both = bf16[512,128]{1,0:T(8,128)(2,1)S(1)} all-gather(bf16[256,128]{1,0:T(8,128)(2,1)S(1)} %get-tuple-element.53), channel_id=1, replica_groups={{0,1},{2,3},{4,5},{6,7},{8,9},{10,11},{12,13},{14,15},{16,17},{18,19},{..., dimensions={0}, use_global_device_ids=true | all-gather | bytes 196608 | tf_op jit(solution)/shard_map/all_gather | solution.py:288
  106.1 0.7 carry.1
  (23 shorter events, 1.0 us)
Async XLA Ops:
  6.2 16.5 %collective-permute-start = (bf16[2048,256]{1,0:T(8,128)(2,1)S(1)}, bf16[2048,256]{1,0:T(8,128)(2,1)S(1)}, u32[]{:S(2)}, u32[]{:S(2)}) collective-permute-start(bf16[2048,256]{1,0:T(8,128)(2,1)S(1)} %get-tuple-element.37), channel_id=1, source_target_pairs={{0,1},{2,3},{4,5},{6,7},{8,9},{10,11},{12,13},{14,15},{16,17},{18,... | collective-permute-start | bytes 3145736 | tf_op jit(solution)/shard_map/ppermute | solution.py:292
  9.0 13.7 %collective-permute-start.2 = (bf16[512,128]{1,0:T(8,128)(2,1)S(1)}, bf16[512,128]{1,0:T(8,128)(2,1)S(1)}, u32[]{:S(2)}, u32[]{:S(2)}) collective-permute-start(bf16[512,128]{1,0:T(8,128)(2,1)S(1)} %maximum_select_fusion.own), channel_id=1, source_target_pairs={{1,17},{3,19},{5,21},{7,23},{9,25},{11,27},{13,29},{15,31},{17,1},... | collective-permute-start | bytes 393224 | tf_op jit(solution)/shard_map/ppermute | solution.py:310
  14.0 8.7 %collective-permute-start.1 = (bf16[256,128]{1,0:T(8,128)(2,1)S(1)}, bf16[256,128]{1,0:T(8,128)(2,1)S(1)}, u32[]{:S(2)}, u32[]{:S(2)}) collective-permute-start(bf16[256,128]{1,0:T(8,128)(2,1)S(1)} %get-tuple-element.28), channel_id=1, source_target_pairs={{1,4},{3,6},{5,8},{7,10},{9,12},{11,14},{13,16},{15,18},{17,20},{1... | collective-permute-start | bytes 196616 | tf_op jit(solution)/shard_map/ppermute | solution.py:292
  23.2 6.8 %collective-permute-start.3 = (bf16[512,128]{1,0:T(8,128)(2,1)S(1)}, bf16[512,128]{1,0:T(8,128)(2,1)S(1)}, u32[]{:S(2)}, u32[]{:S(2)}) collective-permute-start(bf16[512,128]{1,0:T(8,128)(2,1)S(1)} %partial.3), channel_id=1, source_target_pairs={{0,32},{32,64},{64,96},{96,128},{128,160},{160,192},{192,224},{224... | collective-permute-start | bytes 393224 | tf_op jit(solution)/shard_map/ppermute | solution.py:324
  26.7 18.1 %collective-permute-start.5 = (bf16[512,256]{1,0:T(8,128)(2,1)S(1)}, bf16[512,256]{1,0:T(8,128)(2,1)S(1)}, u32[]{:S(2)}, u32[]{:S(2)}) collective-permute-start(bf16[512,256]{1,0:T(8,128)(2,1)S(1)} %pad_maximum_fusion), channel_id=1, source_target_pairs={{1,17},{3,19},{5,21},{7,23},{9,25},{11,27},{13,29},{15,31},{17,1},... | collective-permute-start | bytes 786440 | tf_op jit(solution)/shard_map/ppermute | solution.py:320
  37.0 7.8 %collective-permute-start.4 = (bf16[256,128]{1,0:T(8,128)(2,1)S(1)}, bf16[256,128]{1,0:T(8,128)(2,1)S(1)}, u32[]{:S(2)}, u32[]{:S(2)}) collective-permute-start(bf16[256,128]{1,0:T(8,128)(2,1)S(1)} %slice.25), channel_id=1, source_target_pairs={{1,4},{3,6},{5,8},{7,10},{9,12},{11,14},{13,16},{15,18},{17,20},{1... | collective-permute-start | bytes 196616 | tf_op jit(solution)/shard_map/ppermute | solution.py:292
  45.2 9.1 %collective-permute-start.6 = (bf16[512,128]{1,0:T(8,128)(2,1)S(1)}, bf16[512,128]{1,0:T(8,128)(2,1)S(1)}, u32[]{:S(2)}, u32[]{:S(2)}) collective-permute-start(bf16[512,128]{1,0:T(8,128)(2,1)S(1)} %get-tuple-element.41), channel_id=1, source_target_pairs={{0,32},{32,64},{64,96},{96,128},{128,160},{160,192},{192,224},{224... | collective-permute-start | bytes 393224 | tf_op jit(solution)/shard_map/ppermute | solution.py:324
  49.6 8.1 %collective-permute-start.7 = (bf16[512,128]{1,0:T(8,128)(2,1)S(1)}, bf16[512,128]{1,0:T(8,128)(2,1)S(1)}, u32[]{:S(2)}, u32[]{:S(2)}) collective-permute-start(bf16[512,128]{1,0:T(8,128)(2,1)S(1)} %get-tuple-element.42), channel_id=1, source_target_pairs={{1,49},{3,51},{5,53},{7,55},{9,57},{11,59},{13,61},{15,63},{17,33}... | collective-permute-start | bytes 393224 | tf_op jit(solution)/shard_map/ppermute | solution.py:323
  60.3 10.5 %collective-permute-start.8 = (bf16[256,128]{1,0:T(8,128)(2,1)S(1)}, bf16[256,128]{1,0:T(8,128)(2,1)S(1)}, u32[]{:S(2)}, u32[]{:S(2)}) collective-permute-start(bf16[256,128]{1,0:T(8,128)(2,1)S(1)} %slice.28), channel_id=1, source_target_pairs={{1,4},{3,6},{5,8},{7,10},{9,12},{11,14},{13,16},{15,18},{17,20},{1... | collective-permute-start | bytes 196616 | tf_op jit(solution)/shard_map/ppermute | solution.py:292
  71.3 8.4 %collective-permute-start.10 = (bf16[512,128]{1,0:T(8,128)(2,1)S(1)}, bf16[512,128]{1,0:T(8,128)(2,1)S(1)}, u32[]{:S(2)}, u32[]{:S(2)}) collective-permute-start(bf16[512,128]{1,0:T(8,128)(2,1)S(1)} %get-tuple-element.45), channel_id=1, source_target_pairs={{1,49},{3,51},{5,53},{7,55},{9,57},{11,59},{13,61},{15,63},{17,33}... | collective-permute-start | bytes 393224 | tf_op jit(solution)/shard_map/ppermute | solution.py:323
  74.9 6.8 %collective-permute-start.9 = (bf16[512,128]{1,0:T(8,128)(2,1)S(1)}, bf16[512,128]{1,0:T(8,128)(2,1)S(1)}, u32[]{:S(2)}, u32[]{:S(2)}) collective-permute-start(bf16[512,128]{1,0:T(8,128)(2,1)S(1)} %get-tuple-element.44), channel_id=1, source_target_pairs={{0,32},{32,64},{64,96},{96,128},{128,160},{160,192},{192,224},{224... | collective-permute-start | bytes 393224 | tf_op jit(solution)/shard_map/ppermute | solution.py:324
  87.1 13.6 %collective-permute-start.12 = (bf16[512,128]{1,0:T(8,128)(2,1)S(1)}, bf16[512,128]{1,0:T(8,128)(2,1)S(1)}, u32[]{:S(2)}, u32[]{:S(2)}) collective-permute-start(bf16[512,128]{1,0:T(8,128)(2,1)S(1)} %get-tuple-element.46.own), channel_id=1, source_target_pairs={{1,17},{3,19},{5,21},{7,23},{9,25},{11,27},{13,29},{15,31},{17,1},... | collective-permute-start | bytes 393224 | tf_op jit(solution)/shard_map/ppermute | solution.py:310
  89.4 11.3 %collective-permute-start.11 = (bf16[256,128]{1,0:T(8,128)(2,1)S(1)}, bf16[256,128]{1,0:T(8,128)(2,1)S(1)}, u32[]{:S(2)}, u32[]{:S(2)}) collective-permute-start(bf16[256,128]{1,0:T(8,128)(2,1)S(1)} %slice.29), channel_id=1, source_target_pairs={{1,4},{3,6},{5,8},{7,10},{9,12},{11,14},{13,16},{15,18},{17,20},{1... | collective-permute-start | bytes 196616 | tf_op jit(solution)/shard_map/ppermute | solution.py:292

commit v8 on v6

--- a/solution.py
+++ b/solution.py
@@ -134,8 +134,8 @@
 
 
 def pair_kernel(tick, both, right, inverse, given, *refs):
-    far = refs[:-2]
-    solved, outgoing = refs[-2:]
+    far = refs[:-3]
+    solved, outgoing, alone = refs[-3:]
     block, columns = solved.shape
     odd = lax.rem(lax.axis_index("blk"), 2)
     mine = odd * (2 * block)
@@ -152,6 +152,7 @@
     value = mm(inverse[...], (right[tick - 1] - incoming).astype(BF16))
     solved[...] = value
     outgoing[0:block] = value.astype(BF16)
+    alone[...] = value.astype(BF16)
     rows = pl.ds((4 + tick) * block, block)
     other_right = given[rows, 0:columns].astype(F32) + given[rows, columns:].astype(F32)
     value = mm(given[4 * block : 5 * block, :], (other_right - other).astype(BF16))
@@ -166,9 +167,10 @@
         out_shape=(
             jax.ShapeDtypeStruct((block, columns), F32),
             jax.ShapeDtypeStruct((2 * block, columns), BF16),
+            jax.ShapeDtypeStruct((block, columns), BF16),
         ),
         in_specs=[VMEM] * len(operands),
-        out_specs=(VMEM, VMEM),
+        out_specs=(VMEM, VMEM, VMEM),
         compiler_params=params(),
         name="solve",
     )(*operands)
@@ -188,10 +190,12 @@
     value += mm(kept[2], odd_one)
     value += mm(kept[0], third[...])
     if opposite is not None:
-        value += mm(kept[4], opposite[...])
+        value += mm(kept[4], opposite[0:block])
     other = mm(given[0:block, :], same_one)
     other += mm(given[block : 2 * block, :], odd_one)
     other += mm(given[2 * block : 3 * block, :], self_one)
+    if opposite is not None:
+        other += mm(given[3 * block : 4 * block, :], opposite[block:])
     return value, other
 
 
@@ -293,20 +297,23 @@
     solved, own, inverse, right = first_solve(right_side, carry_in, inverse_diag)
     finished = [solved]
     far_sums = None
+    seconds = [(b, (b + chips) % around) for b in range(1, around, 2)]
     forward = [(g * around + (b + chips) % around, (g + 1) * around + b) for g in range(groups - 1) for b in range(around)]
+    mine = own
     for tick in range(ticks):
         last = tick + 1 == ticks
         near_form = tick == 0 or last
-        mine = own[0:block]
-        third = swapped(mine, third_pairs)
-        opposite = swapped(mine, opposite_pairs) if near_form else None
+        third = swapped(own if last else mine, third_pairs)[0:block]
         if tick == 0:
-            chip = paired(own, chip_pairs)
+            chip = paired(mine, chip_pairs)
             own = jnp.where(odd == 0, chip, jnp.roll(chip, block, 0))
-            held = (own, third, opposite, sources, counts, factor_blocks, inverse, right)
-            own, third, opposite, *held = lax.optimization_barrier(held)
+            held = lax.optimization_barrier((own, sources, counts, factor_blocks, inverse, right))[1:]
             kept, handed = combine(around, *held)
             given = swapped(handed, chip_pairs)
+        opposite = None
+        if near_form:
+            turned = jnp.where(odd == 1, own, jnp.zeros_like(own)) if tick == 0 else own
+            opposite = lax.ppermute(turned, "blk", seconds)
         beside = paired(own, next_pairs)
         operands = [kept, given, own, beside, third]
         if last:
@@ -323,7 +330,7 @@
             far = lax.ppermute(leaving, ("grp", "blk"), forward)
         moved = lax.ppermute(sums, "grp", [(g, g + 1) for g in range(groups - 1)])
         both = paired(moved, chip_pairs)
-        solved, own = pair_solve(tick + 1, both, right, inverse, given, far)
+        solved, own, mine = pair_solve(tick + 1, both, right, inverse, given, far)
         finished.append(solved)
 
 

time: 107 us -> 104 us (0.972)
  starting transfers between devices: 53.3 us -> 47.9 us
    ppermute x8 -> x6, starting transfers between devices: 32.3 us -> 18.4 us  [swapped(): return lax.ppermute(value, 'blk', partner)]
    ppermute x0 -> x2, starting transfers between devices: none -> 9.47 us  [shards(): opposite = lax.ppermute(turned, 'blk', seconds)]
    ppermute x2, waiting for transfers between devices: 0.01 us -> 1.27 us  [shards(): far = lax.ppermute(leaving, ('grp', 'blk'), forward)]
where the time goes in v8:
time: 104 us; the launch traced here: 103 us
  starting transfers between devices  47.9 us (46%)
  blocking collectives  44.9 us (43%)
  Pallas kernels  7.29 us (7%)
  between operations  1.53 us (1%)
  waiting for transfers between devices  1.3 us (1%)
    all_gather x9, blocking collectives, paired(): lax.all_gather(value, 'blk', axis=0, tiled=True, axis_index_groups=pairs)  44.9 us
    ppermute x6, starting transfers between devices, swapped(): return lax.ppermute(value, 'blk', partner)  18.4 us
    ppermute x3, starting transfers between devices, shards(): moved = lax.ppermute(sums, 'grp', [(g, g + 1) for g in range(groups - 1)])  13.4 us
    ppermute x2, starting transfers between devices, shards(): opposite = lax.ppermute(turned, 'blk', seconds)  9.47 us
    ppermute x2, starting transfers between devices, shards(): far = lax.ppermute(leaving, ('grp', 'blk'), forward)  6.7 us
  transfers between devices with their start and end apart: 13, of which 1 were waited for; matrix products, arithmetic and copies ran while one was open for 0% of the time, Pallas kernels for 0%

profile of v8, /device:TPU:97, one launch (start us, length us, event | category | flops | bytes accessed | tf_op | source)
XLA Modules:
  0.0 103.1 jit_solution(150396333115574588)
XLA Ops:
  0.6 1.2 %first.1 = (f32[256,128]{1,0:T(8,128)S(1)}, bf16[256,128]{1,0:T(8,128)(2,1)S(1)}, bf16[256,256]{1,0:T(8,128)(2,1)S(1)}, f32[3,256,128]{2,1,0:T(8,128)S(1)}) custom-call(f32[4,256,128]{2,1,0:T(8,128)} %right.1, f32[256,128]{1,0:T(8,128)} %incoming.1, bf16[256,256]{1,0:T(8,128)(2,1)} %inverse.1), custom_call_target="tpu_custom_call" | custom-call | tf_op jit(solution)/shard_map/first/pallas_call | solution.py:116
  1.9 2.2 %all_gather.27 = bf16[512,128]{1,0:T(8,128)(2,1)S(1)} all-gather(bf16[256,128]{1,0:T(8,128)(2,1)S(1)} %get-tuple-element.30), channel_id=1, replica_groups={{0,1},{2,3},{4,5},{6,7},{8,9},{10,11},{12,13},{14,15},{16,17},{18,19},{..., dimensions={0}, use_global_device_ids=true | all-gather | bytes 196608 | tf_op jit(solution)/shard_map/all_gather | solution.py:291
  4.8 1.5 %combine.1 = (bf16[5,256,256]{2,1,0:T(8,128)(2,1)S(1)}, bf16[2048,256]{1,0:T(8,128)(2,1)S(1)}) custom-call(s32[1]{0:T(128)S(6)} %copy.8.count, s32[1,24]{1,0:T(1,128)} %source_list, bf16[1,24,256,256]{3,2,1,0:T(8,128)(2,1)} %blocks, bf16[256,256]{1,0:T(8,128)(2,1)S(1)} %get-tuple-element.36.inverse, f32[3,256,128]{2,1,0:T(8,128)S(1)} %get-tuple-element.37.right), custom_call_target="tpu_custom_call" | custom-call | flops 4000000 | bytes 10000000 | tf_op jit(solution)/shard_map/combine/pallas_call | solution.py:76
  6.4 2.9 %collective-permute-start = (bf16[2048,256]{1,0:T(8,128)(2,1)S(1)}, bf16[2048,256]{1,0:T(8,128)(2,1)S(1)}, u32[]{:S(2)}, u32[]{:S(2)}) collective-permute-start(bf16[2048,256]{1,0:T(8,128)(2,1)S(1)} %get-tuple-element.39), channel_id=1, source_target_pairs={{0,1},{2,3},{4,5},{6,7},{8,9},{10,11},{12,13},{14,15},{16,17},{18,... | collective-permute-start | bytes 3145736 | tf_op jit(solution)/shard_map/ppermute | solution.py:295
  9.3 4.0 %collective-permute-start.1 = (bf16[256,128]{1,0:T(8,128)(2,1)S(1)}, bf16[256,128]{1,0:T(8,128)(2,1)S(1)}, u32[]{:S(2)}, u32[]{:S(2)}) collective-permute-start(bf16[256,128]{1,0:T(8,128)(2,1)S(1)} %get-tuple-element.30), channel_id=1, source_target_pairs={{1,4},{3,6},{5,8},{7,10},{9,12},{11,14},{13,16},{15,18},{17,20},{1... | collective-permute-start | bytes 196616 | tf_op jit(solution)/shard_map/ppermute | solution.py:295
  13.3 5.0 %collective-permute-start.2 = (bf16[512,128]{1,0:T(8,128)(2,1)S(1)}, bf16[512,128]{1,0:T(8,128)(2,1)S(1)}, u32[]{:S(2)}, u32[]{:S(2)}) collective-permute-start(bf16[512,128]{1,0:T(8,128)(2,1)S(1)} %get-tuple-element.58), channel_id=1, source_target_pairs={{1,17},{3,19},{5,21},{7,23},{9,25},{11,27},{13,29},{15,31},{17,1},... | collective-permute-start | bytes 393224 | tf_op jit(solution)/shard_map/ppermute | solution.py:316
  18.3 5.4 %all_gather.28.beside = bf16[1024,128]{1,0:T(8,128)(2,1)S(1)} all-gather(bf16[512,128]{1,0:T(8,128)(2,1)S(1)} %get-tuple-element.59.own), channel_id=1, replica_groups={{1,2},{3,4},{5,6},{7,8},{9,10},{11,12},{13,14},{15,16},{17,18},{19,20},..., dimensions={0}, use_global_device_ids=true | all-gather | bytes 393216 | tf_op jit(solution)/shard_map/all_gather | solution.py:291
  23.7 0.5 partial.3
  24.2 4.5 %collective-permute-start.3 = (bf16[512,128]{1,0:T(8,128)(2,1)S(1)}, bf16[512,128]{1,0:T(8,128)(2,1)S(1)}, u32[]{:S(2)}, u32[]{:S(2)}) collective-permute-start(bf16[512,128]{1,0:T(8,128)(2,1)S(1)} %partial.3), channel_id=1, source_target_pairs={{0,32},{32,64},{64,96},{96,128},{128,160},{160,192},{192,224},{224... | collective-permute-start | bytes 393224 | tf_op jit(solution)/shard_map/ppermute | solution.py:331
  28.7 2.8 %collective-permute-start.5 = (bf16[512,256]{1,0:T(8,128)(2,1)S(1)}, bf16[512,256]{1,0:T(8,128)(2,1)S(1)}, u32[]{:S(2)}, u32[]{:S(2)}) collective-permute-start(bf16[512,256]{1,0:T(8,128)(2,1)S(1)} %pad_maximum_fusion), channel_id=1, source_target_pairs={{0,16},{1,17},{2,18},{3,19},{4,20},{5,21},{6,22},{7,23},{8,24},{9,... | collective-permute-start | bytes 786440 | tf_op jit(solution)/shard_map/ppermute | solution.py:295
  31.5 3.6 %all_gather.29.both = bf16[1024,128]{1,0:T(8,128)(2,1)S(1)} all-gather(bf16[512,128]{1,0:T(8,128)(2,1)S(1)} %collective-permute-done.3), channel_id=1, replica_groups={{0,1},{2,3},{4,5},{6,7},{8,9},{10,11},{12,13},{14,15},{16,17},{18,19},{..., dimensions={0}, use_global_device_ids=true | all-gather | bytes 393216 | tf_op jit(solution)/shard_map/all_gather | solution.py:291
  35.4 1.9 %collective-permute-start.4 = (bf16[256,128]{1,0:T(8,128)(2,1)S(1)}, bf16[256,128]{1,0:T(8,128)(2,1)S(1)}, u32[]{:S(2)}, u32[]{:S(2)}) collective-permute-start(bf16[256,128]{1,0:T(8,128)(2,1)S(1)} %get-tuple-element.41), channel_id=1, source_target_pairs={{1,4},{3,6},{5,8},{7,10},{9,12},{11,14},{13,16},{15,18},{17,20},{1... | collective-permute-start | bytes 196616 | tf_op jit(solution)/shard_map/ppermute | solution.py:295
  37.4 7.7 %all_gather.30.beside = bf16[1024,128]{1,0:T(8,128)(2,1)S(1)} all-gather(bf16[512,128]{1,0:T(8,128)(2,1)S(1)} %get-tuple-element.40.own), channel_id=1, replica_groups={{1,2},{3,4},{5,6},{7,8},{9,10},{11,12},{13,14},{15,16},{17,18},{19,20},..., dimensions={0}, use_global_device_ids=true | all-gather | bytes 393216 | tf_op jit(solution)/shard_map/all_gather | solution.py:291
  45.1 0.5 partial.4
  45.6 5.2 %collective-permute-start.6 = (bf16[512,128]{1,0:T(8,128)(2,1)S(1)}, bf16[512,128]{1,0:T(8,128)(2,1)S(1)}, u32[]{:S(2)}, u32[]{:S(2)}) collective-permute-start(bf16[512,128]{1,0:T(8,128)(2,1)S(1)} %get-tuple-element.44), channel_id=1, source_target_pairs={{0,32},{32,64},{64,96},{96,128},{128,160},{160,192},{192,224},{224... | collective-permute-start | bytes 393224 | tf_op jit(solution)/shard_map/ppermute | solution.py:331
  50.8 3.8 %collective-permute-start.7 = (bf16[512,128]{1,0:T(8,128)(2,1)S(1)}, bf16[512,128]{1,0:T(8,128)(2,1)S(1)}, u32[]{:S(2)}, u32[]{:S(2)}) collective-permute-start(bf16[512,128]{1,0:T(8,128)(2,1)S(1)} %get-tuple-element.45), channel_id=1, source_target_pairs={{16,32},{17,33},{18,34},{19,35},{20,36},{21,37},{22,38},{23,39},{2... | collective-permute-start | bytes 393224 | tf_op jit(solution)/shard_map/ppermute | solution.py:330
  54.6 3.0 %all_gather.31.both = bf16[1024,128]{1,0:T(8,128)(2,1)S(1)} all-gather(bf16[512,128]{1,0:T(8,128)(2,1)S(1)} %collective-permute-done.6), channel_id=1, replica_groups={{0,1},{2,3},{4,5},{6,7},{8,9},{10,11},{12,13},{14,15},{16,17},{18,19},{..., dimensions={0}, use_global_device_ids=true | all-gather | bytes 393216 | tf_op jit(solution)/shard_map/all_gather | solution.py:291
  57.6 1.3 %collective-permute-done.7.refs_0_ = bf16[512,128]{1,0:T(8,128)(2,1)S(1)} collective-permute-done((bf16[512,128]{1,0:T(8,128)(2,1)S(1)}, bf16[512,128]{1,0:T(8,128)(2,1)S(1)}, u32[]{:S(2)}, u32[]{:S(2)}) %collective-permute-start.7) | collective-permute-done | bytes 131104 | tf_op jit(solution)/shard_map/ppermute | solution.py:330
  58.9 0.3 solve.4
  59.2 4.2 %collective-permute-start.8 = (bf16[256,128]{1,0:T(8,128)(2,1)S(1)}, bf16[256,128]{1,0:T(8,128)(2,1)S(1)}, u32[]{:S(2)}, u32[]{:S(2)}) collective-permute-start(bf16[256,128]{1,0:T(8,128)(2,1)S(1)} %get-tuple-element.47), channel_id=1, source_target_pairs={{1,4},{3,6},{5,8},{7,10},{9,12},{11,14},{13,16},{15,18},{17,20},{1... | collective-permute-start | bytes 196616 | tf_op jit(solution)/shard_map/ppermute | solution.py:295
  63.4 6.6 %all_gather.32.beside = bf16[1024,128]{1,0:T(8,128)(2,1)S(1)} all-gather(bf16[512,128]{1,0:T(8,128)(2,1)S(1)} %get-tuple-element.46.own), channel_id=1, replica_groups={{1,2},{3,4},{5,6},{7,8},{9,10},{11,12},{13,14},{15,16},{17,18},{19,20},..., dimensions={0}, use_global_device_ids=true | all-gather | bytes 393216 | tf_op jit(solution)/shard_map/all_gather | solution.py:291
  70.0 0.5 partial.5
  70.5 3.6 %collective-permute-start.9 = (bf16[512,128]{1,0:T(8,128)(2,1)S(1)}, bf16[512,128]{1,0:T(8,128)(2,1)S(1)}, u32[]{:S(2)}, u32[]{:S(2)}) collective-permute-start(bf16[512,128]{1,0:T(8,128)(2,1)S(1)} %get-tuple-element.48), channel_id=1, source_target_pairs={{0,32},{32,64},{64,96},{96,128},{128,160},{160,192},{192,224},{224... | collective-permute-start | bytes 393224 | tf_op jit(solution)/shard_map/ppermute | solution.py:331
  74.1 2.9 %collective-permute-start.10 = (bf16[512,128]{1,0:T(8,128)(2,1)S(1)}, bf16[512,128]{1,0:T(8,128)(2,1)S(1)}, u32[]{:S(2)}, u32[]{:S(2)}) collective-permute-start(bf16[512,128]{1,0:T(8,128)(2,1)S(1)} %get-tuple-element.49), channel_id=1, source_target_pairs={{16,32},{17,33},{18,34},{19,35},{20,36},{21,37},{22,38},{23,39},{2... | collective-permute-start | bytes 393224 | tf_op jit(solution)/shard_map/ppermute | solution.py:330
  77.0 7.0 %all_gather.33.both = bf16[1024,128]{1,0:T(8,128)(2,1)S(1)} all-gather(bf16[512,128]{1,0:T(8,128)(2,1)S(1)} %collective-permute-done.9), channel_id=1, replica_groups={{0,1},{2,3},{4,5},{6,7},{8,9},{10,11},{12,13},{14,15},{16,17},{18,19},{..., dimensions={0}, use_global_device_ids=true | all-gather | bytes 393216 | tf_op jit(solution)/shard_map/all_gather | solution.py:291
  84.0 0.9 solve.5
  84.9 2.6 %collective-permute-start.11 = (bf16[512,128]{1,0:T(8,128)(2,1)S(1)}, bf16[512,128]{1,0:T(8,128)(2,1)S(1)}, u32[]{:S(2)}, u32[]{:S(2)}) collective-permute-start(bf16[512,128]{1,0:T(8,128)(2,1)S(1)} %get-tuple-element.50.own), channel_id=1, source_target_pairs={{1,4},{3,6},{5,8},{7,10},{9,12},{11,14},{13,16},{15,18},{17,20},{1... | collective-permute-start | bytes 393224 | tf_op jit(solution)/shard_map/ppermute | solution.py:295
  87.4 4.5 %collective-permute-start.12 = (bf16[512,128]{1,0:T(8,128)(2,1)S(1)}, bf16[512,128]{1,0:T(8,128)(2,1)S(1)}, u32[]{:S(2)}, u32[]{:S(2)}) collective-permute-start(bf16[512,128]{1,0:T(8,128)(2,1)S(1)} %get-tuple-element.50.own), channel_id=1, source_target_pairs={{1,17},{3,19},{5,21},{7,23},{9,25},{11,27},{13,29},{15,31},{17,1},... | collective-permute-start | bytes 393224 | tf_op jit(solution)/shard_map/ppermute | solution.py:316
  91.9 5.4 %all_gather.34.beside = bf16[1024,128]{1,0:T(8,128)(2,1)S(1)} all-gather(bf16[512,128]{1,0:T(8,128)(2,1)S(1)} %get-tuple-element.50.own), channel_id=1, replica_groups={{1,2},{3,4},{5,6},{7,8},{9,10},{11,12},{13,14},{15,16},{17,18},{19,20},..., dimensions={0}, use_global_device_ids=true | all-gather | bytes 393216 | tf_op jit(solution)/shard_map/all_gather | solution.py:291
  97.3 1.0 last.1
  98.3 4.1 %all_gather.35.both = bf16[512,128]{1,0:T(8,128)(2,1)S(1)} all-gather(bf16[256,128]{1,0:T(8,128)(2,1)S(1)} %get-tuple-element.57), channel_id=1, replica_groups={{0,1},{2,3},{4,5},{6,7},{8,9},{10,11},{12,13},{14,15},{16,17},{18,19},{..., dimensions={0}, use_global_device_ids=true | all-gather | bytes 196608 | tf_op jit(solution)/shard_map/all_gather | solution.py:291
  102.4 0.7 carry.1
  (19 shorter events, 0.4 us)
Async XLA Ops:
  6.4 17.3 %collective-permute-start = (bf16[2048,256]{1,0:T(8,128)(2,1)S(1)}, bf16[2048,256]{1,0:T(8,128)(2,1)S(1)}, u32[]{:S(2)}, u32[]{:S(2)}) collective-permute-start(bf16[2048,256]{1,0:T(8,128)(2,1)S(1)} %get-tuple-element.39), channel_id=1, source_target_pairs={{0,1},{2,3},{4,5},{6,7},{8,9},{10,11},{12,13},{14,15},{16,17},{18,... | collective-permute-start | bytes 3145736 | tf_op jit(solution)/shard_map/ppermute | solution.py:295
  9.3 14.4 %collective-permute-start.1 = (bf16[256,128]{1,0:T(8,128)(2,1)S(1)}, bf16[256,128]{1,0:T(8,128)(2,1)S(1)}, u32[]{:S(2)}, u32[]{:S(2)}) collective-permute-start(bf16[256,128]{1,0:T(8,128)(2,1)S(1)} %get-tuple-element.30), channel_id=1, source_target_pairs={{1,4},{3,6},{5,8},{7,10},{9,12},{11,14},{13,16},{15,18},{17,20},{1... | collective-permute-start | bytes 196616 | tf_op jit(solution)/shard_map/ppermute | solution.py:295
  13.3 10.4 %collective-permute-start.2 = (bf16[512,128]{1,0:T(8,128)(2,1)S(1)}, bf16[512,128]{1,0:T(8,128)(2,1)S(1)}, u32[]{:S(2)}, u32[]{:S(2)}) collective-permute-start(bf16[512,128]{1,0:T(8,128)(2,1)S(1)} %get-tuple-element.58), channel_id=1, source_target_pairs={{1,17},{3,19},{5,21},{7,23},{9,25},{11,27},{13,29},{15,31},{17,1},... | collective-permute-start | bytes 393224 | tf_op jit(solution)/shard_map/ppermute | solution.py:316
  24.2 7.3 %collective-permute-start.3 = (bf16[512,128]{1,0:T(8,128)(2,1)S(1)}, bf16[512,128]{1,0:T(8,128)(2,1)S(1)}, u32[]{:S(2)}, u32[]{:S(2)}) collective-permute-start(bf16[512,128]{1,0:T(8,128)(2,1)S(1)} %partial.3), channel_id=1, source_target_pairs={{0,32},{32,64},{64,96},{96,128},{128,160},{160,192},{192,224},{224... | collective-permute-start | bytes 393224 | tf_op jit(solution)/shard_map/ppermute | solution.py:331
  28.7 16.4 %collective-permute-start.5 = (bf16[512,256]{1,0:T(8,128)(2,1)S(1)}, bf16[512,256]{1,0:T(8,128)(2,1)S(1)}, u32[]{:S(2)}, u32[]{:S(2)}) collective-permute-start(bf16[512,256]{1,0:T(8,128)(2,1)S(1)} %pad_maximum_fusion), channel_id=1, source_target_pairs={{0,16},{1,17},{2,18},{3,19},{4,20},{5,21},{6,22},{7,23},{8,24},{9,... | collective-permute-start | bytes 786440 | tf_op jit(solution)/shard_map/ppermute | solution.py:295
  35.4 9.7 %collective-permute-start.4 = (bf16[256,128]{1,0:T(8,128)(2,1)S(1)}, bf16[256,128]{1,0:T(8,128)(2,1)S(1)}, u32[]{:S(2)}, u32[]{:S(2)}) collective-permute-start(bf16[256,128]{1,0:T(8,128)(2,1)S(1)} %get-tuple-element.41), channel_id=1, source_target_pairs={{1,4},{3,6},{5,8},{7,10},{9,12},{11,14},{13,16},{15,18},{17,20},{1... | collective-permute-start | bytes 196616 | tf_op jit(solution)/shard_map/ppermute | solution.py:295
  45.6 9.1 %collective-permute-start.6 = (bf16[512,128]{1,0:T(8,128)(2,1)S(1)}, bf16[512,128]{1,0:T(8,128)(2,1)S(1)}, u32[]{:S(2)}, u32[]{:S(2)}) collective-permute-start(bf16[512,128]{1,0:T(8,128)(2,1)S(1)} %get-tuple-element.44), channel_id=1, source_target_pairs={{0,32},{32,64},{64,96},{96,128},{128,160},{160,192},{192,224},{224... | collective-permute-start | bytes 393224 | tf_op jit(solution)/shard_map/ppermute | solution.py:331
  50.8 8.1 %collective-permute-start.7 = (bf16[512,128]{1,0:T(8,128)(2,1)S(1)}, bf16[512,128]{1,0:T(8,128)(2,1)S(1)}, u32[]{:S(2)}, u32[]{:S(2)}) collective-permute-start(bf16[512,128]{1,0:T(8,128)(2,1)S(1)} %get-tuple-element.45), channel_id=1, source_target_pairs={{16,32},{17,33},{18,34},{19,35},{20,36},{21,37},{22,38},{23,39},{2... | collective-permute-start | bytes 393224 | tf_op jit(solution)/shard_map/ppermute | solution.py:330
  59.2 10.8 %collective-permute-start.8 = (bf16[256,128]{1,0:T(8,128)(2,1)S(1)}, bf16[256,128]{1,0:T(8,128)(2,1)S(1)}, u32[]{:S(2)}, u32[]{:S(2)}) collective-permute-start(bf16[256,128]{1,0:T(8,128)(2,1)S(1)} %get-tuple-element.47), channel_id=1, source_target_pairs={{1,4},{3,6},{5,8},{7,10},{9,12},{11,14},{13,16},{15,18},{17,20},{1... | collective-permute-start | bytes 196616 | tf_op jit(solution)/shard_map/ppermute | solution.py:295
  70.5 6.5 %collective-permute-start.9 = (bf16[512,128]{1,0:T(8,128)(2,1)S(1)}, bf16[512,128]{1,0:T(8,128)(2,1)S(1)}, u32[]{:S(2)}, u32[]{:S(2)}) collective-permute-start(bf16[512,128]{1,0:T(8,128)(2,1)S(1)} %get-tuple-element.48), channel_id=1, source_target_pairs={{0,32},{32,64},{64,96},{96,128},{128,160},{160,192},{192,224},{224... | collective-permute-start | bytes 393224 | tf_op jit(solution)/shard_map/ppermute | solution.py:331
  74.1 9.9 %collective-permute-start.10 = (bf16[512,128]{1,0:T(8,128)(2,1)S(1)}, bf16[512,128]{1,0:T(8,128)(2,1)S(1)}, u32[]{:S(2)}, u32[]{:S(2)}) collective-permute-start(bf16[512,128]{1,0:T(8,128)(2,1)S(1)} %get-tuple-element.49), channel_id=1, source_target_pairs={{16,32},{17,33},{18,34},{19,35},{20,36},{21,37},{22,38},{23,39},{2... | collective-permute-start | bytes 393224 | tf_op jit(solution)/shard_map/ppermute | solution.py:330
  84.9 12.4 %collective-permute-start.11 = (bf16[512,128]{1,0:T(8,128)(2,1)S(1)}, bf16[512,128]{1,0:T(8,128)(2,1)S(1)}, u32[]{:S(2)}, u32[]{:S(2)}) collective-permute-start(bf16[512,128]{1,0:T(8,128)(2,1)S(1)} %get-tuple-element.50.own), channel_id=1, source_target_pairs={{1,4},{3,6},{5,8},{7,10},{9,12},{11,14},{13,16},{15,18},{17,20},{1... | collective-permute-start | bytes 393224 | tf_op jit(solution)/shard_map/ppermute | solution.py:295
  87.4 9.9 %collective-permute-start.12 = (bf16[512,128]{1,0:T(8,128)(2,1)S(1)}, bf16[512,128]{1,0:T(8,128)(2,1)S(1)}, u32[]{:S(2)}, u32[]{:S(2)}) collective-permute-start(bf16[512,128]{1,0:T(8,128)(2,1)S(1)} %get-tuple-element.50.own), channel_id=1, source_target_pairs={{1,17},{3,19},{5,21},{7,23},{9,25},{11,27},{13,29},{15,31},{17,1},... | collective-permute-start | bytes 393224 | tf_op jit(solution)/shard_map/ppermute | solution.py:316

commit v9 on v7

--- a/solution.py
+++ b/solution.py
@@ -136,18 +136,14 @@
 def pair_kernel(tick, both, right, inverse, given, solved, outgoing):
     block, columns = solved.shape
     odd = lax.rem(lax.axis_index("blk"), 2)
-    rows = both.shape[0] // 2
-    mine = odd * rows
-    theirs = (1 - odd) * rows
+    mine = odd * (2 * block)
+    theirs = (1 - odd) * (2 * block)
 
     def part(at):
         return both[pl.ds(pl.multiple_of(at, block), block), :].astype(F32)
 
     incoming = part(mine) + part(theirs + block)
     other = part(mine + block) + part(theirs)
-    for i in range(2 * block, rows, 2 * block):
-        incoming += part(mine + i) + part(theirs + i + block)
-        other += part(mine + i + block) + part(theirs + i)
     value = mm(inverse[...], (right[tick - 1] - incoming).astype(BF16))
     solved[...] = value
     outgoing[0:block] = value.astype(BF16)
@@ -186,13 +182,11 @@
     value += mm(kept[1], same_one)
     value += mm(kept[2], odd_one)
     value += mm(kept[0], third[...])
-    if opposite is not None:
-        value += mm(kept[4], opposite[0:block])
+    value += mm(kept[4], opposite[0:block])
     other = mm(given[0:block, :], same_one)
     other += mm(given[block : 2 * block, :], odd_one)
     other += mm(given[2 * block : 3 * block, :], self_one)
-    if opposite is not None:
-        other += mm(given[3 * block : 4 * block, :], opposite[block:])
+    other += mm(given[3 * block : 4 * block, :], opposite[block:])
     return value, other
 
 
@@ -201,15 +195,6 @@
     value, other = products(kept, given, own, beside, third, opposite)
     sums[0:block] = value.astype(BF16)
     sums[block:] = other.astype(BF16)
-
-
-def far_kernel(kept, given, own, beside, third, far_sums, sums, leaving):
-    block = third.shape[0]
-    value, other = products(kept, given, own, beside, third, None)
-    sums[0:block] = value.astype(BF16)
-    sums[block:] = other.astype(BF16)
-    leaving[0:block] = mm(far_sums[0:block, :], own[0:block]).astype(BF16)
-    leaving[block:] = mm(far_sums[block:, :], own[block:]).astype(BF16)
 
 
 def last_kernel(ticks, kept, given, own, beside, third, opposite, *refs):
@@ -225,13 +210,13 @@
         copy.wait()
 
 
-def partial_sums(kernel, operands, pairs_out):
+def partial_sums(operands):
     block, columns = operands[4].shape
     return pl.pallas_call(
-        kernel,
-        out_shape=(jax.ShapeDtypeStruct((2 * block, columns), BF16),) * pairs_out,
+        partial_kernel,
+        out_shape=jax.ShapeDtypeStruct((2 * block, columns), BF16),
         in_specs=[VMEM] * len(operands),
-        out_specs=(VMEM,) * pairs_out,
+        out_specs=VMEM,
         compiler_params=params(),
         name="partial",
     )(*operands)
@@ -282,7 +267,6 @@
     chip_pairs = [[2 * c, 2 * c + 1] for c in range(chips)]
     next_pairs = [[2 * c + 1, (2 * c + 2) % around] for c in range(chips)]
     third_pairs = [[2 * c + 1, (2 * c + 4) % around] for c in range(chips)]
-    opposite_pairs = [[b, b + chips] for b in range(chips)]
 
     def paired(value, pairs):
         return lax.all_gather(value, "blk", axis=0, tiled=True, axis_index_groups=pairs)
@@ -293,38 +277,23 @@
 
     solved, own, inverse, right = first_solve(right_side, carry_in, inverse_diag)
     finished = [solved]
-    far_sums = None
-    seconds = range(1, around, 2)
-    opposite_of = [(b, (b + chips) % around) for b in seconds]
-    forward = [(g * around + a, (g + 1) * around + b) for g in range(groups - 1) for a, b in opposite_of]
+    seconds = [(b, (b + chips) % around) for b in range(1, around, 2)]
     for tick in range(ticks):
-        last = tick + 1 == ticks
-        near_form = tick == 0 or last
-        third = swapped(own[0:block], third_pairs)
         if tick == 0:
             chip = paired(own, chip_pairs)
             own = jnp.where(odd == 0, chip, jnp.roll(chip, block, 0))
             held = lax.optimization_barrier((own, sources, counts, factor_blocks, inverse, right))[1:]
             kept, handed = combine(around, *held)
             given = swapped(handed, chip_pairs)
-        opposite = lax.ppermute(own, "blk", opposite_of) if near_form else None
+        third = swapped(own, third_pairs)[0:block]
+        opposite = lax.ppermute(own, "blk", seconds)
         beside = paired(own, next_pairs)
-        operands = [kept, given, own, beside, third]
-        if last:
-            exact, crossing, outputs = last_sums(operands + [opposite], finished)
-            carry = carry_sum(exact, paired(crossing, chip_pairs))
-            return (outputs, carry)
-        if near_form:
-            (sums,) = partial_sums(partial_kernel, operands + [opposite], 1)
-            own_far, pair_far = lax.optimization_barrier((sums, kept[4], given[3 * block : 4 * block]))[1:]
-            far_sums = lax.ppermute(jnp.concatenate([own_far, pair_far], 0), "blk", opposite_of)
-        else:
-            sums, leaving = partial_sums(far_kernel, operands + [far_sums], 2)
-            far = lax.ppermute(leaving, ("grp", "blk"), forward)
-        sums = lax.ppermute(sums, "grp", [(g, g + 1) for g in range(groups - 1)])
-        if not near_form:
-            sums = jnp.concatenate([sums, far], 0)
-        solved, own = pair_solve(tick + 1, paired(sums, chip_pairs), right, inverse, given)
+        operands = [kept, given, own, beside, third, opposite]
+        if tick + 1 == ticks:
+            exact, crossing, outputs = last_sums(operands, finished)
+            return (outputs, carry_sum(exact, paired(crossing, chip_pairs)))
+        moved = lax.ppermute(partial_sums(operands), "grp", [(g, g + 1) for g in range(groups - 1)])
+        solved, own = pair_solve(tick + 1, paired(moved, chip_pairs), right, inverse, given)
         finished.append(solved)
 
 

time: 107 us -> 101 us (0.944)
  the two profiles are of different devices: /device:TPU:65 before, /device:TPU:257 now
where the time goes in v9:
time: 101 us; the launch traced here: 100 us
  blocking collectives  38.5 us (38%)
  starting transfers between devices  35 us (35%)
  waiting for transfers between devices  18.4 us (18%)
  Pallas kernels  6.75 us (7%)
  between operations  1.5 us (1%)
    all_gather x9, blocking collectives, paired(): lax.all_gather(value, 'blk', axis=0, tiled=True, axis_index_groups=pairs)  38.5 us
    ppermute x3, waiting for transfers between devices, shards(): lax.ppermute(partial_sums(operands), 'grp', [(g, g + 1) for g in range(gr...  15.5 us
    ppermute x4, starting transfers between devices, shards(): opposite = lax.ppermute(own, 'blk', seconds)  15.3 us
    ppermute x5, starting transfers between devices, swapped(): return lax.ppermute(value, 'blk', partner)  13.9 us
    ppermute x3, starting transfers between devices, shards(): lax.ppermute(partial_sums(operands), 'grp', [(g, g + 1) for g in range(gr...  5.83 us
    ppermute x4, waiting for transfers between devices, shards(): opposite = lax.ppermute(own, 'blk', seconds)  2.91 us
  transfers between devices with their start and end apart: 12, of which 5 were waited for; matrix products, arithmetic and copies ran while one was open for 0% of the time, Pallas kernels for 0%

profile of v9, /device:TPU:257, one launch (start us, length us, event | category | flops | bytes accessed | tf_op | source)
XLA Modules:
  0.0 100.3 jit_solution(13829119594687394631)
XLA Ops:
  0.6 1.2 %first.1 = (f32[256,128]{1,0:T(8,128)S(1)}, bf16[256,128]{1,0:T(8,128)(2,1)S(1)}, bf16[256,256]{1,0:T(8,128)(2,1)S(1)}, f32[3,256,128]{2,1,0:T(8,128)S(1)}) custom-call(f32[4,256,128]{2,1,0:T(8,128)} %right.1, f32[256,128]{1,0:T(8,128)} %incoming.1, bf16[256,256]{1,0:T(8,128)(2,1)} %inverse.1), custom_call_target="tpu_custom_call" | custom-call | tf_op jit(solution)/shard_map/first/pallas_call | solution.py:116
  1.9 2.2 %all_gather.27 = bf16[512,128]{1,0:T(8,128)(2,1)S(1)} all-gather(bf16[256,128]{1,0:T(8,128)(2,1)S(1)} %get-tuple-element.22), channel_id=1, replica_groups={{0,1},{2,3},{4,5},{6,7},{8,9},{10,11},{12,13},{14,15},{16,17},{18,19},{..., dimensions={0}, use_global_device_ids=true | all-gather | bytes 196608 | tf_op jit(solution)/shard_map/all_gather | solution.py:272
  4.8 1.7 %combine.1 = (bf16[5,256,256]{2,1,0:T(8,128)(2,1)S(1)}, bf16[2048,256]{1,0:T(8,128)(2,1)S(1)}) custom-call(s32[1]{0:T(128)S(6)} %copy.8.count, s32[1,24]{1,0:T(1,128)} %source_list, bf16[1,24,256,256]{3,2,1,0:T(8,128)(2,1)} %blocks, bf16[256,256]{1,0:T(8,128)(2,1)S(1)} %get-tuple-element.28.inverse, f32[3,256,128]{2,1,0:T(8,128)S(1)} %get-tuple-element.29.right), custom_call_target="tpu_custom_call" | custom-call | flops 4000000 | bytes 10000000 | tf_op jit(solution)/shard_map/combine/pallas_call | solution.py:76
  6.5 2.3 %collective-permute-start = (bf16[2048,256]{1,0:T(8,128)(2,1)S(1)}, bf16[2048,256]{1,0:T(8,128)(2,1)S(1)}, u32[]{:S(2)}, u32[]{:S(2)}) collective-permute-start(bf16[2048,256]{1,0:T(8,128)(2,1)S(1)} %get-tuple-element.31), channel_id=1, source_target_pairs={{0,1},{2,3},{4,5},{6,7},{8,9},{10,11},{12,13},{14,15},{16,17},{18,... | collective-permute-start | bytes 3145736 | tf_op jit(solution)/shard_map/ppermute | solution.py:276
  8.8 5.0 %collective-permute-start.1 = (bf16[512,128]{1,0:T(8,128)(2,1)S(1)}, bf16[512,128]{1,0:T(8,128)(2,1)S(1)}, u32[]{:S(2)}, u32[]{:S(2)}) collective-permute-start(bf16[512,128]{1,0:T(8,128)(2,1)S(1)} %maximum_select_fusion.own), channel_id=1, source_target_pairs={{1,4},{3,6},{5,8},{7,10},{9,12},{11,14},{13,16},{15,18},{17,20},{1... | collective-permute-start | bytes 393224 | tf_op jit(solution)/shard_map/ppermute | solution.py:276
  13.8 5.1 %collective-permute-start.2 = (bf16[512,128]{1,0:T(8,128)(2,1)S(1)}, bf16[512,128]{1,0:T(8,128)(2,1)S(1)}, u32[]{:S(2)}, u32[]{:S(2)}) collective-permute-start(bf16[512,128]{1,0:T(8,128)(2,1)S(1)} %maximum_select_fusion.own), channel_id=1, source_target_pairs={{1,17},{3,19},{5,21},{7,23},{9,25},{11,27},{13,29},{15,31},{17,1},... | collective-permute-start | bytes 393224 | tf_op jit(solution)/shard_map/ppermute | solution.py:289
  18.9 5.4 %all_gather.28.beside = bf16[1024,128]{1,0:T(8,128)(2,1)S(1)} all-gather(bf16[512,128]{1,0:T(8,128)(2,1)S(1)} %maximum_select_fusion.own), channel_id=1, replica_groups={{1,2},{3,4},{5,6},{7,8},{9,10},{11,12},{13,14},{15,16},{17,18},{19,20},..., dimensions={0}, use_global_device_ids=true | all-gather | bytes 393216 | tf_op jit(solution)/shard_map/all_gather | solution.py:272
  24.3 0.5 partial.3
  24.7 2.0 %collective-permute-start.3 = (bf16[512,128]{1,0:T(8,128)(2,1)S(1)}, bf16[512,128]{1,0:T(8,128)(2,1)S(1)}, u32[]{:S(2)}, u32[]{:S(2)}) collective-permute-start(bf16[512,128]{1,0:T(8,128)(2,1)S(1)} %partial.3), channel_id=1, source_target_pairs={{0,32},{32,64},{64,96},{96,128},{128,160},{160,192},{192,224},{224... | collective-permute-start | bytes 393224 | tf_op jit(solution)/shard_map/ppermute | solution.py:295
  26.7 4.9 %collective-permute-done.3 = bf16[512,128]{1,0:T(8,128)(2,1)S(1)} collective-permute-done((bf16[512,128]{1,0:T(8,128)(2,1)S(1)}, bf16[512,128]{1,0:T(8,128)(2,1)S(1)}, u32[]{:S(2)}, u32[]{:S(2)}) %collective-permute-start.3) | collective-permute-done | bytes 131104 | tf_op jit(solution)/shard_map/ppermute | solution.py:295
  31.7 3.8 %all_gather.29.both = bf16[1024,128]{1,0:T(8,128)(2,1)S(1)} all-gather(bf16[512,128]{1,0:T(8,128)(2,1)S(1)} %collective-permute-done.3), channel_id=1, replica_groups={{0,1},{2,3},{4,5},{6,7},{8,9},{10,11},{12,13},{14,15},{16,17},{18,19},{..., dimensions={0}, use_global_device_ids=true | all-gather | bytes 393216 | tf_op jit(solution)/shard_map/all_gather | solution.py:272
  35.8 2.4 %collective-permute-start.4 = (bf16[512,128]{1,0:T(8,128)(2,1)S(1)}, bf16[512,128]{1,0:T(8,128)(2,1)S(1)}, u32[]{:S(2)}, u32[]{:S(2)}) collective-permute-start(bf16[512,128]{1,0:T(8,128)(2,1)S(1)} %get-tuple-element.32.own), channel_id=1, source_target_pairs={{1,4},{3,6},{5,8},{7,10},{9,12},{11,14},{13,16},{15,18},{17,20},{1... | collective-permute-start | bytes 393224 | tf_op jit(solution)/shard_map/ppermute | solution.py:276
  38.2 2.3 %collective-permute-start.5 = (bf16[512,128]{1,0:T(8,128)(2,1)S(1)}, bf16[512,128]{1,0:T(8,128)(2,1)S(1)}, u32[]{:S(2)}, u32[]{:S(2)}) collective-permute-start(bf16[512,128]{1,0:T(8,128)(2,1)S(1)} %get-tuple-element.32.own), channel_id=1, source_target_pairs={{1,17},{3,19},{5,21},{7,23},{9,25},{11,27},{13,29},{15,31},{17,1},... | collective-permute-start | bytes 393224 | tf_op jit(solution)/shard_map/ppermute | solution.py:289
  40.5 5.4 %all_gather.30.beside = bf16[1024,128]{1,0:T(8,128)(2,1)S(1)} all-gather(bf16[512,128]{1,0:T(8,128)(2,1)S(1)} %get-tuple-element.32.own), channel_id=1, replica_groups={{1,2},{3,4},{5,6},{7,8},{9,10},{11,12},{13,14},{15,16},{17,18},{19,20},..., dimensions={0}, use_global_device_ids=true | all-gather | bytes 393216 | tf_op jit(solution)/shard_map/all_gather | solution.py:272
  45.9 2.3 %collective-permute-done.5.opposite = bf16[512,128]{1,0:T(8,128)(2,1)S(1)} collective-permute-done((bf16[512,128]{1,0:T(8,128)(2,1)S(1)}, bf16[512,128]{1,0:T(8,128)(2,1)S(1)}, u32[]{:S(2)}, u32[]{:S(2)}) %collective-permute-start.5) | collective-permute-done | bytes 131104 | tf_op jit(solution)/shard_map/ppermute | solution.py:289
  48.6 1.9 %collective-permute-start.6 = (bf16[512,128]{1,0:T(8,128)(2,1)S(1)}, bf16[512,128]{1,0:T(8,128)(2,1)S(1)}, u32[]{:S(2)}, u32[]{:S(2)}) collective-permute-start(bf16[512,128]{1,0:T(8,128)(2,1)S(1)} %partial.4), channel_id=1, source_target_pairs={{0,32},{32,64},{64,96},{96,128},{128,160},{160,192},{192,224},{224... | collective-permute-start | bytes 393224 | tf_op jit(solution)/shard_map/ppermute | solution.py:295
  50.5 5.6 %collective-permute-done.6 = bf16[512,128]{1,0:T(8,128)(2,1)S(1)} collective-permute-done((bf16[512,128]{1,0:T(8,128)(2,1)S(1)}, bf16[512,128]{1,0:T(8,128)(2,1)S(1)}, u32[]{:S(2)}, u32[]{:S(2)}) %collective-permute-start.6) | collective-permute-done | bytes 131104 | tf_op jit(solution)/shard_map/ppermute | solution.py:295
  56.1 3.1 %all_gather.31.both = bf16[1024,128]{1,0:T(8,128)(2,1)S(1)} all-gather(bf16[512,128]{1,0:T(8,128)(2,1)S(1)} %collective-permute-done.6), channel_id=1, replica_groups={{0,1},{2,3},{4,5},{6,7},{8,9},{10,11},{12,13},{14,15},{16,17},{18,19},{..., dimensions={0}, use_global_device_ids=true | all-gather | bytes 393216 | tf_op jit(solution)/shard_map/all_gather | solution.py:272
  59.5 1.9 %collective-permute-start.7 = (bf16[512,128]{1,0:T(8,128)(2,1)S(1)}, bf16[512,128]{1,0:T(8,128)(2,1)S(1)}, u32[]{:S(2)}, u32[]{:S(2)}) collective-permute-start(bf16[512,128]{1,0:T(8,128)(2,1)S(1)} %get-tuple-element.33.own), channel_id=1, source_target_pairs={{1,4},{3,6},{5,8},{7,10},{9,12},{11,14},{13,16},{15,18},{17,20},{1... | collective-permute-start | bytes 393224 | tf_op jit(solution)/shard_map/ppermute | solution.py:276
  61.4 4.1 %collective-permute-start.8 = (bf16[512,128]{1,0:T(8,128)(2,1)S(1)}, bf16[512,128]{1,0:T(8,128)(2,1)S(1)}, u32[]{:S(2)}, u32[]{:S(2)}) collective-permute-start(bf16[512,128]{1,0:T(8,128)(2,1)S(1)} %get-tuple-element.33.own), channel_id=1, source_target_pairs={{1,17},{3,19},{5,21},{7,23},{9,25},{11,27},{13,29},{15,31},{17,1},... | collective-permute-start | bytes 393224 | tf_op jit(solution)/shard_map/ppermute | solution.py:289
  65.5 5.4 %all_gather.32.beside = bf16[1024,128]{1,0:T(8,128)(2,1)S(1)} all-gather(bf16[512,128]{1,0:T(8,128)(2,1)S(1)} %get-tuple-element.33.own), channel_id=1, replica_groups={{1,2},{3,4},{5,6},{7,8},{9,10},{11,12},{13,14},{15,16},{17,18},{19,20},..., dimensions={0}, use_global_device_ids=true | all-gather | bytes 393216 | tf_op jit(solution)/shard_map/all_gather | solution.py:272
  70.9 0.5 partial.5
  71.4 1.9 %collective-permute-start.9 = (bf16[512,128]{1,0:T(8,128)(2,1)S(1)}, bf16[512,128]{1,0:T(8,128)(2,1)S(1)}, u32[]{:S(2)}, u32[]{:S(2)}) collective-permute-start(bf16[512,128]{1,0:T(8,128)(2,1)S(1)} %partial.5), channel_id=1, source_target_pairs={{0,32},{32,64},{64,96},{96,128},{128,160},{160,192},{192,224},{224... | collective-permute-start | bytes 393224 | tf_op jit(solution)/shard_map/ppermute | solution.py:295
  73.3 5.0 %collective-permute-done.9 = bf16[512,128]{1,0:T(8,128)(2,1)S(1)} collective-permute-done((bf16[512,128]{1,0:T(8,128)(2,1)S(1)}, bf16[512,128]{1,0:T(8,128)(2,1)S(1)}, u32[]{:S(2)}, u32[]{:S(2)}) %collective-permute-start.9) | collective-permute-done | bytes 131104 | tf_op jit(solution)/shard_map/ppermute | solution.py:295
  78.3 4.2 %all_gather.33.both = bf16[1024,128]{1,0:T(8,128)(2,1)S(1)} all-gather(bf16[512,128]{1,0:T(8,128)(2,1)S(1)} %collective-permute-done.9), channel_id=1, replica_groups={{0,1},{2,3},{4,5},{6,7},{8,9},{10,11},{12,13},{14,15},{16,17},{18,19},{..., dimensions={0}, use_global_device_ids=true | all-gather | bytes 393216 | tf_op jit(solution)/shard_map/all_gather | solution.py:272
  82.7 2.2 %collective-permute-start.10 = (bf16[512,128]{1,0:T(8,128)(2,1)S(1)}, bf16[512,128]{1,0:T(8,128)(2,1)S(1)}, u32[]{:S(2)}, u32[]{:S(2)}) collective-permute-start(bf16[512,128]{1,0:T(8,128)(2,1)S(1)} %get-tuple-element.34.own), channel_id=1, source_target_pairs={{1,4},{3,6},{5,8},{7,10},{9,12},{11,14},{13,16},{15,18},{17,20},{1... | collective-permute-start | bytes 393224 | tf_op jit(solution)/shard_map/ppermute | solution.py:276
  85.0 3.9 %collective-permute-start.11 = (bf16[512,128]{1,0:T(8,128)(2,1)S(1)}, bf16[512,128]{1,0:T(8,128)(2,1)S(1)}, u32[]{:S(2)}, u32[]{:S(2)}) collective-permute-start(bf16[512,128]{1,0:T(8,128)(2,1)S(1)} %get-tuple-element.34.own), channel_id=1, source_target_pairs={{1,17},{3,19},{5,21},{7,23},{9,25},{11,27},{13,29},{15,31},{17,1},... | collective-permute-start | bytes 393224 | tf_op jit(solution)/shard_map/ppermute | solution.py:289
  88.9 5.4 %all_gather.34.beside = bf16[1024,128]{1,0:T(8,128)(2,1)S(1)} all-gather(bf16[512,128]{1,0:T(8,128)(2,1)S(1)} %get-tuple-element.34.own), channel_id=1, replica_groups={{1,2},{3,4},{5,6},{7,8},{9,10},{11,12},{13,14},{15,16},{17,18},{19,20},..., dimensions={0}, use_global_device_ids=true | all-gather | bytes 393216 | tf_op jit(solution)/shard_map/all_gather | solution.py:272
  94.2 0.6 collective-permute-done.11.opposite
  94.9 1.0 %last.1 = (f32[256,128]{1,0:T(8,128)S(1)}, bf16[256,128]{1,0:T(8,128)(2,1)S(1)}, f32[4,256,128]{2,1,0:T(8,128)}) custom-call(bf16[5,256,256]{2,1,0:T(8,128)(2,1)S(1)} %get-tuple-element.30.kept, bf16[2048,256]{1,0:T(8,128)(2,1)S(1)} %collective-permute-done.given, bf16[512,128]{1,0:T(8,128)(2,1)S(1)} %get-tuple-element.34.own, ...), custom_call_target="tpu_custom_call" | custom-call | tf_op jit(solution)/shard_map/last/pallas_call | solution.py:228
  95.9 3.7 %all_gather.35.both = bf16[512,128]{1,0:T(8,128)(2,1)S(1)} all-gather(bf16[256,128]{1,0:T(8,128)(2,1)S(1)} %get-tuple-element.41), channel_id=1, replica_groups={{0,1},{2,3},{4,5},{6,7},{8,9},{10,11},{12,13},{14,15},{16,17},{18,19},{..., dimensions={0}, use_global_device_ids=true | all-gather | bytes 196608 | tf_op jit(solution)/shard_map/all_gather | solution.py:272
  99.6 0.7 carry.1
  (17 shorter events, 1.3 us)
Async XLA Ops:
  6.5 17.8 %collective-permute-start = (bf16[2048,256]{1,0:T(8,128)(2,1)S(1)}, bf16[2048,256]{1,0:T(8,128)(2,1)S(1)}, u32[]{:S(2)}, u32[]{:S(2)}) collective-permute-start(bf16[2048,256]{1,0:T(8,128)(2,1)S(1)} %get-tuple-element.31), channel_id=1, source_target_pairs={{0,1},{2,3},{4,5},{6,7},{8,9},{10,11},{12,13},{14,15},{16,17},{18,... | collective-permute-start | bytes 3145736 | tf_op jit(solution)/shard_map/ppermute | solution.py:276
  8.8 15.4 %collective-permute-start.1 = (bf16[512,128]{1,0:T(8,128)(2,1)S(1)}, bf16[512,128]{1,0:T(8,128)(2,1)S(1)}, u32[]{:S(2)}, u32[]{:S(2)}) collective-permute-start(bf16[512,128]{1,0:T(8,128)(2,1)S(1)} %maximum_select_fusion.own), channel_id=1, source_target_pairs={{1,4},{3,6},{5,8},{7,10},{9,12},{11,14},{13,16},{15,18},{17,20},{1... | collective-permute-start | bytes 393224 | tf_op jit(solution)/shard_map/ppermute | solution.py:276
  13.8 10.5 %collective-permute-start.2 = (bf16[512,128]{1,0:T(8,128)(2,1)S(1)}, bf16[512,128]{1,0:T(8,128)(2,1)S(1)}, u32[]{:S(2)}, u32[]{:S(2)}) collective-permute-start(bf16[512,128]{1,0:T(8,128)(2,1)S(1)} %maximum_select_fusion.own), channel_id=1, source_target_pairs={{1,17},{3,19},{5,21},{7,23},{9,25},{11,27},{13,29},{15,31},{17,1},... | collective-permute-start | bytes 393224 | tf_op jit(solution)/shard_map/ppermute | solution.py:289
  24.7 6.9 %collective-permute-start.3 = (bf16[512,128]{1,0:T(8,128)(2,1)S(1)}, bf16[512,128]{1,0:T(8,128)(2,1)S(1)}, u32[]{:S(2)}, u32[]{:S(2)}) collective-permute-start(bf16[512,128]{1,0:T(8,128)(2,1)S(1)} %partial.3), channel_id=1, source_target_pairs={{0,32},{32,64},{64,96},{96,128},{128,160},{160,192},{192,224},{224... | collective-permute-start | bytes 393224 | tf_op jit(solution)/shard_map/ppermute | solution.py:295
  35.8 10.1 %collective-permute-start.4 = (bf16[512,128]{1,0:T(8,128)(2,1)S(1)}, bf16[512,128]{1,0:T(8,128)(2,1)S(1)}, u32[]{:S(2)}, u32[]{:S(2)}) collective-permute-start(bf16[512,128]{1,0:T(8,128)(2,1)S(1)} %get-tuple-element.32.own), channel_id=1, source_target_pairs={{1,4},{3,6},{5,8},{7,10},{9,12},{11,14},{13,16},{15,18},{17,20},{1... | collective-permute-start | bytes 393224 | tf_op jit(solution)/shard_map/ppermute | solution.py:276
  38.2 9.9 %collective-permute-start.5 = (bf16[512,128]{1,0:T(8,128)(2,1)S(1)}, bf16[512,128]{1,0:T(8,128)(2,1)S(1)}, u32[]{:S(2)}, u32[]{:S(2)}) collective-permute-start(bf16[512,128]{1,0:T(8,128)(2,1)S(1)} %get-tuple-element.32.own), channel_id=1, source_target_pairs={{1,17},{3,19},{5,21},{7,23},{9,25},{11,27},{13,29},{15,31},{17,1},... | collective-permute-start | bytes 393224 | tf_op jit(solution)/shard_map/ppermute | solution.py:289
  48.6 7.5 %collective-permute-start.6 = (bf16[512,128]{1,0:T(8,128)(2,1)S(1)}, bf16[512,128]{1,0:T(8,128)(2,1)S(1)}, u32[]{:S(2)}, u32[]{:S(2)}) collective-permute-start(bf16[512,128]{1,0:T(8,128)(2,1)S(1)} %partial.4), channel_id=1, source_target_pairs={{0,32},{32,64},{64,96},{96,128},{128,160},{160,192},{192,224},{224... | collective-permute-start | bytes 393224 | tf_op jit(solution)/shard_map/ppermute | solution.py:295
  59.5 11.4 %collective-permute-start.7 = (bf16[512,128]{1,0:T(8,128)(2,1)S(1)}, bf16[512,128]{1,0:T(8,128)(2,1)S(1)}, u32[]{:S(2)}, u32[]{:S(2)}) collective-permute-start(bf16[512,128]{1,0:T(8,128)(2,1)S(1)} %get-tuple-element.33.own), channel_id=1, source_target_pairs={{1,4},{3,6},{5,8},{7,10},{9,12},{11,14},{13,16},{15,18},{17,20},{1... | collective-permute-start | bytes 393224 | tf_op jit(solution)/shard_map/ppermute | solution.py:276
  61.4 9.5 %collective-permute-start.8 = (bf16[512,128]{1,0:T(8,128)(2,1)S(1)}, bf16[512,128]{1,0:T(8,128)(2,1)S(1)}, u32[]{:S(2)}, u32[]{:S(2)}) collective-permute-start(bf16[512,128]{1,0:T(8,128)(2,1)S(1)} %get-tuple-element.33.own), channel_id=1, source_target_pairs={{1,17},{3,19},{5,21},{7,23},{9,25},{11,27},{13,29},{15,31},{17,1},... | collective-permute-start | bytes 393224 | tf_op jit(solution)/shard_map/ppermute | solution.py:289
  71.4 6.9 %collective-permute-start.9 = (bf16[512,128]{1,0:T(8,128)(2,1)S(1)}, bf16[512,128]{1,0:T(8,128)(2,1)S(1)}, u32[]{:S(2)}, u32[]{:S(2)}) collective-permute-start(bf16[512,128]{1,0:T(8,128)(2,1)S(1)} %partial.5), channel_id=1, source_target_pairs={{0,32},{32,64},{64,96},{96,128},{128,160},{160,192},{192,224},{224... | collective-permute-start | bytes 393224 | tf_op jit(solution)/shard_map/ppermute | solution.py:295
  82.7 11.5 %collective-permute-start.10 = (bf16[512,128]{1,0:T(8,128)(2,1)S(1)}, bf16[512,128]{1,0:T(8,128)(2,1)S(1)}, u32[]{:S(2)}, u32[]{:S(2)}) collective-permute-start(bf16[512,128]{1,0:T(8,128)(2,1)S(1)} %get-tuple-element.34.own), channel_id=1, source_target_pairs={{1,4},{3,6},{5,8},{7,10},{9,12},{11,14},{13,16},{15,18},{17,20},{1... | collective-permute-start | bytes 393224 | tf_op jit(solution)/shard_map/ppermute | solution.py:276
  85.0 9.9 %collective-permute-start.11 = (bf16[512,128]{1,0:T(8,128)(2,1)S(1)}, bf16[512,128]{1,0:T(8,128)(2,1)S(1)}, u32[]{:S(2)}, u32[]{:S(2)}) collective-permute-start(bf16[512,128]{1,0:T(8,128)(2,1)S(1)} %get-tuple-element.34.own), channel_id=1, source_target_pairs={{1,17},{3,19},{5,21},{7,23},{9,25},{11,27},{13,29},{15,31},{17,1},... | collective-permute-start | bytes 393224 | tf_op jit(solution)/shard_map/ppermute | solution.py:289

commit v10 on v9

--- a/solution.py
+++ b/solution.py
@@ -23,12 +23,15 @@
     return jnp.dot(a, b, preferred_element_type=F32)
 
 
-def combine_kernel(around, count, source_list, blocks, inverse, right, kept, handed, source_here, landing, sums, arrived, small):
+def combine_kernel(around, count, source_list, blocks, inverse, right, chip, kept, handed, pair, source_here, landing, sums, arrived, small):
     block = inverse.shape[0]
     copy = pltpu.make_async_copy(source_list, source_here, small)
     copy.start()
     own = lax.axis_index("blk")
-    sign = 2 * lax.rem(own, 2) - 1
+    second = lax.rem(own, 2)
+    sign = 2 * second - 1
+    pair[0:block] = chip[pl.ds(pl.multiple_of(second * block, block), block), :]
+    pair[block:] = chip[pl.ds(pl.multiple_of((1 - second) * block, block), block), :]
 
     def copy_of(k):
         return pltpu.make_async_copy(blocks.at[0, k], landing.at[k], arrived.at[k])
@@ -70,7 +73,7 @@
     return pltpu.with_memory_space_constraint(value, pltpu.HBM)
 
 
-def combine(around, sources, counts, factor_blocks, inverse, right):
+def combine(around, chip, sources, counts, factor_blocks, inverse, right):
     slots, block = factor_blocks.shape[1], factor_blocks.shape[2]
     ticks = right.shape[0]
     return pl.pallas_call(
@@ -78,9 +81,10 @@
         out_shape=(
             jax.ShapeDtypeStruct((5, block, block), BF16),
             jax.ShapeDtypeStruct(((5 + ticks) * block, block), BF16),
+            jax.ShapeDtypeStruct(chip.shape, BF16),
         ),
-        in_specs=[SMEM, HBM, HBM, VMEM, VMEM],
-        out_specs=(VMEM, VMEM),
+        in_specs=[SMEM, HBM, HBM, VMEM, VMEM, VMEM],
+        out_specs=(VMEM, VMEM, VMEM),
         scratch_shapes=[
             pltpu.SMEM(sources.shape, jnp.int32),
             pltpu.VMEM((slots, block, block), BF16),
@@ -91,7 +95,7 @@
         compiler_params=params(),
         cost_estimate=pl.CostEstimate(flops=4_000_000, bytes_accessed=10_000_000, transcendentals=0),
         name="combine",
-    )(counts, in_hbm(sources), in_hbm(factor_blocks), inverse, right)
+    )(counts, in_hbm(sources), in_hbm(factor_blocks), inverse, right, chip)
 
 
 def first_kernel(right, incoming, inverse, solved, outgoing, inverse_here, later_here, right_here, incoming_here, arrived):
@@ -262,8 +266,6 @@
     ticks, block = right_side.shape[0], right_side.shape[1]
     groups, around = lax.axis_size("grp"), lax.axis_size("blk")
     chips = around // 2
-    at = lax.axis_index("blk").astype(jnp.int32)
-    odd = lax.rem(at, 2)
     chip_pairs = [[2 * c, 2 * c + 1] for c in range(chips)]
     next_pairs = [[2 * c + 1, (2 * c + 2) % around] for c in range(chips)]
     third_pairs = [[2 * c + 1, (2 * c + 4) % around] for c in range(chips)]
@@ -281,9 +283,7 @@
     for tick in range(ticks):
         if tick == 0:
             chip = paired(own, chip_pairs)
-            own = jnp.where(odd == 0, chip, jnp.roll(chip, block, 0))
-            held = lax.optimization_barrier((own, sources, counts, factor_blocks, inverse, right))[1:]
-            kept, handed = combine(around, *held)
+            kept, handed, own = combine(around, chip, sources, counts, factor_blocks, inverse, right)
             given = swapped(handed, chip_pairs)
         third = swapped(own, third_pairs)[0:block]
         opposite = lax.ppermute(own, "blk", seconds)

time: 101 us -> 101 us (level)
  the two profiles are of different devices: /device:TPU:257 before, /device:TPU:385 now
where the time goes in v10:
time: 101 us; the launch traced here: 100 us
  blocking collectives  40.1 us (40%)
  starting transfers between devices  35.6 us (35%)
  waiting for transfers between devices  16.6 us (16%)
  Pallas kernels  6.44 us (6%)
  between operations  1.48 us (1%)
    all_gather x9, blocking collectives, paired(): lax.all_gather(value, 'blk', axis=0, tiled=True, axis_index_groups=pairs)  40.1 us
    ppermute x5, starting transfers between devices, swapped(): return lax.ppermute(value, 'blk', partner)  14.8 us
    ppermute x4, starting transfers between devices, shards(): opposite = lax.ppermute(own, 'blk', seconds)  14.5 us
    ppermute x3, waiting for transfers between devices, shards(): lax.ppermute(partial_sums(operands), 'grp', [(g, g + 1) for g in range(gr...  14.4 us
    ppermute x3, starting transfers between devices, shards(): lax.ppermute(partial_sums(operands), 'grp', [(g, g + 1) for g in range(gr...  6.38 us
    ppermute x4, waiting for transfers between devices, shards(): opposite = lax.ppermute(own, 'blk', seconds)  2.24 us
  transfers between devices with their start and end apart: 12, of which 5 were waited for; matrix products, arithmetic and copies ran while one was open for 0% of the time, Pallas kernels for 0%

profile of v10, /device:TPU:385, one launch (start us, length us, event | category | flops | bytes accessed | tf_op | source)
XLA Modules:
  0.0 100.3 jit_solution(11739393915158580407)
XLA Ops:
  0.6 1.2 %first.1 = (f32[256,128]{1,0:T(8,128)S(1)}, bf16[256,128]{1,0:T(8,128)(2,1)S(1)}, bf16[256,256]{1,0:T(8,128)(2,1)S(1)}, f32[3,256,128]{2,1,0:T(8,128)S(1)}) custom-call(f32[4,256,128]{2,1,0:T(8,128)} %right.1, f32[256,128]{1,0:T(8,128)} %incoming.1, bf16[256,256]{1,0:T(8,128)(2,1)} %inverse.1), custom_call_target="tpu_custom_call" | custom-call | tf_op jit(solution)/shard_map/first/pallas_call | solution.py:120
  1.9 2.2 %all_gather.27.chip = bf16[512,128]{1,0:T(8,128)(2,1)S(1)} all-gather(bf16[256,128]{1,0:T(8,128)(2,1)S(1)} %get-tuple-element.20), channel_id=1, replica_groups={{0,1},{2,3},{4,5},{6,7},{8,9},{10,11},{12,13},{14,15},{16,17},{18,19},{..., dimensions={0}, use_global_device_ids=true | all-gather | bytes 196608 | tf_op jit(solution)/shard_map/all_gather | solution.py:274
  4.8 1.4 %combine.1 = (bf16[5,256,256]{2,1,0:T(8,128)(2,1)S(1)}, bf16[2048,256]{1,0:T(8,128)(2,1)S(1)}, bf16[512,128]{1,0:T(8,128)(2,1)S(1)}) custom-call(s32[1]{0:T(128)S(6)} %copy.8.count, s32[1,24]{1,0:T(1,128)} %source_list.1, bf16[1,24,256,256]{3,2,1,0:T(8,128)(2,1)} %blocks.1, bf16[256,256]{1,0:T(8,128)(2,1)S(1)} %get-tuple-element.18.inverse, ...), custom_call_target="tpu_custom_call" | custom-call | flops 4000000 | bytes 10000000 | tf_op jit(solution)/shard_map/combine/pallas_call | solution.py:79
  6.1 2.8 %collective-permute-start = (bf16[2048,256]{1,0:T(8,128)(2,1)S(1)}, bf16[2048,256]{1,0:T(8,128)(2,1)S(1)}, u32[]{:S(2)}, u32[]{:S(2)}) collective-permute-start(bf16[2048,256]{1,0:T(8,128)(2,1)S(1)} %get-tuple-element.22), channel_id=1, source_target_pairs={{0,1},{2,3},{4,5},{6,7},{8,9},{10,11},{12,13},{14,15},{16,17},{18,... | collective-permute-start | bytes 3145736 | tf_op jit(solution)/shard_map/ppermute | solution.py:278
  8.9 5.0 %collective-permute-start.1 = (bf16[512,128]{1,0:T(8,128)(2,1)S(1)}, bf16[512,128]{1,0:T(8,128)(2,1)S(1)}, u32[]{:S(2)}, u32[]{:S(2)}) collective-permute-start(bf16[512,128]{1,0:T(8,128)(2,1)S(1)} %get-tuple-element.23.own), channel_id=1, source_target_pairs={{1,4},{3,6},{5,8},{7,10},{9,12},{11,14},{13,16},{15,18},{17,20},{1... | collective-permute-start | bytes 393224 | tf_op jit(solution)/shard_map/ppermute | solution.py:278
  14.0 4.2 %collective-permute-start.2 = (bf16[512,128]{1,0:T(8,128)(2,1)S(1)}, bf16[512,128]{1,0:T(8,128)(2,1)S(1)}, u32[]{:S(2)}, u32[]{:S(2)}) collective-permute-start(bf16[512,128]{1,0:T(8,128)(2,1)S(1)} %get-tuple-element.23.own), channel_id=1, source_target_pairs={{1,17},{3,19},{5,21},{7,23},{9,25},{11,27},{13,29},{15,31},{17,1},... | collective-permute-start | bytes 393224 | tf_op jit(solution)/shard_map/ppermute | solution.py:289
  18.2 5.4 %all_gather.28.beside = bf16[1024,128]{1,0:T(8,128)(2,1)S(1)} all-gather(bf16[512,128]{1,0:T(8,128)(2,1)S(1)} %get-tuple-element.23.own), channel_id=1, replica_groups={{1,2},{3,4},{5,6},{7,8},{9,10},{11,12},{13,14},{15,16},{17,18},{19,20},..., dimensions={0}, use_global_device_ids=true | all-gather | bytes 393216 | tf_op jit(solution)/shard_map/all_gather | solution.py:274
  23.6 0.5 partial.3
  24.1 2.5 %collective-permute-start.3 = (bf16[512,128]{1,0:T(8,128)(2,1)S(1)}, bf16[512,128]{1,0:T(8,128)(2,1)S(1)}, u32[]{:S(2)}, u32[]{:S(2)}) collective-permute-start(bf16[512,128]{1,0:T(8,128)(2,1)S(1)} %partial.3), channel_id=1, source_target_pairs={{0,32},{32,64},{64,96},{96,128},{128,160},{160,192},{192,224},{224... | collective-permute-start | bytes 393224 | tf_op jit(solution)/shard_map/ppermute | solution.py:295
  26.6 4.4 %collective-permute-done.3 = bf16[512,128]{1,0:T(8,128)(2,1)S(1)} collective-permute-done((bf16[512,128]{1,0:T(8,128)(2,1)S(1)}, bf16[512,128]{1,0:T(8,128)(2,1)S(1)}, u32[]{:S(2)}, u32[]{:S(2)}) %collective-permute-start.3) | collective-permute-done | bytes 131104 | tf_op jit(solution)/shard_map/ppermute | solution.py:295
  31.0 4.6 %all_gather.29.both = bf16[1024,128]{1,0:T(8,128)(2,1)S(1)} all-gather(bf16[512,128]{1,0:T(8,128)(2,1)S(1)} %collective-permute-done.3), channel_id=1, replica_groups={{0,1},{2,3},{4,5},{6,7},{8,9},{10,11},{12,13},{14,15},{16,17},{18,19},{..., dimensions={0}, use_global_device_ids=true | all-gather | bytes 393216 | tf_op jit(solution)/shard_map/all_gather | solution.py:274
  35.9 2.0 %collective-permute-start.4 = (bf16[512,128]{1,0:T(8,128)(2,1)S(1)}, bf16[512,128]{1,0:T(8,128)(2,1)S(1)}, u32[]{:S(2)}, u32[]{:S(2)}) collective-permute-start(bf16[512,128]{1,0:T(8,128)(2,1)S(1)} %get-tuple-element.24.own), channel_id=1, source_target_pairs={{1,4},{3,6},{5,8},{7,10},{9,12},{11,14},{13,16},{15,18},{17,20},{1... | collective-permute-start | bytes 393224 | tf_op jit(solution)/shard_map/ppermute | solution.py:278
  37.8 2.4 %collective-permute-start.5 = (bf16[512,128]{1,0:T(8,128)(2,1)S(1)}, bf16[512,128]{1,0:T(8,128)(2,1)S(1)}, u32[]{:S(2)}, u32[]{:S(2)}) collective-permute-start(bf16[512,128]{1,0:T(8,128)(2,1)S(1)} %get-tuple-element.24.own), channel_id=1, source_target_pairs={{1,17},{3,19},{5,21},{7,23},{9,25},{11,27},{13,29},{15,31},{17,1},... | collective-permute-start | bytes 393224 | tf_op jit(solution)/shard_map/ppermute | solution.py:289
  40.3 5.5 %all_gather.30.beside = bf16[1024,128]{1,0:T(8,128)(2,1)S(1)} all-gather(bf16[512,128]{1,0:T(8,128)(2,1)S(1)} %get-tuple-element.24.own), channel_id=1, replica_groups={{1,2},{3,4},{5,6},{7,8},{9,10},{11,12},{13,14},{15,16},{17,18},{19,20},..., dimensions={0}, use_global_device_ids=true | all-gather | bytes 393216 | tf_op jit(solution)/shard_map/all_gather | solution.py:274
  45.8 1.2 %collective-permute-done.5.opposite = bf16[512,128]{1,0:T(8,128)(2,1)S(1)} collective-permute-done((bf16[512,128]{1,0:T(8,128)(2,1)S(1)}, bf16[512,128]{1,0:T(8,128)(2,1)S(1)}, u32[]{:S(2)}, u32[]{:S(2)}) %collective-permute-start.5) | collective-permute-done | bytes 131104 | tf_op jit(solution)/shard_map/ppermute | solution.py:289
  47.5 1.9 %collective-permute-start.6 = (bf16[512,128]{1,0:T(8,128)(2,1)S(1)}, bf16[512,128]{1,0:T(8,128)(2,1)S(1)}, u32[]{:S(2)}, u32[]{:S(2)}) collective-permute-start(bf16[512,128]{1,0:T(8,128)(2,1)S(1)} %partial.4), channel_id=1, source_target_pairs={{0,32},{32,64},{64,96},{96,128},{128,160},{160,192},{192,224},{224... | collective-permute-start | bytes 393224 | tf_op jit(solution)/shard_map/ppermute | solution.py:295
  49.4 5.0 %collective-permute-done.6 = bf16[512,128]{1,0:T(8,128)(2,1)S(1)} collective-permute-done((bf16[512,128]{1,0:T(8,128)(2,1)S(1)}, bf16[512,128]{1,0:T(8,128)(2,1)S(1)}, u32[]{:S(2)}, u32[]{:S(2)}) %collective-permute-start.6) | collective-permute-done | bytes 131104 | tf_op jit(solution)/shard_map/ppermute | solution.py:295
  54.4 4.5 %all_gather.31.both = bf16[1024,128]{1,0:T(8,128)(2,1)S(1)} all-gather(bf16[512,128]{1,0:T(8,128)(2,1)S(1)} %collective-permute-done.6), channel_id=1, replica_groups={{0,1},{2,3},{4,5},{6,7},{8,9},{10,11},{12,13},{14,15},{16,17},{18,19},{..., dimensions={0}, use_global_device_ids=true | all-gather | bytes 393216 | tf_op jit(solution)/shard_map/all_gather | solution.py:274
  59.2 1.9 %collective-permute-start.7 = (bf16[512,128]{1,0:T(8,128)(2,1)S(1)}, bf16[512,128]{1,0:T(8,128)(2,1)S(1)}, u32[]{:S(2)}, u32[]{:S(2)}) collective-permute-start(bf16[512,128]{1,0:T(8,128)(2,1)S(1)} %get-tuple-element.25.own), channel_id=1, source_target_pairs={{1,4},{3,6},{5,8},{7,10},{9,12},{11,14},{13,16},{15,18},{17,20},{1... | collective-permute-start | bytes 393224 | tf_op jit(solution)/shard_map/ppermute | solution.py:278
  61.1 4.6 %collective-permute-start.8 = (bf16[512,128]{1,0:T(8,128)(2,1)S(1)}, bf16[512,128]{1,0:T(8,128)(2,1)S(1)}, u32[]{:S(2)}, u32[]{:S(2)}) collective-permute-start(bf16[512,128]{1,0:T(8,128)(2,1)S(1)} %get-tuple-element.25.own), channel_id=1, source_target_pairs={{1,17},{3,19},{5,21},{7,23},{9,25},{11,27},{13,29},{15,31},{17,1},... | collective-permute-start | bytes 393224 | tf_op jit(solution)/shard_map/ppermute | solution.py:289
  65.7 5.4 %all_gather.32.beside = bf16[1024,128]{1,0:T(8,128)(2,1)S(1)} all-gather(bf16[512,128]{1,0:T(8,128)(2,1)S(1)} %get-tuple-element.25.own), channel_id=1, replica_groups={{1,2},{3,4},{5,6},{7,8},{9,10},{11,12},{13,14},{15,16},{17,18},{19,20},..., dimensions={0}, use_global_device_ids=true | all-gather | bytes 393216 | tf_op jit(solution)/shard_map/all_gather | solution.py:274
  71.1 0.5 partial.5
  71.5 1.9 %collective-permute-start.9 = (bf16[512,128]{1,0:T(8,128)(2,1)S(1)}, bf16[512,128]{1,0:T(8,128)(2,1)S(1)}, u32[]{:S(2)}, u32[]{:S(2)}) collective-permute-start(bf16[512,128]{1,0:T(8,128)(2,1)S(1)} %partial.5), channel_id=1, source_target_pairs={{0,32},{32,64},{64,96},{96,128},{128,160},{160,192},{192,224},{224... | collective-permute-start | bytes 393224 | tf_op jit(solution)/shard_map/ppermute | solution.py:295
  73.5 5.0 %collective-permute-done.9 = bf16[512,128]{1,0:T(8,128)(2,1)S(1)} collective-permute-done((bf16[512,128]{1,0:T(8,128)(2,1)S(1)}, bf16[512,128]{1,0:T(8,128)(2,1)S(1)}, u32[]{:S(2)}, u32[]{:S(2)}) %collective-permute-start.9) | collective-permute-done | bytes 131104 | tf_op jit(solution)/shard_map/ppermute | solution.py:295
  78.5 3.8 %all_gather.33.both = bf16[1024,128]{1,0:T(8,128)(2,1)S(1)} all-gather(bf16[512,128]{1,0:T(8,128)(2,1)S(1)} %collective-permute-done.9), channel_id=1, replica_groups={{0,1},{2,3},{4,5},{6,7},{8,9},{10,11},{12,13},{14,15},{16,17},{18,19},{..., dimensions={0}, use_global_device_ids=true | all-gather | bytes 393216 | tf_op jit(solution)/shard_map/all_gather | solution.py:274
  82.5 3.0 %collective-permute-start.10 = (bf16[512,128]{1,0:T(8,128)(2,1)S(1)}, bf16[512,128]{1,0:T(8,128)(2,1)S(1)}, u32[]{:S(2)}, u32[]{:S(2)}) collective-permute-start(bf16[512,128]{1,0:T(8,128)(2,1)S(1)} %get-tuple-element.26.own), channel_id=1, source_target_pairs={{1,4},{3,6},{5,8},{7,10},{9,12},{11,14},{13,16},{15,18},{17,20},{1... | collective-permute-start | bytes 393224 | tf_op jit(solution)/shard_map/ppermute | solution.py:278
  85.5 3.3 %collective-permute-start.11 = (bf16[512,128]{1,0:T(8,128)(2,1)S(1)}, bf16[512,128]{1,0:T(8,128)(2,1)S(1)}, u32[]{:S(2)}, u32[]{:S(2)}) collective-permute-start(bf16[512,128]{1,0:T(8,128)(2,1)S(1)} %get-tuple-element.26.own), channel_id=1, source_target_pairs={{1,17},{3,19},{5,21},{7,23},{9,25},{11,27},{13,29},{15,31},{17,1},... | collective-permute-start | bytes 393224 | tf_op jit(solution)/shard_map/ppermute | solution.py:289
  88.8 5.4 %all_gather.34.beside = bf16[1024,128]{1,0:T(8,128)(2,1)S(1)} all-gather(bf16[512,128]{1,0:T(8,128)(2,1)S(1)} %get-tuple-element.26.own), channel_id=1, replica_groups={{1,2},{3,4},{5,6},{7,8},{9,10},{11,12},{13,14},{15,16},{17,18},{19,20},..., dimensions={0}, use_global_device_ids=true | all-gather | bytes 393216 | tf_op jit(solution)/shard_map/all_gather | solution.py:274
  94.2 1.0 %collective-permute-done.11.opposite = bf16[512,128]{1,0:T(8,128)(2,1)S(1)} collective-permute-done((bf16[512,128]{1,0:T(8,128)(2,1)S(1)}, bf16[512,128]{1,0:T(8,128)(2,1)S(1)}, u32[]{:S(2)}, u32[]{:S(2)}) %collective-permute-start.11) | collective-permute-done | bytes 131104 | tf_op jit(solution)/shard_map/ppermute | solution.py:289
  95.2 1.0 %last.1 = (f32[256,128]{1,0:T(8,128)S(1)}, bf16[256,128]{1,0:T(8,128)(2,1)S(1)}, f32[4,256,128]{2,1,0:T(8,128)}) custom-call(bf16[5,256,256]{2,1,0:T(8,128)(2,1)S(1)} %get-tuple-element.21.kept, bf16[2048,256]{1,0:T(8,128)(2,1)S(1)} %collective-permute-done.given, bf16[512,128]{1,0:T(8,128)(2,1)S(1)} %get-tuple-element.26.own, ...), custom_call_target="tpu_custom_call" | custom-call | tf_op jit(solution)/shard_map/last/pallas_call | solution.py:232
  96.2 3.4 %all_gather.35.both = bf16[512,128]{1,0:T(8,128)(2,1)S(1)} all-gather(bf16[256,128]{1,0:T(8,128)(2,1)S(1)} %get-tuple-element.33), channel_id=1, replica_groups={{0,1},{2,3},{4,5},{6,7},{8,9},{10,11},{12,13},{14,15},{16,17},{18,19},{..., dimensions={0}, use_global_device_ids=true | all-gather | bytes 196608 | tf_op jit(solution)/shard_map/all_gather | solution.py:274
  99.6 0.7 carry.1
  (15 shorter events, 1.2 us)
Async XLA Ops:
  6.1 17.5 %collective-permute-start = (bf16[2048,256]{1,0:T(8,128)(2,1)S(1)}, bf16[2048,256]{1,0:T(8,128)(2,1)S(1)}, u32[]{:S(2)}, u32[]{:S(2)}) collective-permute-start(bf16[2048,256]{1,0:T(8,128)(2,1)S(1)} %get-tuple-element.22), channel_id=1, source_target_pairs={{0,1},{2,3},{4,5},{6,7},{8,9},{10,11},{12,13},{14,15},{16,17},{18,... | collective-permute-start | bytes 3145736 | tf_op jit(solution)/shard_map/ppermute | solution.py:278
  8.9 14.6 %collective-permute-start.1 = (bf16[512,128]{1,0:T(8,128)(2,1)S(1)}, bf16[512,128]{1,0:T(8,128)(2,1)S(1)}, u32[]{:S(2)}, u32[]{:S(2)}) collective-permute-start(bf16[512,128]{1,0:T(8,128)(2,1)S(1)} %get-tuple-element.23.own), channel_id=1, source_target_pairs={{1,4},{3,6},{5,8},{7,10},{9,12},{11,14},{13,16},{15,18},{17,20},{1... | collective-permute-start | bytes 393224 | tf_op jit(solution)/shard_map/ppermute | solution.py:278
  14.0 9.6 %collective-permute-start.2 = (bf16[512,128]{1,0:T(8,128)(2,1)S(1)}, bf16[512,128]{1,0:T(8,128)(2,1)S(1)}, u32[]{:S(2)}, u32[]{:S(2)}) collective-permute-start(bf16[512,128]{1,0:T(8,128)(2,1)S(1)} %get-tuple-element.23.own), channel_id=1, source_target_pairs={{1,17},{3,19},{5,21},{7,23},{9,25},{11,27},{13,29},{15,31},{17,1},... | collective-permute-start | bytes 393224 | tf_op jit(solution)/shard_map/ppermute | solution.py:289
  24.1 6.9 %collective-permute-start.3 = (bf16[512,128]{1,0:T(8,128)(2,1)S(1)}, bf16[512,128]{1,0:T(8,128)(2,1)S(1)}, u32[]{:S(2)}, u32[]{:S(2)}) collective-permute-start(bf16[512,128]{1,0:T(8,128)(2,1)S(1)} %partial.3), channel_id=1, source_target_pairs={{0,32},{32,64},{64,96},{96,128},{128,160},{160,192},{192,224},{224... | collective-permute-start | bytes 393224 | tf_op jit(solution)/shard_map/ppermute | solution.py:295
  35.9 10.0 %collective-permute-start.4 = (bf16[512,128]{1,0:T(8,128)(2,1)S(1)}, bf16[512,128]{1,0:T(8,128)(2,1)S(1)}, u32[]{:S(2)}, u32[]{:S(2)}) collective-permute-start(bf16[512,128]{1,0:T(8,128)(2,1)S(1)} %get-tuple-element.24.own), channel_id=1, source_target_pairs={{1,4},{3,6},{5,8},{7,10},{9,12},{11,14},{13,16},{15,18},{17,20},{1... | collective-permute-start | bytes 393224 | tf_op jit(solution)/shard_map/ppermute | solution.py:278
  37.8 9.2 %collective-permute-start.5 = (bf16[512,128]{1,0:T(8,128)(2,1)S(1)}, bf16[512,128]{1,0:T(8,128)(2,1)S(1)}, u32[]{:S(2)}, u32[]{:S(2)}) collective-permute-start(bf16[512,128]{1,0:T(8,128)(2,1)S(1)} %get-tuple-element.24.own), channel_id=1, source_target_pairs={{1,17},{3,19},{5,21},{7,23},{9,25},{11,27},{13,29},{15,31},{17,1},... | collective-permute-start | bytes 393224 | tf_op jit(solution)/shard_map/ppermute | solution.py:289
  47.5 6.9 %collective-permute-start.6 = (bf16[512,128]{1,0:T(8,128)(2,1)S(1)}, bf16[512,128]{1,0:T(8,128)(2,1)S(1)}, u32[]{:S(2)}, u32[]{:S(2)}) collective-permute-start(bf16[512,128]{1,0:T(8,128)(2,1)S(1)} %partial.4), channel_id=1, source_target_pairs={{0,32},{32,64},{64,96},{96,128},{128,160},{160,192},{192,224},{224... | collective-permute-start | bytes 393224 | tf_op jit(solution)/shard_map/ppermute | solution.py:295
  59.2 11.9 %collective-permute-start.7 = (bf16[512,128]{1,0:T(8,128)(2,1)S(1)}, bf16[512,128]{1,0:T(8,128)(2,1)S(1)}, u32[]{:S(2)}, u32[]{:S(2)}) collective-permute-start(bf16[512,128]{1,0:T(8,128)(2,1)S(1)} %get-tuple-element.25.own), channel_id=1, source_target_pairs={{1,4},{3,6},{5,8},{7,10},{9,12},{11,14},{13,16},{15,18},{17,20},{1... | collective-permute-start | bytes 393224 | tf_op jit(solution)/shard_map/ppermute | solution.py:278
  61.1 9.9 %collective-permute-start.8 = (bf16[512,128]{1,0:T(8,128)(2,1)S(1)}, bf16[512,128]{1,0:T(8,128)(2,1)S(1)}, u32[]{:S(2)}, u32[]{:S(2)}) collective-permute-start(bf16[512,128]{1,0:T(8,128)(2,1)S(1)} %get-tuple-element.25.own), channel_id=1, source_target_pairs={{1,17},{3,19},{5,21},{7,23},{9,25},{11,27},{13,29},{15,31},{17,1},... | collective-permute-start | bytes 393224 | tf_op jit(solution)/shard_map/ppermute | solution.py:289
  71.5 6.9 %collective-permute-start.9 = (bf16[512,128]{1,0:T(8,128)(2,1)S(1)}, bf16[512,128]{1,0:T(8,128)(2,1)S(1)}, u32[]{:S(2)}, u32[]{:S(2)}) collective-permute-start(bf16[512,128]{1,0:T(8,128)(2,1)S(1)} %partial.5), channel_id=1, source_target_pairs={{0,32},{32,64},{64,96},{96,128},{128,160},{160,192},{192,224},{224... | collective-permute-start | bytes 393224 | tf_op jit(solution)/shard_map/ppermute | solution.py:295
  82.5 11.7 %collective-permute-start.10 = (bf16[512,128]{1,0:T(8,128)(2,1)S(1)}, bf16[512,128]{1,0:T(8,128)(2,1)S(1)}, u32[]{:S(2)}, u32[]{:S(2)}) collective-permute-start(bf16[512,128]{1,0:T(8,128)(2,1)S(1)} %get-tuple-element.26.own), channel_id=1, source_target_pairs={{1,4},{3,6},{5,8},{7,10},{9,12},{11,14},{13,16},{15,18},{17,20},{1... | collective-permute-start | bytes 393224 | tf_op jit(solution)/shard_map/ppermute | solution.py:278
  85.5 9.7 %collective-permute-start.11 = (bf16[512,128]{1,0:T(8,128)(2,1)S(1)}, bf16[512,128]{1,0:T(8,128)(2,1)S(1)}, u32[]{:S(2)}, u32[]{:S(2)}) collective-permute-start(bf16[512,128]{1,0:T(8,128)(2,1)S(1)} %get-tuple-element.26.own), channel_id=1, source_target_pairs={{1,17},{3,19},{5,21},{7,23},{9,25},{11,27},{13,29},{15,31},{17,1},... | collective-permute-start | bytes 393224 | tf_op jit(solution)/shard_map/ppermute | solution.py:289

commit v11 on v10

--- a/solution.py
+++ b/solution.py
@@ -174,18 +174,14 @@
 
 
 def products(kept, given, own, beside, third, opposite):
-    block = third.shape[0]
-    near = lax.rem(lax.axis_index("blk"), 2) * (2 * block)
-
-    def part(at):
-        return beside[pl.ds(pl.multiple_of(at, block), block), :]
-
-    odd_one, same_one = part(near), part(near + block)
+    block = beside.shape[0] // 2
+    there = pl.multiple_of(lax.rem(lax.axis_index("blk"), 2) * block, block)
+    odd_one, same_one = beside[0:block], beside[block:]
     self_one = own[0:block]
     value = mm(kept[3], self_one)
     value += mm(kept[1], same_one)
     value += mm(kept[2], odd_one)
-    value += mm(kept[0], third[...])
+    value += mm(kept[0], third[pl.ds(there, block), :])
     value += mm(kept[4], opposite[0:block])
     other = mm(given[0:block, :], same_one)
     other += mm(given[block : 2 * block, :], odd_one)
@@ -195,7 +191,7 @@
 
 
 def partial_kernel(kept, given, own, beside, third, opposite, sums):
-    block = third.shape[0]
+    block = beside.shape[0] // 2
     value, other = products(kept, given, own, beside, third, opposite)
     sums[0:block] = value.astype(BF16)
     sums[block:] = other.astype(BF16)
@@ -215,7 +211,7 @@
 
 
 def partial_sums(operands):
-    block, columns = operands[4].shape
+    block, columns = operands[4].shape[0] // 2, operands[4].shape[1]
     return pl.pallas_call(
         partial_kernel,
         out_shape=jax.ShapeDtypeStruct((2 * block, columns), BF16),
@@ -227,7 +223,7 @@
 
 
 def last_sums(operands, solved):
-    block, columns = operands[4].shape
+    block, columns = operands[4].shape[0] // 2, operands[4].shape[1]
     ticks = len(solved)
     return pl.pallas_call(
         functools.partial(last_kernel, ticks),
@@ -285,9 +281,9 @@
             chip = paired(own, chip_pairs)
             kept, handed, own = combine(around, chip, sources, counts, factor_blocks, inverse, right)
             given = swapped(handed, chip_pairs)
-        third = swapped(own, third_pairs)[0:block]
+        beside = swapped(own, next_pairs)
         opposite = lax.ppermute(own, "blk", seconds)
-        beside = paired(own, next_pairs)
+        third = paired(own[0:block], third_pairs)
         operands = [kept, given, own, beside, third, opposite]
         if tick + 1 == ticks:
             exact, crossing, outputs = last_sums(operands, finished)

time: 101 us -> 100 us (0.990)
  blocking collectives: 40.1 us -> 44.8 us
  starting transfers between devices: 35.6 us -> 32 us
  waiting for transfers between devices: 16.6 us -> 14.9 us
    all_gather x9, blocking collectives: 40.1 us -> 44.8 us  [paired(): lax.all_gather(value, 'blk', axis=0, tiled=True, axis_index_groups=pairs)]
    ppermute x5, starting transfers between devices: 14.8 us -> 11.3 us  [swapped(): return lax.ppermute(value, 'blk', partner)]
    ppermute x4, waiting for transfers between devices: 2.24 us -> 0.46 us  [shards(): opposite = lax.ppermute(own, 'blk', seconds)]
  transfers between devices with their start and end apart: 12 -> 12, of which waited for: 5 -> 4; matrix products, arithmetic and copies ran while one was open for 0% -> 0% of each run, Pallas kernels for 0% -> 0%
where the time goes in v11:
time: 100 us; the launch traced here: 99.8 us
  blocking collectives  44.8 us (45%)
  starting transfers between devices  32 us (32%)
  waiting for transfers between devices  14.9 us (15%)
  Pallas kernels  6.59 us (7%)
  between operations  1.48 us (1%)
    all_gather x9, blocking collectives, paired(): lax.all_gather(value, 'blk', axis=0, tiled=True, axis_index_groups=pairs)  44.8 us
    ppermute x4, starting transfers between devices, shards(): opposite = lax.ppermute(own, 'blk', seconds)  14.5 us
    ppermute x3, waiting for transfers between devices, shards(): lax.ppermute(partial_sums(operands), 'grp', [(g, g + 1) for g in range(gr...  14.4 us
    ppermute x5, starting transfers between devices, swapped(): return lax.ppermute(value, 'blk', partner)  11.3 us
    ppermute x3, starting transfers between devices, shards(): lax.ppermute(partial_sums(operands), 'grp', [(g, g + 1) for g in range(gr...  6.3 us
  transfers between devices with their start and end apart: 12, of which 4 were waited for; matrix products, arithmetic and copies ran while one was open for 0% of the time, Pallas kernels for 0%

profile of v11, /device:TPU:385, one launch (start us, length us, event | category | flops | bytes accessed | tf_op | source)
XLA Modules:
  0.0 99.8 jit_solution(15523663803475719607)
XLA Ops:
  0.6 1.2 %first.1 = (f32[256,128]{1,0:T(8,128)S(1)}, bf16[256,128]{1,0:T(8,128)(2,1)S(1)}, bf16[256,256]{1,0:T(8,128)(2,1)S(1)}, f32[3,256,128]{2,1,0:T(8,128)S(1)}) custom-call(f32[4,256,128]{2,1,0:T(8,128)} %right.1, f32[256,128]{1,0:T(8,128)} %incoming.1, bf16[256,256]{1,0:T(8,128)(2,1)} %inverse.1), custom_call_target="tpu_custom_call" | custom-call | tf_op jit(solution)/shard_map/first/pallas_call | solution.py:120
  1.9 2.2 %all_gather.27.chip = bf16[512,128]{1,0:T(8,128)(2,1)S(1)} all-gather(bf16[256,128]{1,0:T(8,128)(2,1)S(1)} %get-tuple-element.20), channel_id=1, replica_groups={{0,1},{2,3},{4,5},{6,7},{8,9},{10,11},{12,13},{14,15},{16,17},{18,19},{..., dimensions={0}, use_global_device_ids=true | all-gather | bytes 196608 | tf_op jit(solution)/shard_map/all_gather | solution.py:270
  4.8 1.6 %combine.1 = (bf16[5,256,256]{2,1,0:T(8,128)(2,1)S(1)}, bf16[2048,256]{1,0:T(8,128)(2,1)S(1)}, bf16[512,128]{1,0:T(8,128)(2,1)S(1)}) custom-call(s32[1]{0:T(128)S(6)} %copy.8.count, s32[1,24]{1,0:T(1,128)} %source_list.1, bf16[1,24,256,256]{3,2,1,0:T(8,128)(2,1)} %blocks.1, bf16[256,256]{1,0:T(8,128)(2,1)S(1)} %get-tuple-element.18.inverse, ...), custom_call_target="tpu_custom_call" | custom-call | flops 4000000 | bytes 10000000 | tf_op jit(solution)/shard_map/combine/pallas_call | solution.py:79
  6.3 2.2 %collective-permute-start = (bf16[2048,256]{1,0:T(8,128)(2,1)S(1)}, bf16[2048,256]{1,0:T(8,128)(2,1)S(1)}, u32[]{:S(2)}, u32[]{:S(2)}) collective-permute-start(bf16[2048,256]{1,0:T(8,128)(2,1)S(1)} %get-tuple-element.22), channel_id=1, source_target_pairs={{0,1},{2,3},{4,5},{6,7},{8,9},{10,11},{12,13},{14,15},{16,17},{18,... | collective-permute-start | bytes 3145736 | tf_op jit(solution)/shard_map/ppermute | solution.py:274
  8.5 3.1 %collective-permute-start.1 = (bf16[512,128]{1,0:T(8,128)(2,1)S(1)}, bf16[512,128]{1,0:T(8,128)(2,1)S(1)}, u32[]{:S(2)}, u32[]{:S(2)}) collective-permute-start(bf16[512,128]{1,0:T(8,128)(2,1)S(1)} %get-tuple-element.23.own), channel_id=1, source_target_pairs={{1,2},{3,4},{5,6},{7,8},{9,10},{11,12},{13,14},{15,16},{17,18},{19... | collective-permute-start | bytes 393224 | tf_op jit(solution)/shard_map/ppermute | solution.py:274
  11.6 5.1 %collective-permute-start.2 = (bf16[512,128]{1,0:T(8,128)(2,1)S(1)}, bf16[512,128]{1,0:T(8,128)(2,1)S(1)}, u32[]{:S(2)}, u32[]{:S(2)}) collective-permute-start(bf16[512,128]{1,0:T(8,128)(2,1)S(1)} %get-tuple-element.23.own), channel_id=1, source_target_pairs={{1,17},{3,19},{5,21},{7,23},{9,25},{11,27},{13,29},{15,31},{17,1},... | collective-permute-start | bytes 393224 | tf_op jit(solution)/shard_map/ppermute | solution.py:285
  16.7 6.2 %all_gather.28.third = bf16[512,128]{1,0:T(8,128)(2,1)S(1)} all-gather(bf16[256,128]{1,0:T(8,128)(2,1)S(1)} %slice.12), channel_id=1, replica_groups={{1,4},{3,6},{5,8},{7,10},{9,12},{11,14},{13,16},{15,18},{17,20},{19,22}..., dimensions={0}, use_global_device_ids=true | all-gather | bytes 196608 | tf_op jit(solution)/shard_map/all_gather | solution.py:270
  22.9 0.5 partial.3
  23.4 2.5 %collective-permute-start.3 = (bf16[512,128]{1,0:T(8,128)(2,1)S(1)}, bf16[512,128]{1,0:T(8,128)(2,1)S(1)}, u32[]{:S(2)}, u32[]{:S(2)}) collective-permute-start(bf16[512,128]{1,0:T(8,128)(2,1)S(1)} %partial.3), channel_id=1, source_target_pairs={{0,32},{32,64},{64,96},{96,128},{128,160},{160,192},{192,224},{224... | collective-permute-start | bytes 393224 | tf_op jit(solution)/shard_map/ppermute | solution.py:291
  25.8 4.5 %collective-permute-done.3 = bf16[512,128]{1,0:T(8,128)(2,1)S(1)} collective-permute-done((bf16[512,128]{1,0:T(8,128)(2,1)S(1)}, bf16[512,128]{1,0:T(8,128)(2,1)S(1)}, u32[]{:S(2)}, u32[]{:S(2)}) %collective-permute-start.3) | collective-permute-done | bytes 131104 | tf_op jit(solution)/shard_map/ppermute | solution.py:291
  30.3 4.8 %all_gather.29.both = bf16[1024,128]{1,0:T(8,128)(2,1)S(1)} all-gather(bf16[512,128]{1,0:T(8,128)(2,1)S(1)} %collective-permute-done.3), channel_id=1, replica_groups={{0,1},{2,3},{4,5},{6,7},{8,9},{10,11},{12,13},{14,15},{16,17},{18,19},{..., dimensions={0}, use_global_device_ids=true | all-gather | bytes 393216 | tf_op jit(solution)/shard_map/all_gather | solution.py:270
  35.3 2.1 %collective-permute-start.4 = (bf16[512,128]{1,0:T(8,128)(2,1)S(1)}, bf16[512,128]{1,0:T(8,128)(2,1)S(1)}, u32[]{:S(2)}, u32[]{:S(2)}) collective-permute-start(bf16[512,128]{1,0:T(8,128)(2,1)S(1)} %get-tuple-element.24.own), channel_id=1, source_target_pairs={{1,2},{3,4},{5,6},{7,8},{9,10},{11,12},{13,14},{15,16},{17,18},{19... | collective-permute-start | bytes 393224 | tf_op jit(solution)/shard_map/ppermute | solution.py:274
  37.4 2.2 %collective-permute-start.5 = (bf16[512,128]{1,0:T(8,128)(2,1)S(1)}, bf16[512,128]{1,0:T(8,128)(2,1)S(1)}, u32[]{:S(2)}, u32[]{:S(2)}) collective-permute-start(bf16[512,128]{1,0:T(8,128)(2,1)S(1)} %get-tuple-element.24.own), channel_id=1, source_target_pairs={{1,17},{3,19},{5,21},{7,23},{9,25},{11,27},{13,29},{15,31},{17,1},... | collective-permute-start | bytes 393224 | tf_op jit(solution)/shard_map/ppermute | solution.py:285
  39.7 5.9 %all_gather.30.third = bf16[512,128]{1,0:T(8,128)(2,1)S(1)} all-gather(bf16[256,128]{1,0:T(8,128)(2,1)S(1)} %slice.13), channel_id=1, replica_groups={{1,4},{3,6},{5,8},{7,10},{9,12},{11,14},{13,16},{15,18},{17,20},{19,22}..., dimensions={0}, use_global_device_ids=true | all-gather | bytes 196608 | tf_op jit(solution)/shard_map/all_gather | solution.py:270
  45.6 0.4 collective-permute-done.5.opposite
  46.0 0.5 partial.4
  46.5 1.9 %collective-permute-start.6 = (bf16[512,128]{1,0:T(8,128)(2,1)S(1)}, bf16[512,128]{1,0:T(8,128)(2,1)S(1)}, u32[]{:S(2)}, u32[]{:S(2)}) collective-permute-start(bf16[512,128]{1,0:T(8,128)(2,1)S(1)} %partial.4), channel_id=1, source_target_pairs={{0,32},{32,64},{64,96},{96,128},{128,160},{160,192},{192,224},{224... | collective-permute-start | bytes 393224 | tf_op jit(solution)/shard_map/ppermute | solution.py:291
  48.4 5.0 %collective-permute-done.6 = bf16[512,128]{1,0:T(8,128)(2,1)S(1)} collective-permute-done((bf16[512,128]{1,0:T(8,128)(2,1)S(1)}, bf16[512,128]{1,0:T(8,128)(2,1)S(1)}, u32[]{:S(2)}, u32[]{:S(2)}) %collective-permute-start.6) | collective-permute-done | bytes 131104 | tf_op jit(solution)/shard_map/ppermute | solution.py:291
  53.4 5.4 %all_gather.31.both = bf16[1024,128]{1,0:T(8,128)(2,1)S(1)} all-gather(bf16[512,128]{1,0:T(8,128)(2,1)S(1)} %collective-permute-done.6), channel_id=1, replica_groups={{0,1},{2,3},{4,5},{6,7},{8,9},{10,11},{12,13},{14,15},{16,17},{18,19},{..., dimensions={0}, use_global_device_ids=true | all-gather | bytes 393216 | tf_op jit(solution)/shard_map/all_gather | solution.py:270
  59.1 1.9 %collective-permute-start.7 = (bf16[512,128]{1,0:T(8,128)(2,1)S(1)}, bf16[512,128]{1,0:T(8,128)(2,1)S(1)}, u32[]{:S(2)}, u32[]{:S(2)}) collective-permute-start(bf16[512,128]{1,0:T(8,128)(2,1)S(1)} %get-tuple-element.25.own), channel_id=1, source_target_pairs={{1,2},{3,4},{5,6},{7,8},{9,10},{11,12},{13,14},{15,16},{17,18},{19... | collective-permute-start | bytes 393224 | tf_op jit(solution)/shard_map/ppermute | solution.py:274
  61.0 4.0 %collective-permute-start.8 = (bf16[512,128]{1,0:T(8,128)(2,1)S(1)}, bf16[512,128]{1,0:T(8,128)(2,1)S(1)}, u32[]{:S(2)}, u32[]{:S(2)}) collective-permute-start(bf16[512,128]{1,0:T(8,128)(2,1)S(1)} %get-tuple-element.25.own), channel_id=1, source_target_pairs={{1,17},{3,19},{5,21},{7,23},{9,25},{11,27},{13,29},{15,31},{17,1},... | collective-permute-start | bytes 393224 | tf_op jit(solution)/shard_map/ppermute | solution.py:285
  65.1 6.2 %all_gather.32.third = bf16[512,128]{1,0:T(8,128)(2,1)S(1)} all-gather(bf16[256,128]{1,0:T(8,128)(2,1)S(1)} %slice.14), channel_id=1, replica_groups={{1,4},{3,6},{5,8},{7,10},{9,12},{11,14},{13,16},{15,18},{17,20},{19,22}..., dimensions={0}, use_global_device_ids=true | all-gather | bytes 196608 | tf_op jit(solution)/shard_map/all_gather | solution.py:270
  71.2 0.5 partial.5
  71.7 1.9 %collective-permute-start.9 = (bf16[512,128]{1,0:T(8,128)(2,1)S(1)}, bf16[512,128]{1,0:T(8,128)(2,1)S(1)}, u32[]{:S(2)}, u32[]{:S(2)}) collective-permute-start(bf16[512,128]{1,0:T(8,128)(2,1)S(1)} %partial.5), channel_id=1, source_target_pairs={{0,32},{32,64},{64,96},{96,128},{128,160},{160,192},{192,224},{224... | collective-permute-start | bytes 393224 | tf_op jit(solution)/shard_map/ppermute | solution.py:291
  73.6 5.0 %collective-permute-done.9 = bf16[512,128]{1,0:T(8,128)(2,1)S(1)} collective-permute-done((bf16[512,128]{1,0:T(8,128)(2,1)S(1)}, bf16[512,128]{1,0:T(8,128)(2,1)S(1)}, u32[]{:S(2)}, u32[]{:S(2)}) %collective-permute-start.9) | collective-permute-done | bytes 131104 | tf_op jit(solution)/shard_map/ppermute | solution.py:291
  78.6 4.4 %all_gather.33.both = bf16[1024,128]{1,0:T(8,128)(2,1)S(1)} all-gather(bf16[512,128]{1,0:T(8,128)(2,1)S(1)} %collective-permute-done.9), channel_id=1, replica_groups={{0,1},{2,3},{4,5},{6,7},{8,9},{10,11},{12,13},{14,15},{16,17},{18,19},{..., dimensions={0}, use_global_device_ids=true | all-gather | bytes 393216 | tf_op jit(solution)/shard_map/all_gather | solution.py:270
  83.3 1.9 %collective-permute-start.10 = (bf16[512,128]{1,0:T(8,128)(2,1)S(1)}, bf16[512,128]{1,0:T(8,128)(2,1)S(1)}, u32[]{:S(2)}, u32[]{:S(2)}) collective-permute-start(bf16[512,128]{1,0:T(8,128)(2,1)S(1)} %get-tuple-element.26.own), channel_id=1, source_target_pairs={{1,2},{3,4},{5,6},{7,8},{9,10},{11,12},{13,14},{15,16},{17,18},{19... | collective-permute-start | bytes 393224 | tf_op jit(solution)/shard_map/ppermute | solution.py:274
  85.3 3.1 %collective-permute-start.11 = (bf16[512,128]{1,0:T(8,128)(2,1)S(1)}, bf16[512,128]{1,0:T(8,128)(2,1)S(1)}, u32[]{:S(2)}, u32[]{:S(2)}) collective-permute-start(bf16[512,128]{1,0:T(8,128)(2,1)S(1)} %get-tuple-element.26.own), channel_id=1, source_target_pairs={{1,17},{3,19},{5,21},{7,23},{9,25},{11,27},{13,29},{15,31},{17,1},... | collective-permute-start | bytes 393224 | tf_op jit(solution)/shard_map/ppermute | solution.py:285
  88.4 6.2 %all_gather.34.third = bf16[512,128]{1,0:T(8,128)(2,1)S(1)} all-gather(bf16[256,128]{1,0:T(8,128)(2,1)S(1)} %slice.15), channel_id=1, replica_groups={{1,4},{3,6},{5,8},{7,10},{9,12},{11,14},{13,16},{15,18},{17,20},{19,22}..., dimensions={0}, use_global_device_ids=true | all-gather | bytes 196608 | tf_op jit(solution)/shard_map/all_gather | solution.py:270
  94.6 1.0 %last.1 = (f32[256,128]{1,0:T(8,128)S(1)}, bf16[256,128]{1,0:T(8,128)(2,1)S(1)}, f32[4,256,128]{2,1,0:T(8,128)}) custom-call(bf16[5,256,256]{2,1,0:T(8,128)(2,1)S(1)} %get-tuple-element.21.kept, bf16[2048,256]{1,0:T(8,128)(2,1)S(1)} %collective-permute-done.given, bf16[512,128]{1,0:T(8,128)(2,1)S(1)} %get-tuple-element.26.own, ...), custom_call_target="tpu_custom_call" | custom-call | tf_op jit(solution)/shard_map/last/pallas_call | solution.py:228
  95.6 3.5 %all_gather.35.both = bf16[512,128]{1,0:T(8,128)(2,1)S(1)} all-gather(bf16[256,128]{1,0:T(8,128)(2,1)S(1)} %get-tuple-element.33), channel_id=1, replica_groups={{0,1},{2,3},{4,5},{6,7},{8,9},{10,11},{12,13},{14,15},{16,17},{18,19},{..., dimensions={0}, use_global_device_ids=true | all-gather | bytes 196608 | tf_op jit(solution)/shard_map/all_gather | solution.py:270
  99.1 0.7 carry.1
  (15 shorter events, 0.8 us)
Async XLA Ops:
  6.3 16.6 %collective-permute-start = (bf16[2048,256]{1,0:T(8,128)(2,1)S(1)}, bf16[2048,256]{1,0:T(8,128)(2,1)S(1)}, u32[]{:S(2)}, u32[]{:S(2)}) collective-permute-start(bf16[2048,256]{1,0:T(8,128)(2,1)S(1)} %get-tuple-element.22), channel_id=1, source_target_pairs={{0,1},{2,3},{4,5},{6,7},{8,9},{10,11},{12,13},{14,15},{16,17},{18,... | collective-permute-start | bytes 3145736 | tf_op jit(solution)/shard_map/ppermute | solution.py:274
  8.5 14.4 %collective-permute-start.1 = (bf16[512,128]{1,0:T(8,128)(2,1)S(1)}, bf16[512,128]{1,0:T(8,128)(2,1)S(1)}, u32[]{:S(2)}, u32[]{:S(2)}) collective-permute-start(bf16[512,128]{1,0:T(8,128)(2,1)S(1)} %get-tuple-element.23.own), channel_id=1, source_target_pairs={{1,2},{3,4},{5,6},{7,8},{9,10},{11,12},{13,14},{15,16},{17,18},{19... | collective-permute-start | bytes 393224 | tf_op jit(solution)/shard_map/ppermute | solution.py:274
  11.6 11.3 %collective-permute-start.2 = (bf16[512,128]{1,0:T(8,128)(2,1)S(1)}, bf16[512,128]{1,0:T(8,128)(2,1)S(1)}, u32[]{:S(2)}, u32[]{:S(2)}) collective-permute-start(bf16[512,128]{1,0:T(8,128)(2,1)S(1)} %get-tuple-element.23.own), channel_id=1, source_target_pairs={{1,17},{3,19},{5,21},{7,23},{9,25},{11,27},{13,29},{15,31},{17,1},... | collective-permute-start | bytes 393224 | tf_op jit(solution)/shard_map/ppermute | solution.py:285
  23.4 6.9 %collective-permute-start.3 = (bf16[512,128]{1,0:T(8,128)(2,1)S(1)}, bf16[512,128]{1,0:T(8,128)(2,1)S(1)}, u32[]{:S(2)}, u32[]{:S(2)}) collective-permute-start(bf16[512,128]{1,0:T(8,128)(2,1)S(1)} %partial.3), channel_id=1, source_target_pairs={{0,32},{32,64},{64,96},{96,128},{128,160},{160,192},{192,224},{224... | collective-permute-start | bytes 393224 | tf_op jit(solution)/shard_map/ppermute | solution.py:291
  35.3 10.2 %collective-permute-start.4 = (bf16[512,128]{1,0:T(8,128)(2,1)S(1)}, bf16[512,128]{1,0:T(8,128)(2,1)S(1)}, u32[]{:S(2)}, u32[]{:S(2)}) collective-permute-start(bf16[512,128]{1,0:T(8,128)(2,1)S(1)} %get-tuple-element.24.own), channel_id=1, source_target_pairs={{1,2},{3,4},{5,6},{7,8},{9,10},{11,12},{13,14},{15,16},{17,18},{19... | collective-permute-start | bytes 393224 | tf_op jit(solution)/shard_map/ppermute | solution.py:274
  37.4 8.6 %collective-permute-start.5 = (bf16[512,128]{1,0:T(8,128)(2,1)S(1)}, bf16[512,128]{1,0:T(8,128)(2,1)S(1)}, u32[]{:S(2)}, u32[]{:S(2)}) collective-permute-start(bf16[512,128]{1,0:T(8,128)(2,1)S(1)} %get-tuple-element.24.own), channel_id=1, source_target_pairs={{1,17},{3,19},{5,21},{7,23},{9,25},{11,27},{13,29},{15,31},{17,1},... | collective-permute-start | bytes 393224 | tf_op jit(solution)/shard_map/ppermute | solution.py:285
  46.5 6.9 %collective-permute-start.6 = (bf16[512,128]{1,0:T(8,128)(2,1)S(1)}, bf16[512,128]{1,0:T(8,128)(2,1)S(1)}, u32[]{:S(2)}, u32[]{:S(2)}) collective-permute-start(bf16[512,128]{1,0:T(8,128)(2,1)S(1)} %partial.4), channel_id=1, source_target_pairs={{0,32},{32,64},{64,96},{96,128},{128,160},{160,192},{192,224},{224... | collective-permute-start | bytes 393224 | tf_op jit(solution)/shard_map/ppermute | solution.py:291
  59.1 12.2 %collective-permute-start.7 = (bf16[512,128]{1,0:T(8,128)(2,1)S(1)}, bf16[512,128]{1,0:T(8,128)(2,1)S(1)}, u32[]{:S(2)}, u32[]{:S(2)}) collective-permute-start(bf16[512,128]{1,0:T(8,128)(2,1)S(1)} %get-tuple-element.25.own), channel_id=1, source_target_pairs={{1,2},{3,4},{5,6},{7,8},{9,10},{11,12},{13,14},{15,16},{17,18},{19... | collective-permute-start | bytes 393224 | tf_op jit(solution)/shard_map/ppermute | solution.py:274
  61.0 10.2 %collective-permute-start.8 = (bf16[512,128]{1,0:T(8,128)(2,1)S(1)}, bf16[512,128]{1,0:T(8,128)(2,1)S(1)}, u32[]{:S(2)}, u32[]{:S(2)}) collective-permute-start(bf16[512,128]{1,0:T(8,128)(2,1)S(1)} %get-tuple-element.25.own), channel_id=1, source_target_pairs={{1,17},{3,19},{5,21},{7,23},{9,25},{11,27},{13,29},{15,31},{17,1},... | collective-permute-start | bytes 393224 | tf_op jit(solution)/shard_map/ppermute | solution.py:285
  71.7 6.9 %collective-permute-start.9 = (bf16[512,128]{1,0:T(8,128)(2,1)S(1)}, bf16[512,128]{1,0:T(8,128)(2,1)S(1)}, u32[]{:S(2)}, u32[]{:S(2)}) collective-permute-start(bf16[512,128]{1,0:T(8,128)(2,1)S(1)} %partial.5), channel_id=1, source_target_pairs={{0,32},{32,64},{64,96},{96,128},{128,160},{160,192},{192,224},{224... | collective-permute-start | bytes 393224 | tf_op jit(solution)/shard_map/ppermute | solution.py:291
  83.3 11.3 %collective-permute-start.10 = (bf16[512,128]{1,0:T(8,128)(2,1)S(1)}, bf16[512,128]{1,0:T(8,128)(2,1)S(1)}, u32[]{:S(2)}, u32[]{:S(2)}) collective-permute-start(bf16[512,128]{1,0:T(8,128)(2,1)S(1)} %get-tuple-element.26.own), channel_id=1, source_target_pairs={{1,2},{3,4},{5,6},{7,8},{9,10},{11,12},{13,14},{15,16},{17,18},{19... | collective-permute-start | bytes 393224 | tf_op jit(solution)/shard_map/ppermute | solution.py:274
  85.3 9.3 %collective-permute-start.11 = (bf16[512,128]{1,0:T(8,128)(2,1)S(1)}, bf16[512,128]{1,0:T(8,128)(2,1)S(1)}, u32[]{:S(2)}, u32[]{:S(2)}) collective-permute-start(bf16[512,128]{1,0:T(8,128)(2,1)S(1)} %get-tuple-element.26.own), channel_id=1, source_target_pairs={{1,17},{3,19},{5,21},{7,23},{9,25},{11,27},{13,29},{15,31},{17,1},... | collective-permute-start | bytes 393224 | tf_op jit(solution)/shard_map/ppermute | solution.py:285

commit v12 on v11

--- a/solution.py
+++ b/solution.py
@@ -23,20 +23,25 @@
     return jnp.dot(a, b, preferred_element_type=F32)
 
 
-def combine_kernel(around, count, source_list, blocks, inverse, right, chip, kept, handed, pair, source_here, landing, sums, arrived, small):
-    block = inverse.shape[0]
-    copy = pltpu.make_async_copy(source_list, source_here, small)
-    copy.start()
-    own = lax.axis_index("blk")
-    second = lax.rem(own, 2)
-    sign = 2 * second - 1
-    pair[0:block] = chip[pl.ds(pl.multiple_of(second * block, block), block), :]
-    pair[block:] = chip[pl.ds(pl.multiple_of((1 - second) * block, block), block), :]
+def first_kernel(
+    around, count, source_list, blocks, right, incoming, inverse,
+    solved, outgoing, inverse_here, later, kept, handed,
+    right_here, incoming_here, source_here, landing, sums, arrived, small,
+):
+    block = inverse_here.shape[0]
+    live = count[0]
+    copies = (
+        pltpu.make_async_copy(right.at[0], right_here, small.at[0]),
+        pltpu.make_async_copy(incoming, incoming_here, small.at[1]),
+        pltpu.make_async_copy(inverse, inverse_here, small.at[2]),
+        pltpu.make_async_copy(right.at[pl.ds(1, later.shape[0])], later, small.at[3]),
+        pltpu.make_async_copy(source_list, source_here, small.at[4]),
+    )
+    for copy in copies:
+        copy.start()
 
     def copy_of(k):
         return pltpu.make_async_copy(blocks.at[0, k], landing.at[k], arrived.at[k])
-
-    live = count[0]
 
     def begin(k, carry):
         copy_of(k).start()
@@ -44,14 +49,22 @@
 
     lax.fori_loop(0, live, begin, 0)
     sums[...] = jnp.zeros_like(sums)
-    handed[4 * block : 5 * block, :] = inverse[...]
-    for tick in range(right.shape[0]):
-        value = right[tick]
+    own = lax.axis_index("blk")
+    sign = 2 * lax.rem(own, 2) - 1
+    for copy in copies[:3]:
+        copy.wait()
+    value = mm(inverse_here[...], (right_here[...] - incoming_here[...]).astype(BF16))
+    solved[...] = value
+    outgoing[...] = value.astype(BF16)
+    handed[4 * block : 5 * block, :] = inverse_here[...]
+    for copy in copies[3:]:
+        copy.wait()
+    for tick in range(later.shape[0]):
+        value = later[tick]
         high = value.astype(BF16)
         rows = pl.ds((5 + tick) * block, block)
         handed[rows, 0 : value.shape[1]] = high
         handed[rows, value.shape[1] :] = (value - high.astype(F32)).astype(BF16)
-    copy.wait()
 
     def add(k, carry):
         copy_of(k).wait()
@@ -73,68 +86,33 @@
     return pltpu.with_memory_space_constraint(value, pltpu.HBM)
 
 
-def combine(around, chip, sources, counts, factor_blocks, inverse, right):
-    slots, block = factor_blocks.shape[1], factor_blocks.shape[2]
-    ticks = right.shape[0]
-    return pl.pallas_call(
-        functools.partial(combine_kernel, around),
-        out_shape=(
-            jax.ShapeDtypeStruct((5, block, block), BF16),
-            jax.ShapeDtypeStruct(((5 + ticks) * block, block), BF16),
-            jax.ShapeDtypeStruct(chip.shape, BF16),
-        ),
-        in_specs=[SMEM, HBM, HBM, VMEM, VMEM, VMEM],
-        out_specs=(VMEM, VMEM, VMEM),
-        scratch_shapes=[
-            pltpu.SMEM(sources.shape, jnp.int32),
-            pltpu.VMEM((slots, block, block), BF16),
-            pltpu.VMEM((8, block, block), F32),
-            pltpu.SemaphoreType.DMA((slots,)),
-            pltpu.SemaphoreType.DMA,
-        ],
-        compiler_params=params(),
-        cost_estimate=pl.CostEstimate(flops=4_000_000, bytes_accessed=10_000_000, transcendentals=0),
-        name="combine",
-    )(counts, in_hbm(sources), in_hbm(factor_blocks), inverse, right, chip)
-
-
-def first_kernel(right, incoming, inverse, solved, outgoing, inverse_here, later_here, right_here, incoming_here, arrived):
-    copies = (
-        pltpu.make_async_copy(right.at[0], right_here, arrived.at[0]),
-        pltpu.make_async_copy(incoming, incoming_here, arrived.at[1]),
-        pltpu.make_async_copy(inverse, inverse_here, arrived.at[2]),
-        pltpu.make_async_copy(right.at[pl.ds(1, later_here.shape[0])], later_here, arrived.at[3]),
-    )
-    for copy in copies:
-        copy.start()
-    for copy in copies[:3]:
-        copy.wait()
-    value = mm(inverse_here[...], (right_here[...] - incoming_here[...]).astype(BF16))
-    solved[...] = value
-    outgoing[...] = value.astype(BF16)
-    copies[3].wait()
-
-
-def first_solve(right_side, carry_in, inverse_diag):
+def first_solve(around, sources, counts, factor_blocks, right_side, carry_in, inverse_diag):
+    slots = factor_blocks.shape[1]
     ticks, block, columns = right_side.shape
     return pl.pallas_call(
-        first_kernel,
+        functools.partial(first_kernel, around),
         out_shape=(
             jax.ShapeDtypeStruct((block, columns), F32),
             jax.ShapeDtypeStruct((block, columns), BF16),
             jax.ShapeDtypeStruct((block, block), BF16),
             jax.ShapeDtypeStruct((ticks - 1, block, columns), F32),
+            jax.ShapeDtypeStruct((5, block, block), BF16),
+            jax.ShapeDtypeStruct(((4 + ticks) * block, block), BF16),
         ),
-        in_specs=[HBM, HBM, HBM],
-        out_specs=(VMEM, VMEM, VMEM, VMEM),
+        in_specs=[SMEM, HBM, HBM, HBM, HBM, HBM],
+        out_specs=(VMEM,) * 6,
         scratch_shapes=[
             pltpu.VMEM((block, columns), F32),
             pltpu.VMEM((block, columns), F32),
-            pltpu.SemaphoreType.DMA((4,)),
+            pltpu.SMEM(sources.shape, jnp.int32),
+            pltpu.VMEM((slots, block, block), BF16),
+            pltpu.VMEM((8, block, block), F32),
+            pltpu.SemaphoreType.DMA((slots,)),
+            pltpu.SemaphoreType.DMA((5,)),
         ],
         compiler_params=params(),
         name="first",
-    )(in_hbm(right_side), in_hbm(carry_in), in_hbm(inverse_diag))
+    )(counts, *(in_hbm(a) for a in (sources, factor_blocks, right_side, carry_in, inverse_diag)))
 
 
 def pair_kernel(tick, both, right, inverse, given, solved, outgoing):
@@ -273,13 +251,16 @@
         partner = [(a, b) for a, b in pairs] + [(b, a) for a, b in pairs]
         return lax.ppermute(value, "blk", partner)
 
-    solved, own, inverse, right = first_solve(right_side, carry_in, inverse_diag)
+    solved, own, inverse, right, kept, handed = first_solve(
+        around, sources, counts, factor_blocks, right_side, carry_in, inverse_diag
+    )
     finished = [solved]
     seconds = [(b, (b + chips) % around) for b in range(1, around, 2)]
     for tick in range(ticks):
         if tick == 0:
             chip = paired(own, chip_pairs)
-            kept, handed, own = combine(around, chip, sources, counts, factor_blocks, inverse, right)
+            second = lax.rem(lax.axis_index("blk"), 2)
+            own = jnp.where(second == 0, chip, jnp.roll(chip, block, 0))
             given = swapped(handed, chip_pairs)
         beside = swapped(own, next_pairs)
         opposite = lax.ppermute(own, "blk", seconds)

time: 100 us -> 100 us (level)
  the two profiles are of different devices: /device:TPU:385 before, /device:TPU:129 now
where the time goes in v12:
time: 100 us; the launch traced here: 99.7 us
  blocking collectives  44.7 us (45%)
  starting transfers between devices  33.6 us (34%)
  waiting for transfers between devices  14 us (14%)
  Pallas kernels  5.89 us (6%)
  between operations  1.49 us (1%)
    all_gather x9, blocking collectives, paired(): lax.all_gather(value, 'blk', axis=0, tiled=True, axis_index_groups=pairs)  44.7 us
    ppermute x4, starting transfers between devices, shards(): opposite = lax.ppermute(own, 'blk', seconds)  14.8 us
    ppermute x3, waiting for transfers between devices, shards(): lax.ppermute(partial_sums(operands), 'grp', [(g, g + 1) for g in range(gr...  13.5 us
    ppermute x5, starting transfers between devices, swapped(): return lax.ppermute(value, 'blk', partner)  11.6 us
    ppermute x3, starting transfers between devices, shards(): lax.ppermute(partial_sums(operands), 'grp', [(g, g + 1) for g in range(gr...  7.2 us
    pallas_call x1, Pallas kernels, first_solve(): pl.pallas_call(functools.partial(first_kernel, around), out_shape=(jax.Sh...  2.1 us
  transfers between devices with their start and end apart: 12, of which 4 were waited for; matrix products, arithmetic and copies ran while one was open for 0% of the time, Pallas kernels for 0%

profile of v12, /device:TPU:129, one launch (start us, length us, event | category | flops | bytes accessed | tf_op | source)
XLA Modules:
  0.0 99.7 jit_solution(9232783450467894626)
XLA Ops:
  1.3 2.1 %first.1 = (f32[256,128]{1,0:T(8,128)S(1)}, bf16[256,128]{1,0:T(8,128)(2,1)S(1)}, bf16[256,256]{1,0:T(8,128)(2,1)S(1)}, f32[3,256,128]{2,1,0:T(8,128)S(1)}, bf16...) custom-call(s32[1]{0:T(128)S(6)} %copy.8.count, s32[1,24]{1,0:T(1,128)} %source_list.1, ...), custom_call_target="tpu_custom_call" | custom-call | tf_op jit(solution)/shard_map/first/pallas_call | solution.py:92
  3.4 2.7 %collective-permute-start = (bf16[2048,256]{1,0:T(8,128)(2,1)S(1)}, bf16[2048,256]{1,0:T(8,128)(2,1)S(1)}, u32[]{:S(2)}, u32[]{:S(2)}) collective-permute-start(bf16[2048,256]{1,0:T(8,128)(2,1)S(1)} %get-tuple-element.18), channel_id=1, source_target_pairs={{0,1},{2,3},{4,5},{6,7},{8,9},{10,11},{12,13},{14,15},{16,17},{18,... | collective-permute-start | bytes 3145736 | tf_op jit(solution)/shard_map/ppermute | solution.py:252
  6.1 2.4 %all_gather.27 = bf16[512,128]{1,0:T(8,128)(2,1)S(1)} all-gather(bf16[256,128]{1,0:T(8,128)(2,1)S(1)} %get-tuple-element.19), channel_id=1, replica_groups={{0,1},{2,3},{4,5},{6,7},{8,9},{10,11},{12,13},{14,15},{16,17},{18,19},{..., dimensions={0}, use_global_device_ids=true | all-gather | bytes 196608 | tf_op jit(solution)/shard_map/all_gather | solution.py:248
  8.5 2.9 %collective-permute-start.1 = (bf16[512,128]{1,0:T(8,128)(2,1)S(1)}, bf16[512,128]{1,0:T(8,128)(2,1)S(1)}, u32[]{:S(2)}, u32[]{:S(2)}) collective-permute-start(bf16[512,128]{1,0:T(8,128)(2,1)S(1)} %maximum_select_fusion.own), channel_id=1, source_target_pairs={{1,2},{3,4},{5,6},{7,8},{9,10},{11,12},{13,14},{15,16},{17,18},{19... | collective-permute-start | bytes 393224 | tf_op jit(solution)/shard_map/ppermute | solution.py:252
  11.5 5.4 %collective-permute-start.2 = (bf16[512,128]{1,0:T(8,128)(2,1)S(1)}, bf16[512,128]{1,0:T(8,128)(2,1)S(1)}, u32[]{:S(2)}, u32[]{:S(2)}) collective-permute-start(bf16[512,128]{1,0:T(8,128)(2,1)S(1)} %maximum_select_fusion.own), channel_id=1, source_target_pairs={{1,17},{3,19},{5,21},{7,23},{9,25},{11,27},{13,29},{15,31},{17,1},... | collective-permute-start | bytes 393224 | tf_op jit(solution)/shard_map/ppermute | solution.py:266
  16.9 6.2 %all_gather.28.third = bf16[512,128]{1,0:T(8,128)(2,1)S(1)} all-gather(bf16[256,128]{1,0:T(8,128)(2,1)S(1)} %slice.28), channel_id=1, replica_groups={{1,4},{3,6},{5,8},{7,10},{9,12},{11,14},{13,16},{15,18},{17,20},{19,22}..., dimensions={0}, use_global_device_ids=true | all-gather | bytes 196608 | tf_op jit(solution)/shard_map/all_gather | solution.py:248
  23.1 0.5 partial.3
  23.6 3.1 %collective-permute-start.3 = (bf16[512,128]{1,0:T(8,128)(2,1)S(1)}, bf16[512,128]{1,0:T(8,128)(2,1)S(1)}, u32[]{:S(2)}, u32[]{:S(2)}) collective-permute-start(bf16[512,128]{1,0:T(8,128)(2,1)S(1)} %partial.3), channel_id=1, source_target_pairs={{0,32},{32,64},{64,96},{96,128},{128,160},{160,192},{192,224},{224... | collective-permute-start | bytes 393224 | tf_op jit(solution)/shard_map/ppermute | solution.py:272
  26.6 3.8 %collective-permute-done.3 = bf16[512,128]{1,0:T(8,128)(2,1)S(1)} collective-permute-done((bf16[512,128]{1,0:T(8,128)(2,1)S(1)}, bf16[512,128]{1,0:T(8,128)(2,1)S(1)}, u32[]{:S(2)}, u32[]{:S(2)}) %collective-permute-start.3) | collective-permute-done | bytes 131104 | tf_op jit(solution)/shard_map/ppermute | solution.py:272
  30.5 4.0 %all_gather.29.both = bf16[1024,128]{1,0:T(8,128)(2,1)S(1)} all-gather(bf16[512,128]{1,0:T(8,128)(2,1)S(1)} %collective-permute-done.3), channel_id=1, replica_groups={{0,1},{2,3},{4,5},{6,7},{8,9},{10,11},{12,13},{14,15},{16,17},{18,19},{..., dimensions={0}, use_global_device_ids=true | all-gather | bytes 393216 | tf_op jit(solution)/shard_map/all_gather | solution.py:248
  34.5 0.2 solve.3
  34.8 2.1 %collective-permute-start.4 = (bf16[512,128]{1,0:T(8,128)(2,1)S(1)}, bf16[512,128]{1,0:T(8,128)(2,1)S(1)}, u32[]{:S(2)}, u32[]{:S(2)}) collective-permute-start(bf16[512,128]{1,0:T(8,128)(2,1)S(1)} %get-tuple-element.22.own), channel_id=1, source_target_pairs={{1,2},{3,4},{5,6},{7,8},{9,10},{11,12},{13,14},{15,16},{17,18},{19... | collective-permute-start | bytes 393224 | tf_op jit(solution)/shard_map/ppermute | solution.py:252
  36.9 2.2 %collective-permute-start.5 = (bf16[512,128]{1,0:T(8,128)(2,1)S(1)}, bf16[512,128]{1,0:T(8,128)(2,1)S(1)}, u32[]{:S(2)}, u32[]{:S(2)}) collective-permute-start(bf16[512,128]{1,0:T(8,128)(2,1)S(1)} %get-tuple-element.22.own), channel_id=1, source_target_pairs={{1,17},{3,19},{5,21},{7,23},{9,25},{11,27},{13,29},{15,31},{17,1},... | collective-permute-start | bytes 393224 | tf_op jit(solution)/shard_map/ppermute | solution.py:266
  39.1 5.9 %all_gather.30.third = bf16[512,128]{1,0:T(8,128)(2,1)S(1)} all-gather(bf16[256,128]{1,0:T(8,128)(2,1)S(1)} %slice.23), channel_id=1, replica_groups={{1,4},{3,6},{5,8},{7,10},{9,12},{11,14},{13,16},{15,18},{17,20},{19,22}..., dimensions={0}, use_global_device_ids=true | all-gather | bytes 196608 | tf_op jit(solution)/shard_map/all_gather | solution.py:248
  45.0 0.4 collective-permute-done.5.opposite
  45.5 0.5 partial.4
  45.9 2.2 %collective-permute-start.6 = (bf16[512,128]{1,0:T(8,128)(2,1)S(1)}, bf16[512,128]{1,0:T(8,128)(2,1)S(1)}, u32[]{:S(2)}, u32[]{:S(2)}) collective-permute-start(bf16[512,128]{1,0:T(8,128)(2,1)S(1)} %partial.4), channel_id=1, source_target_pairs={{0,32},{32,64},{64,96},{96,128},{128,160},{160,192},{192,224},{224... | collective-permute-start | bytes 393224 | tf_op jit(solution)/shard_map/ppermute | solution.py:272
  48.1 4.7 %collective-permute-done.6 = bf16[512,128]{1,0:T(8,128)(2,1)S(1)} collective-permute-done((bf16[512,128]{1,0:T(8,128)(2,1)S(1)}, bf16[512,128]{1,0:T(8,128)(2,1)S(1)}, u32[]{:S(2)}, u32[]{:S(2)}) %collective-permute-start.6) | collective-permute-done | bytes 131104 | tf_op jit(solution)/shard_map/ppermute | solution.py:272
  52.8 5.9 %all_gather.31.both = bf16[1024,128]{1,0:T(8,128)(2,1)S(1)} all-gather(bf16[512,128]{1,0:T(8,128)(2,1)S(1)} %collective-permute-done.6), channel_id=1, replica_groups={{0,1},{2,3},{4,5},{6,7},{8,9},{10,11},{12,13},{14,15},{16,17},{18,19},{..., dimensions={0}, use_global_device_ids=true | all-gather | bytes 393216 | tf_op jit(solution)/shard_map/all_gather | solution.py:248
  59.0 1.9 %collective-permute-start.7 = (bf16[512,128]{1,0:T(8,128)(2,1)S(1)}, bf16[512,128]{1,0:T(8,128)(2,1)S(1)}, u32[]{:S(2)}, u32[]{:S(2)}) collective-permute-start(bf16[512,128]{1,0:T(8,128)(2,1)S(1)} %get-tuple-element.23.own), channel_id=1, source_target_pairs={{1,2},{3,4},{5,6},{7,8},{9,10},{11,12},{13,14},{15,16},{17,18},{19... | collective-permute-start | bytes 393224 | tf_op jit(solution)/shard_map/ppermute | solution.py:252
  60.9 3.6 %collective-permute-start.8 = (bf16[512,128]{1,0:T(8,128)(2,1)S(1)}, bf16[512,128]{1,0:T(8,128)(2,1)S(1)}, u32[]{:S(2)}, u32[]{:S(2)}) collective-permute-start(bf16[512,128]{1,0:T(8,128)(2,1)S(1)} %get-tuple-element.23.own), channel_id=1, source_target_pairs={{1,17},{3,19},{5,21},{7,23},{9,25},{11,27},{13,29},{15,31},{17,1},... | collective-permute-start | bytes 393224 | tf_op jit(solution)/shard_map/ppermute | solution.py:266
  64.6 6.2 %all_gather.32.third = bf16[512,128]{1,0:T(8,128)(2,1)S(1)} all-gather(bf16[256,128]{1,0:T(8,128)(2,1)S(1)} %slice.24), channel_id=1, replica_groups={{1,4},{3,6},{5,8},{7,10},{9,12},{11,14},{13,16},{15,18},{17,20},{19,22}..., dimensions={0}, use_global_device_ids=true | all-gather | bytes 196608 | tf_op jit(solution)/shard_map/all_gather | solution.py:248
  70.7 0.5 partial.5
  71.2 1.9 %collective-permute-start.9 = (bf16[512,128]{1,0:T(8,128)(2,1)S(1)}, bf16[512,128]{1,0:T(8,128)(2,1)S(1)}, u32[]{:S(2)}, u32[]{:S(2)}) collective-permute-start(bf16[512,128]{1,0:T(8,128)(2,1)S(1)} %partial.5), channel_id=1, source_target_pairs={{0,32},{32,64},{64,96},{96,128},{128,160},{160,192},{192,224},{224... | collective-permute-start | bytes 393224 | tf_op jit(solution)/shard_map/ppermute | solution.py:272
  73.1 5.0 %collective-permute-done.9 = bf16[512,128]{1,0:T(8,128)(2,1)S(1)} collective-permute-done((bf16[512,128]{1,0:T(8,128)(2,1)S(1)}, bf16[512,128]{1,0:T(8,128)(2,1)S(1)}, u32[]{:S(2)}, u32[]{:S(2)}) %collective-permute-start.9) | collective-permute-done | bytes 131104 | tf_op jit(solution)/shard_map/ppermute | solution.py:272
  78.1 4.5 %all_gather.33.both = bf16[1024,128]{1,0:T(8,128)(2,1)S(1)} all-gather(bf16[512,128]{1,0:T(8,128)(2,1)S(1)} %collective-permute-done.9), channel_id=1, replica_groups={{0,1},{2,3},{4,5},{6,7},{8,9},{10,11},{12,13},{14,15},{16,17},{18,19},{..., dimensions={0}, use_global_device_ids=true | all-gather | bytes 393216 | tf_op jit(solution)/shard_map/all_gather | solution.py:248
  82.9 1.9 %collective-permute-start.10 = (bf16[512,128]{1,0:T(8,128)(2,1)S(1)}, bf16[512,128]{1,0:T(8,128)(2,1)S(1)}, u32[]{:S(2)}, u32[]{:S(2)}) collective-permute-start(bf16[512,128]{1,0:T(8,128)(2,1)S(1)} %get-tuple-element.24.own), channel_id=1, source_target_pairs={{1,2},{3,4},{5,6},{7,8},{9,10},{11,12},{13,14},{15,16},{17,18},{19... | collective-permute-start | bytes 393224 | tf_op jit(solution)/shard_map/ppermute | solution.py:252
  84.8 3.5 %collective-permute-start.11 = (bf16[512,128]{1,0:T(8,128)(2,1)S(1)}, bf16[512,128]{1,0:T(8,128)(2,1)S(1)}, u32[]{:S(2)}, u32[]{:S(2)}) collective-permute-start(bf16[512,128]{1,0:T(8,128)(2,1)S(1)} %get-tuple-element.24.own), channel_id=1, source_target_pairs={{1,17},{3,19},{5,21},{7,23},{9,25},{11,27},{13,29},{15,31},{17,1},... | collective-permute-start | bytes 393224 | tf_op jit(solution)/shard_map/ppermute | solution.py:266
  88.3 6.2 %all_gather.34.third = bf16[512,128]{1,0:T(8,128)(2,1)S(1)} all-gather(bf16[256,128]{1,0:T(8,128)(2,1)S(1)} %slice.25), channel_id=1, replica_groups={{1,4},{3,6},{5,8},{7,10},{9,12},{11,14},{13,16},{15,18},{17,20},{19,22}..., dimensions={0}, use_global_device_ids=true | all-gather | bytes 196608 | tf_op jit(solution)/shard_map/all_gather | solution.py:248
  94.5 1.0 %last.1 = (f32[256,128]{1,0:T(8,128)S(1)}, bf16[256,128]{1,0:T(8,128)(2,1)S(1)}, f32[4,256,128]{2,1,0:T(8,128)}) custom-call(bf16[5,256,256]{2,1,0:T(8,128)(2,1)S(1)} %get-tuple-element.17.kept, bf16[2048,256]{1,0:T(8,128)(2,1)S(1)} %collective-permute-done.given, bf16[512,128]{1,0:T(8,128)(2,1)S(1)} %get-tuple-element.24.own, ...), custom_call_target="tpu_custom_call" | custom-call | tf_op jit(solution)/shard_map/last/pallas_call | solution.py:206
  95.5 3.5 %all_gather.35.both = bf16[512,128]{1,0:T(8,128)(2,1)S(1)} all-gather(bf16[256,128]{1,0:T(8,128)(2,1)S(1)} %get-tuple-element.31), channel_id=1, replica_groups={{0,1},{2,3},{4,5},{6,7},{8,9},{10,11},{12,13},{14,15},{16,17},{18,19},{..., dimensions={0}, use_global_device_ids=true | all-gather | bytes 196608 | tf_op jit(solution)/shard_map/all_gather | solution.py:248
  99.1 0.7 carry.1
  (16 shorter events, 0.6 us)
Async XLA Ops:
  3.4 19.7 %collective-permute-start = (bf16[2048,256]{1,0:T(8,128)(2,1)S(1)}, bf16[2048,256]{1,0:T(8,128)(2,1)S(1)}, u32[]{:S(2)}, u32[]{:S(2)}) collective-permute-start(bf16[2048,256]{1,0:T(8,128)(2,1)S(1)} %get-tuple-element.18), channel_id=1, source_target_pairs={{0,1},{2,3},{4,5},{6,7},{8,9},{10,11},{12,13},{14,15},{16,17},{18,... | collective-permute-start | bytes 3145736 | tf_op jit(solution)/shard_map/ppermute | solution.py:252
  8.5 14.6 %collective-permute-start.1 = (bf16[512,128]{1,0:T(8,128)(2,1)S(1)}, bf16[512,128]{1,0:T(8,128)(2,1)S(1)}, u32[]{:S(2)}, u32[]{:S(2)}) collective-permute-start(bf16[512,128]{1,0:T(8,128)(2,1)S(1)} %maximum_select_fusion.own), channel_id=1, source_target_pairs={{1,2},{3,4},{5,6},{7,8},{9,10},{11,12},{13,14},{15,16},{17,18},{19... | collective-permute-start | bytes 393224 | tf_op jit(solution)/shard_map/ppermute | solution.py:252
  11.5 11.6 %collective-permute-start.2 = (bf16[512,128]{1,0:T(8,128)(2,1)S(1)}, bf16[512,128]{1,0:T(8,128)(2,1)S(1)}, u32[]{:S(2)}, u32[]{:S(2)}) collective-permute-start(bf16[512,128]{1,0:T(8,128)(2,1)S(1)} %maximum_select_fusion.own), channel_id=1, source_target_pairs={{1,17},{3,19},{5,21},{7,23},{9,25},{11,27},{13,29},{15,31},{17,1},... | collective-permute-start | bytes 393224 | tf_op jit(solution)/shard_map/ppermute | solution.py:266
  23.6 6.9 %collective-permute-start.3 = (bf16[512,128]{1,0:T(8,128)(2,1)S(1)}, bf16[512,128]{1,0:T(8,128)(2,1)S(1)}, u32[]{:S(2)}, u32[]{:S(2)}) collective-permute-start(bf16[512,128]{1,0:T(8,128)(2,1)S(1)} %partial.3), channel_id=1, source_target_pairs={{0,32},{32,64},{64,96},{96,128},{128,160},{160,192},{192,224},{224... | collective-permute-start | bytes 393224 | tf_op jit(solution)/shard_map/ppermute | solution.py:272
  34.8 10.2 %collective-permute-start.4 = (bf16[512,128]{1,0:T(8,128)(2,1)S(1)}, bf16[512,128]{1,0:T(8,128)(2,1)S(1)}, u32[]{:S(2)}, u32[]{:S(2)}) collective-permute-start(bf16[512,128]{1,0:T(8,128)(2,1)S(1)} %get-tuple-element.22.own), channel_id=1, source_target_pairs={{1,2},{3,4},{5,6},{7,8},{9,10},{11,12},{13,14},{15,16},{17,18},{19... | collective-permute-start | bytes 393224 | tf_op jit(solution)/shard_map/ppermute | solution.py:252
  36.9 8.6 %collective-permute-start.5 = (bf16[512,128]{1,0:T(8,128)(2,1)S(1)}, bf16[512,128]{1,0:T(8,128)(2,1)S(1)}, u32[]{:S(2)}, u32[]{:S(2)}) collective-permute-start(bf16[512,128]{1,0:T(8,128)(2,1)S(1)} %get-tuple-element.22.own), channel_id=1, source_target_pairs={{1,17},{3,19},{5,21},{7,23},{9,25},{11,27},{13,29},{15,31},{17,1},... | collective-permute-start | bytes 393224 | tf_op jit(solution)/shard_map/ppermute | solution.py:266
  45.9 6.9 %collective-permute-start.6 = (bf16[512,128]{1,0:T(8,128)(2,1)S(1)}, bf16[512,128]{1,0:T(8,128)(2,1)S(1)}, u32[]{:S(2)}, u32[]{:S(2)}) collective-permute-start(bf16[512,128]{1,0:T(8,128)(2,1)S(1)} %partial.4), channel_id=1, source_target_pairs={{0,32},{32,64},{64,96},{96,128},{128,160},{160,192},{192,224},{224... | collective-permute-start | bytes 393224 | tf_op jit(solution)/shard_map/ppermute | solution.py:272
  59.0 11.7 %collective-permute-start.7 = (bf16[512,128]{1,0:T(8,128)(2,1)S(1)}, bf16[512,128]{1,0:T(8,128)(2,1)S(1)}, u32[]{:S(2)}, u32[]{:S(2)}) collective-permute-start(bf16[512,128]{1,0:T(8,128)(2,1)S(1)} %get-tuple-element.23.own), channel_id=1, source_target_pairs={{1,2},{3,4},{5,6},{7,8},{9,10},{11,12},{13,14},{15,16},{17,18},{19... | collective-permute-start | bytes 393224 | tf_op jit(solution)/shard_map/ppermute | solution.py:252
  60.9 9.8 %collective-permute-start.8 = (bf16[512,128]{1,0:T(8,128)(2,1)S(1)}, bf16[512,128]{1,0:T(8,128)(2,1)S(1)}, u32[]{:S(2)}, u32[]{:S(2)}) collective-permute-start(bf16[512,128]{1,0:T(8,128)(2,1)S(1)} %get-tuple-element.23.own), channel_id=1, source_target_pairs={{1,17},{3,19},{5,21},{7,23},{9,25},{11,27},{13,29},{15,31},{17,1},... | collective-permute-start | bytes 393224 | tf_op jit(solution)/shard_map/ppermute | solution.py:266
  71.2 6.9 %collective-permute-start.9 = (bf16[512,128]{1,0:T(8,128)(2,1)S(1)}, bf16[512,128]{1,0:T(8,128)(2,1)S(1)}, u32[]{:S(2)}, u32[]{:S(2)}) collective-permute-start(bf16[512,128]{1,0:T(8,128)(2,1)S(1)} %partial.5), channel_id=1, source_target_pairs={{0,32},{32,64},{64,96},{96,128},{128,160},{160,192},{192,224},{224... | collective-permute-start | bytes 393224 | tf_op jit(solution)/shard_map/ppermute | solution.py:272
  82.9 11.6 %collective-permute-start.10 = (bf16[512,128]{1,0:T(8,128)(2,1)S(1)}, bf16[512,128]{1,0:T(8,128)(2,1)S(1)}, u32[]{:S(2)}, u32[]{:S(2)}) collective-permute-start(bf16[512,128]{1,0:T(8,128)(2,1)S(1)} %get-tuple-element.24.own), channel_id=1, source_target_pairs={{1,2},{3,4},{5,6},{7,8},{9,10},{11,12},{13,14},{15,16},{17,18},{19... | collective-permute-start | bytes 393224 | tf_op jit(solution)/shard_map/ppermute | solution.py:252
  84.8 9.7 %collective-permute-start.11 = (bf16[512,128]{1,0:T(8,128)(2,1)S(1)}, bf16[512,128]{1,0:T(8,128)(2,1)S(1)}, u32[]{:S(2)}, u32[]{:S(2)}) collective-permute-start(bf16[512,128]{1,0:T(8,128)(2,1)S(1)} %get-tuple-element.24.own), channel_id=1, source_target_pairs={{1,17},{3,19},{5,21},{7,23},{9,25},{11,27},{13,29},{15,31},{17,1},... | collective-permute-start | bytes 393224 | tf_op jit(solution)/shard_map/ppermute | solution.py:266
